TPU v7x, 128 devices: a whole 4x4x4 slice. The times are simulated.
128 devices in a mesh: dev: 128 (over x, y, z, core).
Axes of the slice: x: 4, y: 4, z: 4, core: 2. Of those that a mesh axis runs over, the one named last changes fastest.
Arguments:
- bottom: bfloat16 [3, 16384, 128], P(None, 'dev'), may hold values from -6 to 6
- labels: int32 [3, 16384], P(None, 'dev'), may hold values 0 or 1
- freq_ids: int32 [3, 16384, 26, 2], P(None, 'dev'), may hold values from 0 to 16383
- req_rows: int32 [3, 128, 128, 32], P(None, 'dev'), may hold values from 0 to 4096, as said below
- req_slot: int32 [3, 128, 128, 32], P(None, 'dev'), may hold values from 0 to 3328, as said below
- freq_table: bfloat16 [16384, 128], replicated, may hold values from -3 to 3
- inf_table: bfloat16 [524288, 128], P('dev'), may hold values from -3 to 3
- cross_u: bfloat16 [3456, 512], replicated, may hold values from -0.109375 to 0.109375
- cross_v: bfloat16 [512, 3456], replicated, may hold values from -0.25 to 0.25
- cross_bias: float32 [3456], replicated, may hold values from -3 to 3
- out_w: bfloat16 [3456], replicated, may hold values from -0.109375 to 0.109375
- out_b: float32 [], replicated, may hold values from -3 to 3
Outputs:
- grad_u: float32 [3456, 512], P('dev')
- grad_v: float32 [512, 3456], P(None, 'dev')
- grad_cross_bias: float32 [3456], P('dev')
- grad_out_w: float32 [3456], P('dev')
- grad_freq: bfloat16 [16384, 128], replicated
- grad_inf: bfloat16 [524288, 128], P('dev')
Inputs may be any that keep to these rules, and one draw needn't show every extreme that they name: req_rows[m, d, o, c] is request c of device d to owner o in micro-batch m: a row number within o's 4096 rows, or 4096 for an empty request. In each list [m, d, o] the live requests come first and there is at least one; in every micro-batch some owner gets 32 live requests from every device. req_slot[m, d, o, c] = s * 26 + f names sample s of device d and feature f, or is 3328 where req_rows is 4096.
All inputs are finite; a program needn't handle non-finite values. No bound on the sum of `labels` on one device may be relied on, other than what follows from the above.
Results may differ from a plain program's by a relative error of at most 0.0062.
Values may be sent and summed in bfloat16 or wider, within the bound.
No kernel may reach another device: no remote copies, remote signals or barrier semaphores. Data moves between devices by JAX's collectives and lax.ppermute only.
A program may use at most 192 MiB of HBM per device.

v0:
```python
import math

import jax
import jax.numpy as jnp
from jax import lax
from jax.sharding import PartitionSpec as P

loss_scale = 1024.0


def in_blocks(value, dim, peers):
    lengths = value.shape
    blocks = value.reshape(*lengths[:dim], peers, lengths[dim] // peers, *lengths[dim + 1 :])
    return jnp.moveaxis(blocks, dim, 0)


def one_scatter(arrays, axis, dims):
    peers = lax.axis_size(axis)
    blocks = [in_blocks(a, dim, peers) for a, dim in zip(arrays, dims)]
    lines = jnp.concatenate([b.reshape(peers, -1) for b in blocks], axis=1)
    rows = max(16, -(-lines.shape[1] // 1024) * 8)
    lines = jnp.pad(lines, ((0, 0), (0, rows * 128 - lines.shape[1]))).reshape(-1, 128)
    vector, at, gathered = (lax.psum_scatter(lines, axis, tiled=True).reshape(-1), 0, [])
    for b in blocks:
        part = b[0]
        gathered.append(vector[at : at + part.size].reshape(part.shape))
        at += part.size
    return tuple(gathered)


def micro_pass(
    bottom_rows,
    label_rows,
    freq_rows,
    want_rows,
    want_slots,
    fetched,
    freq_table,
    cross_u,
    cross_v,
    cross_bias,
    out_w,
    out_b,
    rows_limit,
    loss_mult,
    totals,
):
    grad_u, grad_v, grad_b, grad_w, grad_f = totals
    samples, emb_width = bottom_rows.shape
    features = freq_rows.shape[1]
    hot_count = freq_rows.shape[2]
    is_live = (want_rows < rows_limit) & (want_slots < samples * features)
    slot_idx = jnp.where(is_live, want_slots, 0).reshape(-1)
    arrived = fetched.astype(jnp.float32) * is_live[:, :, None].astype(jnp.float32)
    inf_part = (
        jnp.zeros((samples * features, emb_width), jnp.float32)
        .at[slot_idx]
        .add(arrived.reshape(-1, emb_width))
    )
    freq_part = jnp.sum(jnp.take(freq_table, freq_rows, axis=0), axis=2, dtype=jnp.float32).reshape(
        samples * features, emb_width
    )
    pooled = (freq_part + inf_part).astype(jnp.bfloat16)
    x_zero = jnp.concatenate([bottom_rows, pooled.reshape(samples, features * emb_width)], axis=1)
    hidden = jnp.dot(x_zero, cross_u, preferred_element_type=jnp.float32).astype(jnp.bfloat16)
    gate_val = jnp.dot(hidden, cross_v, preferred_element_type=jnp.float32) + cross_bias
    x_float = x_zero.astype(jnp.float32)
    crossed = x_float * gate_val + x_float
    w_float = out_w.astype(jnp.float32)
    logits = jnp.sum(crossed * w_float, axis=1) + out_b
    d_logit = (jax.nn.sigmoid(logits) - label_rows.astype(jnp.float32)) * loss_mult
    d_crossed = d_logit[:, None] * w_float
    d_gate = d_crossed * x_float
    gate_low = d_gate.astype(jnp.bfloat16)
    d_hidden = jnp.dot(gate_low, cross_v.T, preferred_element_type=jnp.float32).astype(jnp.bfloat16)
    d_input = d_crossed * (gate_val + 1.0) + jnp.dot(
        d_hidden, cross_u.T, preferred_element_type=jnp.float32
    )
    d_pooled = d_input[:, emb_width:].reshape(samples, features, emb_width)
    spread = jnp.broadcast_to(
        d_pooled[:, :, None, :], (samples, features, hot_count, emb_width)
    ).reshape(-1, emb_width)
    grad_f = grad_f.at[freq_rows.reshape(-1)].add(spread)
    pooled_low = d_pooled.reshape(samples * features, emb_width).astype(jnp.bfloat16)
    returned = jnp.take(pooled_low, slot_idx, axis=0).reshape(
        want_rows.shape + (emb_width,)
    ) * is_live[:, :, None].astype(jnp.bfloat16)
    grad_u = grad_u + jnp.dot(x_zero.T, d_hidden, preferred_element_type=jnp.float32)
    grad_v = grad_v + jnp.dot(hidden.T, gate_low, preferred_element_type=jnp.float32)
    grad_b = grad_b + jnp.sum(d_gate, axis=0)
    grad_w = grad_w + jnp.sum(d_logit[:, None] * crossed, axis=0)
    return (returned, (grad_u, grad_v, grad_b, grad_w, grad_f))


def on_device(
    bottom,
    labels,
    freq_ids,
    req_rows,
    req_slot,
    freq_table,
    inf_table,
    cross_u,
    cross_v,
    cross_bias,
    out_w,
    out_b,
):
    devices = lax.axis_size("dev")
    micro_count, samples, emb_width = bottom.shape
    rows_limit = inf_table.shape[0]
    capacity = req_rows.shape[3]
    loss_mult = loss_scale / math.sqrt(micro_count * samples * devices)
    zero_cols = jnp.zeros((cross_u.shape[0],), jnp.float32)
    totals = (
        jnp.zeros(cross_u.shape, jnp.float32),
        jnp.zeros(cross_v.shape, jnp.float32),
        zero_cols,
        zero_cols,
        jnp.zeros(freq_table.shape, jnp.float32),
    )
    grad_inf = jnp.zeros(inf_table.shape, jnp.float32)
    asked_all = jnp.transpose(req_rows[:, 0], (1, 0, 2)).reshape(devices, micro_count * capacity)
    asked = lax.all_to_all(asked_all, "dev", split_axis=0, concat_axis=0, tiled=True)
    looked_up = jnp.take(inf_table, jnp.minimum(asked, rows_limit - 1), axis=0)
    fetched_all = lax.all_to_all(looked_up, "dev", split_axis=0, concat_axis=0, tiled=True)
    pieces = []
    for batch_idx in range(micro_count):
        fetched = fetched_all[:, batch_idx * capacity : (batch_idx + 1) * capacity]
        returned, totals = micro_pass(
            bottom[batch_idx],
            labels[batch_idx],
            freq_ids[batch_idx],
            req_rows[batch_idx, 0],
            req_slot[batch_idx, 0],
            fetched,
            freq_table,
            cross_u,
            cross_v,
            cross_bias,
            out_w,
            out_b,
            rows_limit,
            loss_mult,
            totals,
        )
        pieces.append(returned)
    arrived = lax.all_to_all(
        jnp.concatenate(pieces, axis=1), "dev", split_axis=0, concat_axis=0, tiled=True
    )
    grad_inf = grad_inf.at[jnp.minimum(asked, rows_limit - 1).reshape(-1)].add(
        arrived.astype(jnp.float32).reshape(-1, emb_width)
    )
    grad_u, grad_v, grad_b, grad_w, grad_f = totals
    grad_u, grad_v, grad_b, grad_w = one_scatter(
        (grad_u, grad_v, grad_b, grad_w), "dev", (0, 1, 0, 0)
    )
    freq_total = lax.psum(grad_f, "dev").astype(jnp.bfloat16)
    return (grad_u, grad_v, grad_b, grad_w, freq_total, grad_inf.astype(jnp.bfloat16))


def solution(mesh):
    in_specs = (
        P(None, "dev", None),
        P(None, "dev"),
        P(None, "dev", None, None),
        P(None, "dev", None, None),
        P(None, "dev", None, None),
        P(),
        P("dev", None),
        P(),
        P(),
        P(),
        P(),
        P(),
    )
    out_specs = (P("dev", None), P(None, "dev"), P("dev"), P("dev"), P(), P("dev", None))
    return jax.shard_map(
        on_device, mesh=mesh, in_specs=in_specs, out_specs=out_specs, check_vma=False
    )
```

profile of v0, /device:TPU:1, one launch (start us, length us, event | category | flops | bytes accessed | tf_op | source)
XLA Modules:
  0.0 1217.3 jit_solution(3045698938043089616)
XLA Ops:
  8.9 12.0 all-to-all-start
  34.1 3.6 copy.152
  41.8 3.6 copy.158
  49.5 16.9 %gather_fusion.1 = bf16[6656,128]{1,0:T(8,128)(2,1)} fusion(bf16[16384,128]{1,0:T(8,128)(2,1)} %param.21, s32[7168]{0:T(1024)} %pad_clamp_fusion.2), kind=kCustom, calls=%fused_computation.clone | custom fusion | bytes 3434496 | tf_op jit(solution)/shard_map/jit(_take)/gather | solution.py:60
  66.4 16.9 %gather_fusion.2 = bf16[6656,128]{1,0:T(8,128)(2,1)} fusion(bf16[16384,128]{1,0:T(8,128)(2,1)} %param.21, s32[7168]{0:T(1024)} %pad_clamp_fusion.1), kind=kCustom, calls=%fused_computation.2.clone | custom fusion | bytes 3434496 | tf_op jit(solution)/shard_map/jit(_take)/gather | solution.py:60
  83.3 3.6 copy.163
  91.0 17.3 %gather_fusion.3 = bf16[6656,128]{1,0:T(8,128)(2,1)} fusion(bf16[16384,128]{1,0:T(8,128)(2,1)} %param.21, s32[7168]{0:T(1024)} %pad_clamp_fusion), kind=kCustom, calls=%fused_computation.3.clone | custom fusion | bytes 3434496 | tf_op jit(solution)/shard_map/jit(_take)/gather | solution.py:60
  108.3 9.3 convert_reduce_fusion.2
  117.6 8.0 convert_reduce_fusion.1
  125.7 8.0 convert_reduce_fusion
  154.3 47.1 %gather_fusion = bf16[12288,128]{1,0:T(8,128)(2,1)} fusion(bf16[4096,128]{1,0:T(8,128)(2,1)} %param.22, s32[12288]{0:T(1024)} %broadcast_clamp_fusion), kind=kCustom, calls=%fused_computation.6 | custom fusion | bytes 6340608 | tf_op jit(solution)/shard_map/jit(_take)/gather | solution.py:125
  201.5 7.0 broadcast_select_fusion.3
  208.4 10.2 all-to-all-start.1
  242.1 18.1 %all-to-all-done.1 = bf16[128,96,128]{2,1,0:T(8,128)(2,1)} async-done(((bf16[128,96,128]{2,1,0:T(8,128)(2,1)}), bf16[128,96,128]{2,1,0:T(8,128)(2,1)}, u32[]{:S(2)}, u32[]{:S(2)}) %all-to-all-start.1) | async-done | bytes 3145760 | tf_op jit(solution)/shard_map/all_to_all | solution.py:126
  260.1 5.8 convert_multiply_fusion.5
  265.9 24.3 %scatter_fusion.1 = f32[3328,128]{1,0:T(8,128)} fusion(f32[3328,128]{1,0:T(8,128)} %reshape.537, s32[4096]{0:T(1024)} %bitcast.147, f32[4096,128]{1,0:T(8,128)} %bitcast.130), kind=kCustom, calls=%fused_computation.8 | custom fusion | flops 524288 | bytes 6307840 | tf_op jit(solution)/shard_map/scatter-add | solution.py:58
  295.4 24.2 %scatter_fusion = f32[3328,128]{1,0:T(8,128)} fusion(f32[3328,128]{1,0:T(8,128)} %reshape.534, s32[4096]{0:T(1024)} %bitcast.146, f32[4096,128]{1,0:T(8,128)} %bitcast.129), kind=kCustom, calls=%fused_computation.7 | custom fusion | flops 524288 | bytes 6307840 | tf_op jit(solution)/shard_map/scatter-add | solution.py:58
  324.8 24.2 %scatter_fusion.2 = f32[3328,128]{1,0:T(8,128)} fusion(f32[3328,128]{1,0:T(8,128)} %reshape.540, s32[4096]{0:T(1024)} %bitcast.145, f32[4096,128]{1,0:T(8,128)} %bitcast.128), kind=kCustom, calls=%fused_computation.9 | custom fusion | flops 524288 | bytes 6307840 | tf_op jit(solution)/shard_map/scatter-add | solution.py:58
  363.4 3.4 multiply_reduce_fusion
  368.8 4.0 fusion.16
  374.8 4.1 fusion.13
  382.3 4.7 fusion.30
  388.0 7.3 add_add_fusion
  395.3 8.4 copy.167
  403.7 8.0 reshape.543
  411.7 11.0 copy.168
  422.7 8.9 reshape.544
  432.7 7.2 add_add_fusion.1
  439.9 9.2 reshape_reshape.2
  449.1 8.4 copy.169
  457.5 34.5 %concatenate.18 = f32[128,27702]{0,1:T(8,128)} concatenate(f32[128,13824]{0,1:T(8,128)} %copy.169, f32[128,13824]{0,1:T(8,128)} %reshape.544, f32[128,27]{0,1:T(8,128)S(1)} %copy.170, f32[128,27]{0,1:T(8,128)S(1)} %copy.171), dimensions={1} | concatenate | bytes 28366848 | tf_op jit(solution)/shard_map/concatenate | solution.py:20
  492.1 14.7 %copy.192 = f32[128,27702]{1,0:T(8,128)} copy(f32[128,27702]{0,1:T(8,128)} %concatenate.18) | data formatting | bytes 28366848
  506.8 11.7 pad.4.clone
  518.5 13.2 %reshape.545 = f32[28672,128]{1,0:T(8,128)} reshape(f32[128,28672]{1,0:T(8,128)} %pad.4.clone) | data formatting | bytes 29360128 | tf_op jit(solution)/shard_map/reshape | solution.py:22
  544.9 3.7 copy.176
  569.7 3.4 fusion.38
  575.8 3.5 fusion.39
  583.5 15.0 %gather_fusion.6 = bf16[4096,128]{1,0:T(8,128)(2,1)} fusion(bf16[3328,128]{1,0:T(8,128)(2,1)S(1)} %convert_element_type.227, s32[4096]{0:T(1024)S(1)} %fusion.24), kind=kCustom, calls=%fused_computation.5.clone | custom fusion | bytes 2113536 | tf_op jit(solution)/shard_map/jit(_take)/gather | solution.py:85
  598.5 14.9 %gather_fusion.5 = bf16[4096,128]{1,0:T(8,128)(2,1)} fusion(bf16[3328,128]{1,0:T(8,128)(2,1)S(1)} %convert_element_type.224, s32[4096]{0:T(1024)S(1)} %copy-done.54), kind=kCustom, calls=%fused_computation.4.clone | custom fusion | bytes 2113536 | tf_op jit(solution)/shard_map/jit(_take)/gather | solution.py:85
  613.4 12.1 gather_fusion.4
  625.6 3.5 broadcast_select_fusion.4
  637.4 5.8 all-to-all-start.2
  656.9 40.1 %scatter_custom_fusion.3 = f32[16384,128]{1,0:T(8,128)} fusion(s32[6656]{0:T(1024)} %fusion.19, f32[6656,128]{1,0:T(8,128)} %bitcast.140, f32[]{:T(128)} %constant.13.clone.1), kind=kCustom, calls=%fused_computation.21 | custom fusion | flops 851968 | bytes 8389120 | tf_op jit(solution)/shard_map/scatter-add | solution.py:83
  700.0 39.0 %scatter_fusion.3 = f32[16384,128]{1,0:T(8,128)} fusion(f32[16384,128]{1,0:T(8,128)} %scatter_custom_fusion.3, s32[6656]{0:T(1024)S(1)} %copy-done.52, f32[6656,128]{1,0:T(8,128)S(1)} %bitcast.125), kind=kCustom, calls=%fused_computation.11 | custom fusion | flops 851968 | bytes 10250240 | tf_op jit(solution)/shard_map/scatter-add | solution.py:83
  742.0 39.0 %scatter_fusion.4 = f32[16384,128]{1,0:T(8,128)} fusion(f32[16384,128]{1,0:T(8,128)} %scatter_fusion.3, s32[6656]{0:T(1024)S(1)} %copy-done.51, f32[6656,128]{1,0:T(8,128)S(1)} %bitcast.126), kind=kCustom, calls=%fused_computation.12 | custom fusion | flops 851968 | bytes 10250240 | tf_op jit(solution)/shard_map/scatter-add | solution.py:83
  781.0 117.4 %all-reduce.2 = bf16[16384,128]{1,0:T(8,128)(2,1)} all-reduce(f32[16384,128]{1,0:T(8,128)} %scatter_fusion.4), channel_id=1, replica_groups=mesh['dev'=128] {'dev'}, use_global_device_ids=true, to_apply=%region_19.21 | all-reduce | flops 2097152 | bytes 12582912 | tf_op jit(solution)/shard_map/psum | solution.py:158
  898.4 68.8 %scatter_custom_fusion.6 = f32[4096,128]{1,0:T(8,128)} fusion(s32[12288]{0:T(1024)} %bitcast.148, bf16[12288,128]{1,0:T(8,128)(2,1)} %bitcast.45, f32[]{:T(128)} %constant.13.clone.1), kind=kCustom, calls=%fused_computation.16 | custom fusion | flops 3145728 | bytes 5243392 | tf_op jit(solution)/shard_map/scatter-add | solution.py:151
  969.9 232.4 %reduce-scatter.2.cloned.1.call-done = f32[224,128]{1,0:T(8,128)} async-done(((f32[28672,128]{1,0:T(8,128)}), f32[224,128]{1,0:T(8,128)}) %reduce-scatter.2.cloned.1.call-update) | async-done | bytes 114704 | tf_op jit(solution)/shard_map/reduce_scatter | solution.py:23
  (261 shorter events, 183.9 us)
Async XLA Ops:
  7.2 351.4 %copy-start = (bf16[512,3456]{1,0:T(8,128)(2,1)S(1)}, bf16[512,3456]{1,0:T(8,128)(2,1)}, u32[]{:S(2)}) copy-start(bf16[512,3456]{1,0:T(8,128)(2,1)} %param.24) | copy-start | bytes 10616836
  8.9 139.5 %all-to-all-start = ((s32[128,1,96]{2,1,0:T(1,128)}), s32[128,1,96]{2,1,0:T(1,128)}, u32[]{:S(2)}, u32[]{:S(2)}) async-start(s32[128,1,96]{2,1,0:T(1,128)} %copy.155), calls=%async_computation | async-start | bytes 131072 | tf_op jit(solution)/shard_map/all_to_all | solution.py:124
  108.3 9.4 copy-start.17
  108.3 9.3 copy-start.24
  117.6 8.0 copy-start.18
  117.6 8.0 copy-start.23
  125.7 8.0 copy-start.62
  125.7 8.0 copy-start.63
  208.4 51.7 %all-to-all-start.1 = ((bf16[128,96,128]{2,1,0:T(8,128)(2,1)}), bf16[128,96,128]{2,1,0:T(8,128)(2,1)}, u32[]{:S(2)}, u32[]{:S(2)}) async-start(bf16[128,96,128]{2,1,0:T(8,128)(2,1)} %broadcast_select_fusion.3), calls=%async_computation.1 | async-start | bytes 6291456 | tf_op jit(solution)/shard_map/all_to_all | solution.py:126
  218.6 983.7 %reduce-scatter.2.cloned.1.call-start = ((), (), s32[]{:S(2)}) async-start(), calls=%async_computation.4 | async-start | bytes 14794752 | tf_op jit(solution)/shard_map/reduce_scatter | solution.py:23
  354.4 3.3 copy-start.2
  354.4 3.5 copy-start.9
  354.4 3.5 copy-start.33
  359.8 19.1 %copy-start.5 = (f32[128,3456]{1,0:T(8,128)}, f32[128,3456]{1,0:T(8,128)S(1)}, u32[]{:S(2)}) copy-start(f32[128,3456]{1,0:T(8,128)S(1)} %convolution_add_fusion.2) | copy-start | bytes 5308420
  366.8 12.1 copy-start.13
  378.9 3.0 copy-start.64
  378.9 3.3 copy-start.10
  378.9 3.3 copy-start.34
  378.9 3.3 copy-start.37
  382.2 5.1 copy-start.4
  382.2 5.7 copy-start.12
  382.3 5.7 copy-start.41
  382.3 5.7 copy-start.47
  382.3 5.7 copy-start.66
  422.7 8.9 copy-start.8
  422.7 8.9 copy-start.32
  422.7 8.9 copy-start.36
  531.7 3.0 copy-start.29
  531.7 3.6 copy-start.30
  531.7 4.3 copy-start.57
  531.7 5.0 copy-start.56
  531.7 5.7 copy-start.55
  531.7 6.4 copy-start.39
  544.9 19.9 %copy-start.3 = (bf16[3456,512]{1,0:T(8,128)(2,1)S(1)}, bf16[3456,512]{1,0:T(8,128)(2,1)}, u32[]{:S(2)}) copy-start(bf16[3456,512]{1,0:T(8,128)(2,1)} %param.23) | copy-start | bytes 10616836
  569.6 3.5 copy-start.6
  569.7 3.5 copy-start.16
  575.7 3.5 copy-start.14
  575.7 3.5 copy-start.15
  583.5 15.0 %copy-start.54 = (s32[4096]{0:T(1024)S(1)}, s32[4096]{0:T(1024)}, u32[]{:S(2)}) copy-start(s32[4096]{0:T(1024)} %fusion.23) | copy-start | bytes 49156
  598.5 14.9 %copy-start.53 = (s32[4096]{0:T(1024)S(1)}, s32[4096]{0:T(1024)}, u32[]{:S(2)}) copy-start(s32[4096]{0:T(1024)} %fusion.22) | copy-start | bytes 49156
  613.4 12.1 copy-start.61
  625.5 3.5 copy-start.50
  625.6 4.2 copy-start.22
  625.6 4.2 copy-start.60
  637.4 5.8 copy-start.42
  637.4 6.5 copy-start.19
  637.4 261.0 %all-to-all-start.2 = ((bf16[128,96,128]{2,1,0:T(8,128)(2,1)}), bf16[128,96,128]{2,1,0:T(8,128)(2,1)}, u32[]{:S(2)}, u32[]{:S(2)}) async-start(bf16[128,96,128]{2,1,0:T(8,128)(2,1)} %pad_maximum_fusion), calls=%async_computation.3 | async-start | bytes 6291456 | tf_op jit(solution)/shard_map/all_to_all | solution.py:148
  898.4 311.7 %copy-start.1 = (bf16[512,3456]{1,0:T(8,128)(2,1)S(1)}, bf16[512,3456]{1,0:T(8,128)(2,1)}, u32[]{:S(2)}) copy-start(bf16[512,3456]{1,0:T(8,128)(2,1)} %param.24) | copy-start | bytes 10616836
  (24 other events, 46.6 us)
Sparse Core Ops, SparseCore 0:
  531.9 670.3 reduce-scatter.1
where the time goes:
time: 1240 us; the launch traced here: 1220 us
  local copies, waits for them, and re-layouts  395 us (32%)
  other arithmetic  358 us (29%)
  waiting for transfers between devices  250 us (20%)
  blocking collectives  117 us (9%)
  matrix products  52.9 us (4%)
  starting transfers between devices  28 us (2%)
  between operations  15.9 us (1%)
    reduce_scatter x1, waiting for transfers between devices, one_scatter(): lax.psum_scatter(lines, axis, tiled=True).reshape(-1)  232 us
    scatter-add x3, other arithmetic, micro_pass(): grad_f = grad_f.at[freq_rows.reshape(-1)].add(spread)  118 us
    psum x1, blocking collectives, on_device(): freq_total = lax.psum(grad_f, 'dev').astype(jnp.bfloat16)  117 us
    scatter-add x3, other arithmetic, micro_pass(): inf_part = jnp.zeros((samples * features, emb_width), jnp.float32).at[slo...  72.7 us
    scatter-add x1, other arithmetic, on_device(): grad_inf.at[jnp.minimum(asked, rows_limit - 1).reshape(-1)]  68.8 us
    gather x3, local copies, waits for them, and re-layouts, micro_pass(): jnp.take(freq_table, freq_rows, axis=0)  51 us
    gather x1, local copies, waits for them, and re-layouts, on_device(): looked_up = jnp.take(inf_table, jnp.minimum(asked, rows_limit - 1), axis=0)  47.1 us
    gather x3, local copies, waits for them, and re-layouts, micro_pass(): jnp.take(pooled_low, slot_idx, axis=0)  42 us
  transfers between devices with their start and end apart: 4, of which 2 were waited for; matrix products, arithmetic and copies ran while one was open for 38% of the time, Pallas kernels for 0%

commit v1 on v0

v1 whole, which is shorter than its diff:
```python
import functools
import math

import jax
import jax.numpy as jnp
from jax import lax
from jax.experimental import pallas as pl
from jax.experimental.pallas import tpu as pltpu
from jax.sharding import PartitionSpec as P

loss_scale = 1024.0
f32 = jnp.float32
bf16 = jnp.bfloat16
MIB = 1024 * 1024
SMEM = pl.BlockSpec(memory_space=pltpu.SMEM)
VMEM = pl.BlockSpec(memory_space=pltpu.VMEM)
NT = (((1,), (1,)), ((), ()))
TN = (((0,), (0,)), ((), ()))


def local_call(kernel, outs, in_specs, scratch, name, limit, flops, bytes_accessed):
    return pl.pallas_call(
        kernel,
        out_shape=[jax.ShapeDtypeStruct(s, d) for s, d in outs],
        in_specs=in_specs,
        out_specs=[VMEM] * len(outs),
        scratch_shapes=scratch,
        compiler_params=pltpu.CompilerParams(vmem_limit_bytes=limit * MIB),
        cost_estimate=pl.CostEstimate(
            flops=flops, bytes_accessed=bytes_accessed, transcendentals=0
        ),
        name=name,
    )


def freq_kernel(blocks, samples, ids, table_ref, out, table):
    table[...] = table_ref[...].astype(f32)
    unroll = 32

    def group(g, carry):
        def some(k, carry):
            for u in range(unroll):
                s = k * unroll + u
                first = ids[g * 2 * samples + s]
                second = ids[g * 2 * samples + samples + s]
                out[pl.ds(g * samples + s, 1), :] = (
                    table[pl.ds(first, 1), :] + table[pl.ds(second, 1), :]
                )
            return carry

        return lax.fori_loop(0, samples // unroll, some, carry)

    lax.fori_loop(0, blocks, group, 0)


def lookup_kernel(peers, stride, start, cap, asked, table_ref, out, table, rows):
    table[...] = table_ref[...].astype(f32)

    def peer(d, carry):
        for c in range(cap):
            r = asked[d * stride + start + c]
            rows[pl.ds(d * cap + c, 1), :] = table[pl.ds(r, 1), :]
        return carry

    lax.fori_loop(0, peers, peer, 0)
    out[...] = rows[...].astype(bf16)


def micro_kernel(
    peers,
    cap,
    features,
    slot_start,
    freq_start,
    loss_mult,
    slots,
    out_b,
    fetched,
    freq_part,
    bottom,
    labels,
    cross_u,
    cross_v,
    bias,
    weight,
    returned,
    d_pooled,
    x_zero,
    hidden_out,
    d_hidden_out,
    gate_low,
    grad_bw,
    arrived,
    acc0,
    acc1,
    acc2,
    acc3,
    gate,
):
    samples, width = x_zero.shape
    emb = bottom.shape[1]
    n_slots = features * samples
    accs = (acc0, acc1, acc2, acc3)
    arrived[...] = fetched[...].astype(f32)
    acc0[pl.ds(0, n_slots), :] = freq_part[pl.ds(freq_start, n_slots), :]
    for a in accs[1:]:
        a[...] = jnp.zeros_like(a)

    def add_peer(o, carry):
        for c in range(0, cap, 4):
            at = [slots[slot_start + (c + j) * peers + o] for j in range(4)]
            new = [
                accs[j][pl.ds(at[j], 1), :] + arrived[pl.ds(o * cap + c + j, 1), :]
                for j in range(4)
            ]
            for j in range(4):
                accs[j][pl.ds(at[j], 1), :] = new[j]
        return carry

    lax.fori_loop(0, peers, add_peer, 0)

    x_zero[:, 0:emb] = bottom[...]
    for f in range(features):
        rows = pl.ds(f * samples, samples)
        total = (acc0[rows, :] + acc1[rows, :]) + (acc2[rows, :] + acc3[rows, :])
        x_zero[:, (f + 1) * emb : (f + 2) * emb] = total.astype(bf16)

    hidden = jnp.dot(x_zero[...], cross_u[...], preferred_element_type=f32).astype(bf16)
    hidden_out[...] = hidden
    chunk = 3 * emb
    chunks = width // chunk
    partial = jnp.zeros((samples, emb), f32)
    for k in range(chunks):
        cols = slice(k * chunk, (k + 1) * chunk)
        value = jnp.dot(hidden, cross_v[:, cols], preferred_element_type=f32) + bias[:, cols]
        gate[:, cols] = value
        x_float = x_zero[:, cols].astype(f32)
        scored = (x_float * value + x_float) * weight[:, cols]
        for j in range(3):
            partial = partial + scored[:, j * emb : (j + 1) * emb]
    logits = jnp.sum(partial, axis=1, keepdims=True) + out_b[0]
    d_logit = (jax.nn.sigmoid(logits) - labels[...]) * loss_mult
    for k in range(chunks):
        cols = slice(k * chunk, (k + 1) * chunk)
        x_float = x_zero[:, cols].astype(f32)
        d_gate = (d_logit * weight[:, cols]) * x_float
        gate_low[:, cols] = d_gate.astype(bf16)
        crossed = x_float * gate[:, cols] + x_float
        grad_bw[0:1, cols] = jnp.sum(d_gate, axis=0, keepdims=True)
        grad_bw[1:2, cols] = jnp.sum(d_logit * crossed, axis=0, keepdims=True)
    d_hidden = lax.dot_general(
        gate_low[...], cross_v[...], NT, preferred_element_type=f32
    ).astype(bf16)
    d_hidden_out[...] = d_hidden
    for k in range(chunks):
        cols = slice(k * chunk, (k + 1) * chunk)
        back = lax.dot_general(d_hidden, cross_u[cols, :], NT, preferred_element_type=f32)
        d_input = (d_logit * weight[:, cols]) * (gate[:, cols] + 1.0) + back
        for j in range(3):
            f = 3 * k + j - 1
            if f >= 0:
                block = d_input[:, j * emb : (j + 1) * emb]
                d_pooled[f * samples : (f + 1) * samples, :] = block
                acc0[f * samples : (f + 1) * samples, :] = block
    acc0[n_slots:, :] = jnp.zeros((acc0.shape[0] - n_slots, emb), f32)

    def take_peer(o, carry):
        for c in range(cap):
            at = slots[slot_start + c * peers + o]
            arrived[pl.ds(o * cap + c, 1), :] = acc0[pl.ds(at, 1), :]
        return carry

    lax.fori_loop(0, peers, take_peer, 0)
    returned[...] = arrived[...].astype(bf16)


def dense_grad_kernel(peers, per, core, x0, x1, x2, g0, g1, g2, h0, h1, h2, e0, e1, e2, keep, send, total):
    width = x0.shape[1]
    rank = h0.shape[1]
    chunk = 128
    h_all = jnp.concatenate([h0[...], h1[...], h2[...]], axis=0)
    e_all = jnp.concatenate([e0[...], e1[...], e2[...]], axis=0)
    for k in range(width // chunk):
        cols = slice(k * chunk, (k + 1) * chunk)
        x_all = jnp.concatenate([x0[:, cols], x1[:, cols], x2[:, cols]], axis=0)
        g_all = jnp.concatenate([g0[:, cols], g1[:, cols], g2[:, cols]], axis=0)
        total[cols, 0:rank] = lax.dot_general(x_all, e_all, TN, preferred_element_type=f32)
        total[cols, rank : 2 * rank] = lax.dot_general(
            g_all, h_all, TN, preferred_element_type=f32
        )
    total[width:, :] = jnp.zeros((total.shape[0] - width, 2 * rank), f32)
    rows = keep.shape[1]
    even = core[0] == 0

    def pairs(q, carry):
        base = q * 8 * per

        def block(i):
            skip = i * per % 8
            window = total[pl.ds(pl.multiple_of(base + (i * per - skip), 8), rows + 8), :]
            return window[skip : skip + rows]

        for i in range(4):
            first = block(2 * i)
            second = block(2 * i + 1)
            keep[q * 4 + i] = jnp.where(even, first, second).astype(bf16)
            send[q * 4 + i] = jnp.where(even, second, first).astype(bf16)
        return carry

    lax.fori_loop(0, peers // 8, pairs, 0)


def freq_grad_kernel(features, core, ids, d0, d1, d2, keep, send, acc0, acc1, acc2, acc3):
    accs = (acc0, acc1, acc2, acc3)
    samples = d0.shape[0] // features
    for a in accs:
        a[...] = jnp.zeros_like(a)
    unroll = 32
    for m, source in enumerate((d0, d1, d2)):
        start = m * features * 2 * samples

        def feature(f, carry):
            def some(k, carry):
                for u in range(0, unroll, 2):
                    s = k * unroll + u
                    at = [
                        ids[start + (2 * f + h) * samples + s + j]
                        for j in range(2)
                        for h in range(2)
                    ]
                    value = [source[pl.ds(f * samples + s + j, 1), :] for j in range(2)]
                    new = [accs[j][pl.ds(at[j], 1), :] + value[j // 2] for j in range(4)]
                    for j in range(4):
                        accs[j][pl.ds(at[j], 1), :] = new[j]
                return carry

            return lax.fori_loop(0, samples // unroll, some, carry)

        lax.fori_loop(0, features, feature, 0)
    rows = 128
    mine = core[0]

    def block(q, carry):
        for ref, parity in ((keep, mine), (send, 1 - mine)):
            at = pl.ds(pl.multiple_of((2 * q + parity) * rows, rows), rows)
            total = (acc0[at, :] + acc1[at, :]) + (acc2[at, :] + acc3[at, :])
            ref[q] = total.astype(bf16)
        return carry

    lax.fori_loop(0, keep.shape[0], block, 0)


def owner_kernel(peers, stride, cap, asked, r0, r1, r2, out, rows, acc0, acc1, acc2, acc3):
    accs = (acc0, acc1, acc2, acc3)
    for a in accs:
        a[...] = jnp.zeros_like(a)
    for m, source in enumerate((r0, r1, r2)):
        rows[...] = source[...].astype(f32)

        def peer(d, carry):
            for c in range(0, cap, 4):
                at = [asked[d * stride + m * cap + c + j] for j in range(4)]
                new = [
                    accs[j][pl.ds(at[j], 1), :] + rows[pl.ds(d * cap + c + j, 1), :]
                    for j in range(4)
                ]
                for j in range(4):
                    accs[j][pl.ds(at[j], 1), :] = new[j]
            return carry

        lax.fori_loop(0, peers, peer, 0)
    at = slice(0, out.shape[0])
    out[...] = ((acc0[at, :] + acc1[at, :]) + (acc2[at, :] + acc3[at, :])).astype(bf16)


def on_device(
    bottom,
    labels,
    freq_ids,
    req_rows,
    req_slot,
    freq_table,
    inf_table,
    cross_u,
    cross_v,
    cross_bias,
    out_w,
    out_b,
):
    devices = lax.axis_size("dev")
    micro, samples, emb = bottom.shape
    features = freq_ids.shape[2]
    hot = freq_ids.shape[3]
    owned = inf_table.shape[0]
    cap = req_rows.shape[3]
    width, rank = cross_u.shape
    freq_rows = freq_table.shape[0]
    n_slots = samples * features
    n_req = devices * cap
    per = width // devices
    loss_mult = loss_scale / math.sqrt(micro * samples * devices)
    me = lax.axis_index("dev")
    core = (me % 2).astype(jnp.int32).reshape(1)
    other_core = [(d, d ^ 1) for d in range(devices)]
    same_core = [list(range(c, devices, 2)) for c in range(2)]

    ids = jnp.transpose(freq_ids, (0, 2, 3, 1)).reshape(-1)
    rows_mc = jnp.transpose(req_rows[:, 0], (0, 2, 1))
    slot_mc = jnp.transpose(req_slot[:, 0], (0, 2, 1))
    is_live = (rows_mc < owned) & (slot_mc < n_slots)
    place = jnp.where(
        is_live, (slot_mc % features) * samples + slot_mc // features, n_slots
    ).reshape(-1)
    line = jnp.where(
        (req_rows < owned) & (req_slot < n_slots), req_rows, owned
    )[:, 0]
    line = jnp.transpose(line, (1, 0, 2)).reshape(devices, micro * cap)
    stride = -(-micro * cap // 128) * 128
    line = jnp.pad(line, ((0, 0), (0, stride - micro * cap)), constant_values=owned)
    asked = lax.all_to_all(line, "dev", split_axis=0, concat_axis=0, tiled=True).reshape(-1)
    asked_row = jnp.minimum(asked, owned - 1)

    (freq_part,) = local_call(
        functools.partial(freq_kernel, micro * features, samples),
        [((micro * n_slots, emb), f32)],
        [SMEM, VMEM],
        [pltpu.VMEM((freq_rows, emb), f32)],
        "freq_rows",
        40,
        0,
        50 * MIB,
    )(ids, freq_table)

    weight = out_w.astype(f32).reshape(1, width)
    bias = cross_bias.reshape(1, width)
    label_cols = labels.astype(f32).reshape(micro, samples, 1)
    bias_b = out_b.reshape(1)
    outs = []
    arrived = []
    for m in range(micro):
        (looked,) = local_call(
            functools.partial(lookup_kernel, devices, stride, m * cap, cap),
            [((n_req, emb), bf16)],
            [SMEM, VMEM],
            [pltpu.VMEM((owned, emb), f32), pltpu.VMEM((n_req, emb), f32)],
            f"lookup{m}",
            24,
            0,
            20 * MIB,
        )(asked_row, inf_table)
        fetched = lax.all_to_all(
            looked.reshape(devices, cap, emb), "dev", split_axis=0, concat_axis=0, tiled=True
        ).reshape(n_req, emb)
        out = local_call(
            functools.partial(
                micro_kernel,
                devices,
                cap,
                features,
                m * n_req,
                m * n_slots,
                loss_mult,
            ),
            [
                ((n_req, emb), bf16),
                ((n_slots, emb), f32),
                ((samples, width), bf16),
                ((samples, rank), bf16),
                ((samples, rank), bf16),
                ((samples, width), bf16),
                ((2, width), f32),
            ],
            [SMEM, SMEM] + [VMEM] * 8,
            [pltpu.VMEM((n_req, emb), f32)]
            + [pltpu.VMEM((n_slots + 8, emb), f32)] * 4
            + [pltpu.VMEM((samples, width), f32)],
            f"micro{m}",
            48,
            6 * samples * width * rank,
            60 * MIB,
        )(
            place,
            bias_b,
            fetched,
            freq_part,
            bottom[m],
            label_cols[m],
            cross_u,
            cross_v,
            bias,
            weight,
        )
        outs.append(out)
        arrived.append(
            lax.all_to_all(
                out[0].reshape(devices, cap, emb), "dev", split_axis=0, concat_axis=0, tiled=True
            ).reshape(n_req, emb)
        )
    d_pooled = [o[1] for o in outs]
    grad_bw = lax.psum((outs[0][6] + outs[1][6]) + outs[2][6], "dev")

    rows_pad = -(-per // 16) * 16
    keep, send = local_call(
        functools.partial(dense_grad_kernel, devices, per),
        [((devices // 2, rows_pad, 2 * rank), bf16)] * 2,
        [SMEM] + [VMEM] * 12,
        [pltpu.VMEM((width + 16, 2 * rank), f32)],
        "dense_grads",
        48,
        12 * samples * width * rank,
        40 * MIB,
    )(
        core,
        *[o[2] for o in outs],
        *[o[5] for o in outs],
        *[o[3] for o in outs],
        *[o[4] for o in outs],
    )
    got = lax.ppermute(send, "dev", other_core)
    both = (keep.astype(f32) + got.astype(f32)).astype(bf16)
    parts = lax.all_to_all(
        both, "dev", split_axis=0, concat_axis=0, axis_index_groups=same_core, tiled=True
    )
    dense = jnp.sum(parts.astype(f32), axis=0)[:per]
    grad_u = dense[:, :rank]
    grad_v = dense[:, rank:].T

    per_freq = freq_rows // devices
    keep, send = local_call(
        functools.partial(freq_grad_kernel, features),
        [((devices // 2, per_freq, emb), bf16)] * 2,
        [SMEM, SMEM] + [VMEM] * 3,
        [pltpu.VMEM((freq_rows, emb), f32)] * 4,
        "freq_grads",
        56,
        0,
        120 * MIB,
    )(core, ids, *d_pooled)
    got = lax.ppermute(send, "dev", other_core)
    both = (keep.astype(f32) + got.astype(f32)).astype(bf16)
    parts = lax.all_to_all(
        both, "dev", split_axis=0, concat_axis=0, axis_index_groups=same_core, tiled=True
    )
    mine = jnp.sum(parts.astype(f32), axis=0).astype(bf16)
    grad_freq = lax.all_gather(mine, "dev", tiled=True)

    (grad_inf,) = local_call(
        functools.partial(owner_kernel, devices, stride, cap),
        [((owned, emb), bf16)],
        [SMEM] + [VMEM] * 3,
        [pltpu.VMEM((n_req, emb), f32)] + [pltpu.VMEM((owned + 8, emb), f32)] * 4,
        "owner_grads",
        32,
        0,
        60 * MIB,
    )(asked, *arrived)

    grad_b = lax.dynamic_slice_in_dim(grad_bw[0], me * per, per)
    grad_w = lax.dynamic_slice_in_dim(grad_bw[1], me * per, per)
    return (grad_u, grad_v, grad_b, grad_w, grad_freq, grad_inf)


def solution(mesh):
    in_specs = (
        P(None, "dev", None),
        P(None, "dev"),
        P(None, "dev", None, None),
        P(None, "dev", None, None),
        P(None, "dev", None, None),
        P(),
        P("dev", None),
        P(),
        P(),
        P(),
        P(),
        P(),
    )
    out_specs = (P("dev", None), P(None, "dev"), P("dev"), P("dev"), P(), P("dev", None))
    return jax.shard_map(
        on_device, mesh=mesh, in_specs=in_specs, out_specs=out_specs, check_vma=False
    )
```

time: 1240 us -> 509 us (0.41); the launches traced: 1220 us -> 507 us
  local copies, waits for them, and re-layouts: 395 us -> 37.8 us
  other arithmetic: 358 us -> 18.4 us
  waiting for transfers between devices: 250 us -> 51.7 us
  Pallas kernels: 0 us -> 168 us
  blocking collectives: 117 us -> 180 us
  matrix products: 52.9 us -> 0 us
    scatter-add x7 -> x0, other arithmetic: 260 us -> none  [the longest x3 118 us: micro_pass(): grad_f = grad_f.at[freq_rows.reshape(-1)].add(spread)]
    reduce_scatter x1 -> x0, waiting for transfers between devices: 232 us -> none  [one_scatter(): lax.psum_scatter(lines, axis, tiled=True).reshape(-1)]
    pallas_call x0 -> x10, Pallas kernels: none -> 168 us  [the longest x3 57.2 us: on_device(): local_call(functools.partial(micro_kernel, devices, cap, features, m * n_...]
    gather x7 -> x0, local copies, waits for them, and re-layouts: 140 us -> none  [the longest x3 51 us: micro_pass(): jnp.take(freq_table, freq_rows, axis=0)]
    all_to_all x0 -> x3, blocking collectives: none -> 71.4 us  [the longest x2 50.7 us: on_device(): lax.all_to_all(out[0].reshape(devices, cap, emb), 'dev', split_axis=0, co...]
    dot_general x18 -> x0, matrix products: 52.9 us -> none  [the longest x3 15.5 us: micro_pass(): jnp.dot(hidden.T, gate_low, preferred_element_type=jnp.float32)]
    reshape x11 -> x3, local copies, waits for them, and re-layouts: 49.5 us -> 1.56 us  [the longest x1 0.94 us: on_device(): ids = jnp.transpose(freq_ids, (0, 2, 3, 1)).reshape(-1)]
    concatenate x1 -> x0, local copies, waits for them, and re-layouts: 34.5 us -> none  [one_scatter(): lines = jnp.concatenate([b.reshape(peers, -1) for b in blocks], axis=1)]
  transfers between devices with their start and end apart: 4 -> 9, of which waited for: 2 -> 5; matrix products, arithmetic and copies ran while one was open for 38% -> 3% of each run, Pallas kernels for 0% -> 21%
where the time goes in v1:
time: 509 us; the launch traced here: 507 us
  blocking collectives  180 us (35%)
  Pallas kernels  168 us (33%)
  waiting for transfers between devices  51.7 us (10%)
  local copies, waits for them, and re-layouts  37.8 us (7%)
  starting transfers between devices  36.2 us (7%)
  other arithmetic  18.4 us (4%)
  between operations  15.1 us (3%)
    psum x1, blocking collectives, on_device(): grad_bw = lax.psum(outs[0][6] + outs[1][6] + outs[2][6], 'dev')  109 us
    pallas_call x3, Pallas kernels, on_device(): local_call(functools.partial(micro_kernel, devices, cap, features, m * n_...  57.2 us
    all_to_all x2, blocking collectives, on_device(): lax.all_to_all(out[0].reshape(devices, cap, emb), 'dev', split_axis=0, co...  50.7 us
    pallas_call x1, Pallas kernels, on_device(): local_call(functools.partial(freq_grad_kernel, features), [((devices // 2...  35.3 us
    unnamed x93, local copies, waits for them, and re-layouts  33.9 us
    all_to_all x3, waiting for transfers between devices, on_device(): lax.all_to_all(looked.reshape(devices, cap, emb), 'dev', split_axis=0, co...  25.2 us
    pallas_call x1, Pallas kernels, on_device(): local_call(functools.partial(freq_kernel, micro * features, samples), [((...  23.1 us
    pallas_call x1, Pallas kernels, on_device(): local_call(functools.partial(owner_kernel, devices, stride, cap), [((owne...  21 us
  transfers between devices with their start and end apart: 9, of which 5 were waited for; matrix products, arithmetic and copies ran while one was open for 3% of the time, Pallas kernels for 21%

profile of v1, /device:TPU:1, one launch (start us, length us, event | category | flops | bytes accessed | tf_op | source)
XLA Modules:
  0.0 507.4 jit_solution(5750350950707944653)
XLA Ops:
  8.1 20.7 %all_to_all.49 = s32[128,1,128]{2,1,0:T(1,128)S(1)} all-to-all(s32[128,1,128]{2,1,0:T(1,128)S(1)} %copy.53), channel_id=1, replica_groups=mesh['dev'=128] {'dev'}, dimensions={0} | all-to-all | bytes 131072 | tf_op jit(solution)/shard_map/all_to_all | solution.py:320
  28.8 1.2 copy-done.1
  30.0 6.7 %lookup2.1 = bf16[4096,128]{1,0:T(8,128)(2,1)} custom-call(s32[16384]{0:T(1024)S(1)} %broadcast_minimum_fusion.asked, bf16[4096,128]{1,0:T(8,128)(2,1)S(1)} %copy-done.1), custom_call_target="tpu_custom_call" | custom-call | bytes 20971520 | tf_op jit(solution)/shard_map/lookup2/pallas_call | solution.py:341
  36.7 4.8 all-to-all-start.3
  41.5 6.7 %lookup1.1 = bf16[4096,128]{1,0:T(8,128)(2,1)} custom-call(s32[16384]{0:T(1024)S(1)} %broadcast_minimum_fusion.asked, bf16[4096,128]{1,0:T(8,128)(2,1)S(1)} %copy-done.2), custom_call_target="tpu_custom_call" | custom-call | bytes 20971520 | tf_op jit(solution)/shard_map/lookup1/pallas_call | solution.py:341
  48.3 12.5 %all-to-all-done.3 = bf16[128,32,128]{2,1,0:T(8,128)(2,1)S(1)} async-done(((bf16[128,32,128]{2,1,0:T(8,128)(2,1)}), bf16[128,32,128]{2,1,0:T(8,128)(2,1)S(1)}, u32[]{:S(2)}, u32[]{:S(2)}) %all-to-all-start.3) | async-done | bytes 1048608 | tf_op jit(solution)/shard_map/all_to_all | solution.py:351
  60.8 4.6 all-to-all-start.2
  65.4 6.7 %lookup0.1 = bf16[4096,128]{1,0:T(8,128)(2,1)} custom-call(s32[16384]{0:T(1024)S(1)} %broadcast_minimum_fusion.asked, bf16[4096,128]{1,0:T(8,128)(2,1)S(1)} %copy-done.2), custom_call_target="tpu_custom_call" | custom-call | bytes 20971520 | tf_op jit(solution)/shard_map/lookup0/pallas_call | solution.py:341
  72.1 12.7 %all-to-all-done.2 = bf16[128,32,128]{2,1,0:T(8,128)(2,1)S(1)} async-done(((bf16[128,32,128]{2,1,0:T(8,128)(2,1)}), bf16[128,32,128]{2,1,0:T(8,128)(2,1)S(1)}, u32[]{:S(2)}, u32[]{:S(2)}) %all-to-all-start.2) | async-done | bytes 1048608 | tf_op jit(solution)/shard_map/all_to_all | solution.py:351
  84.8 4.6 all-to-all-start.1
  91.1 0.9 reshape.105.ids
  92.1 2.2 copy-done.3
  94.3 23.1 %freq_rows.1.freq_part = f32[9984,128]{1,0:T(8,128)S(1)} custom-call(s32[19968]{0:T(1024)S(1)} %reshape.105.ids, bf16[16384,128]{1,0:T(8,128)(2,1)S(1)} %copy-done.3), custom_call_target="tpu_custom_call" | custom-call | bytes 52428800 | tf_op jit(solution)/shard_map/freq_rows/pallas_call | solution.py:323
  117.4 2.3 copy-done
  120.4 19.0 %micro2.1 = (bf16[4096,128]{1,0:T(8,128)(2,1)S(1)}, f32[3328,128]{1,0:T(8,128)S(1)}, bf16[128,3456]{1,0:T(8,128)(2,1)S(1)}, bf16[128,512]{1,0:T(8,128)(2,1)S(1)}...) custom-call(s32[12288]{0:T(1024)S(1)} %bitcast.116, f32[1]{0:T(128)} %bitcast.106.out_b, ...), custom_call_target="tpu_custom_call" | custom-call | flops 1358954496 | bytes 62914560 | tf_op jit(solution)/shard_map/micro2/pallas_call | solution.py:354
  139.5 1.2 copy-done.4
  140.6 1.0 copy-done.7
  141.6 0.9 copy-done.16
  144.8 19.1 %micro1.1 = (bf16[4096,128]{1,0:T(8,128)(2,1)S(1)}, f32[3328,128]{1,0:T(8,128)S(1)}, bf16[128,3456]{1,0:T(8,128)(2,1)S(1)}, bf16[128,512]{1,0:T(8,128)(2,1)S(1)}...) custom-call(s32[12288]{0:T(1024)S(1)} %bitcast.117, f32[1]{0:T(128)} %bitcast.105.out_b, ...), custom_call_target="tpu_custom_call" | custom-call | flops 1358954496 | bytes 62914560 | tf_op jit(solution)/shard_map/micro1/pallas_call | solution.py:354
  163.8 1.3 copy-done.5
  165.1 1.0 copy-done.9
  167.0 1.0 copy-done.22
  169.3 19.1 %micro0.1 = (bf16[4096,128]{1,0:T(8,128)(2,1)S(1)}, f32[3328,128]{1,0:T(8,128)S(1)}, bf16[128,3456]{1,0:T(8,128)(2,1)S(1)}, bf16[128,512]{1,0:T(8,128)(2,1)S(1)}...) custom-call(s32[12288]{0:T(1024)S(1)} %bitcast.118, f32[1]{0:T(128)} %bitcast.104.out_b, ...), custom_call_target="tpu_custom_call" | custom-call | flops 1358954496 | bytes 62914560 | tf_op jit(solution)/shard_map/micro0/pallas_call | solution.py:354
  188.4 1.2 copy-done.6
  189.6 1.0 copy-done.11
  190.6 0.9 copy-done.24
  193.8 35.3 %freq_grads.1 = (bf16[64,128,128]{2,1,0:T(8,128)(2,1)}, bf16[64,128,128]{2,1,0:T(8,128)(2,1)}) custom-call(s32[1]{0:T(128)} %bitcast.core, s32[19968]{0:T(1024)} %copy-done.12, f32[3328,128]{1,0:T(8,128)} %copy-done.6, f32[3328,128]{1,0:T(8,128)} %copy-done.5, f32[3328,128]{1,0:T(8,128)} %copy-done.4), custom_call_target="tpu_custom_call" | custom-call | bytes 125829120 | tf_op jit(solution)/shard_map/freq_grads/pallas_call | solution.py:429
  229.1 1.4 collective-permute-start.1
  230.5 4.0 collective-permute-done.1
  234.5 3.9 add_convert_fusion.1
  238.4 9.9 %all-to-all-start.5 = ((bf16[64,128,128]{2,1,0:T(8,128)(2,1)}), bf16[64,128,128]{2,1,0:T(8,128)(2,1)}, u32[]{:S(2)}, u32[]{:S(2)}) async-start(bf16[64,128,128]{2,1,0:T(8,128)(2,1)} %add_convert_fusion.1), calls=%async_computation.5 | async-start | bytes 4194304 | tf_op jit(solution)/shard_map/all_to_all | solution.py:441
  248.5 1.2 copy-done.21
  249.6 1.2 copy-done.23
  250.8 1.2 copy-done.25
  252.0 1.2 copy-done.27
  256.8 11.1 %dense_grads.1 = (bf16[64,32,1024]{2,1,0:T(8,128)(2,1)}, bf16[64,32,1024]{2,1,0:T(8,128)(2,1)}) custom-call(s32[1]{0:T(128)} %bitcast.core, bf16[128,3456]{1,0:T(8,128)(2,1)S(1)} %copy-done.25, bf16[128,3456]{1,0:T(8,128)(2,1)S(1)} %copy-done.21, bf16[128,3456]{1,0:T(8,128)(2,1)S(1)} %copy-done.17, bf16[128,3456]{1,0:T(8,128)(2,1)S(1)} %copy-done.27, ...), custom_call_target="tpu_custom_call" | custom-call | flops 2717908992 | bytes 41943040 | tf_op jit(solution)/shard_map/dense_grads/pallas_call | solution.py:403
  268.5 7.3 %all-to-all-done.5 = bf16[64,128,128]{2,1,0:T(8,128)(2,1)} async-done(((bf16[64,128,128]{2,1,0:T(8,128)(2,1)}), bf16[64,128,128]{2,1,0:T(8,128)(2,1)}, u32[]{:S(2)}, u32[]{:S(2)}) %all-to-all-start.5) | async-done | bytes 2097184 | tf_op jit(solution)/shard_map/all_to_all | solution.py:441
  275.8 2.5 reduce_sum.22
  278.4 26.4 %all_to_all.50 = bf16[128,32,128]{2,1,0:T(8,128)(2,1)S(1)} all-to-all(bf16[128,32,128]{2,1,0:T(8,128)(2,1)S(1)} %bitcast.113), channel_id=1, replica_groups=mesh['dev'=128] {'dev'}, dimensions={0} | all-to-all | bytes 2097152 | tf_op jit(solution)/shard_map/all_to_all | solution.py:395
  304.7 24.4 %all_to_all.51 = bf16[128,32,128]{2,1,0:T(8,128)(2,1)S(1)} all-to-all(bf16[128,32,128]{2,1,0:T(8,128)(2,1)S(1)} %bitcast.114), channel_id=1, replica_groups=mesh['dev'=128] {'dev'}, dimensions={0} | all-to-all | bytes 2097152 | tf_op jit(solution)/shard_map/all_to_all | solution.py:395
  329.1 4.6 all-to-all-start.6
  333.7 8.0 %add_convert_fusion = bf16[64,32,1024]{2,1,0:T(8,128)(2,1)} fusion(bf16[64,32,1024]{2,1,0:T(8,128)(2,1)} %collective-permute-done, bf16[64,32,1024]{2,1,0:T(8,128)(2,1)} %get-tuple-element.43), kind=kLoop, calls=%fused_computation.1 | loop fusion | flops 8388608 | bytes 12582912 | tf_op jit(solution)/shard_map/convert_element_type | solution.py:420
  341.7 15.1 %all-to-all-done.6 = bf16[128,32,128]{2,1,0:T(8,128)(2,1)S(1)} async-done(((bf16[128,32,128]{2,1,0:T(8,128)(2,1)}), bf16[128,32,128]{2,1,0:T(8,128)(2,1)S(1)}, u32[]{:S(2)}, u32[]{:S(2)}) %all-to-all-start.6) | async-done | bytes 1048608 | tf_op jit(solution)/shard_map/all_to_all | solution.py:395
  356.8 5.7 %all-to-all-start.4 = ((bf16[64,32,1024]{2,1,0:T(8,128)(2,1)}), bf16[64,32,1024]{2,1,0:T(8,128)(2,1)}, u32[]{:S(2)}, u32[]{:S(2)}) async-start(bf16[64,32,1024]{2,1,0:T(8,128)(2,1)} %add_convert_fusion), calls=%async_computation.4 | async-start | bytes 8388608 | tf_op jit(solution)/shard_map/all_to_all | solution.py:421
  362.5 109.1 %psum.7 = f32[2,3456]{1,0:T(2,128)S(1)} all-reduce(f32[2,3456]{1,0:T(2,128)S(1)} %add_add_fusion), channel_id=1, replica_groups=mesh['dev'=128] {'dev'}, use_global_device_ids=true, to_apply=%region_1.2 | all-reduce | flops 6912 | bytes 55296 | tf_op jit(solution)/shard_map/psum | solution.py:400
  472.2 21.0 %owner_grads.1 = bf16[4096,128]{1,0:T(8,128)(2,1)} custom-call(s32[16384]{0:T(1024)S(1)} %bitcast.120, bf16[4096,128]{1,0:T(8,128)(2,1)S(1)} %bitcast.109, bf16[4096,128]{1,0:T(8,128)(2,1)S(1)} %bitcast.108, bf16[4096,128]{1,0:T(8,128)(2,1)S(1)} %bitcast.107), custom_call_target="tpu_custom_call" | custom-call | bytes 62914560 | tf_op jit(solution)/shard_map/owner_grads/pallas_call | solution.py:447
  493.2 3.0 convert_reduce_fusion
  496.8 3.7 copy.61
  (100 shorter events, 15.0 us)
Async XLA Ops:
  28.8 1.2 copy-start.1
  30.0 11.5 %copy-start.2 = (bf16[4096,128]{1,0:T(8,128)(2,1)S(1)}, bf16[4096,128]{1,0:T(8,128)(2,1)}, u32[]{:S(2)}) copy-start(bf16[4096,128]{1,0:T(8,128)(2,1)} %table_ref.7) | copy-start | bytes 3145732
  36.7 24.1 %all-to-all-start.3 = ((bf16[128,32,128]{2,1,0:T(8,128)(2,1)}), bf16[128,32,128]{2,1,0:T(8,128)(2,1)S(1)}, u32[]{:S(2)}, u32[]{:S(2)}) async-start(bf16[128,32,128]{2,1,0:T(8,128)(2,1)} %bitcast.28), calls=%async_computation.3 | async-start | bytes 2097152 | tf_op jit(solution)/shard_map/all_to_all | solution.py:351
  41.5 48.6 %copy-start.45 = (s32[3,128]{1,0:T(4,128)S(1)}, s32[3,128]{1,0:T(4,128)}, u32[]{:S(2)}) copy-start(s32[3,128]{1,0:T(4,128)} %param.13) | copy-start | bytes 4612
  41.5 48.6 %copy-start.43 = (f32[3456]{0:T(1024)S(1)}, f32[3456]{0:T(1024)}, u32[]{:S(2)}) copy-start(f32[3456]{0:T(1024)} %param.21) | copy-start | bytes 41476
  41.5 48.6 %copy-start.44 = (bf16[3456]{0:T(1024)(128)(2,1)S(1)}, bf16[3456]{0:T(1024)(128)(2,1)}, u32[]{:S(2)}) copy-start(bf16[3456]{0:T(1024)(128)(2,1)} %param.22) | copy-start | bytes 20740
  60.8 24.0 %all-to-all-start.2 = ((bf16[128,32,128]{2,1,0:T(8,128)(2,1)}), bf16[128,32,128]{2,1,0:T(8,128)(2,1)S(1)}, u32[]{:S(2)}, u32[]{:S(2)}) async-start(bf16[128,32,128]{2,1,0:T(8,128)(2,1)} %bitcast.24), calls=%async_computation.2 | async-start | bytes 2097152 | tf_op jit(solution)/shard_map/all_to_all | solution.py:351
  84.8 84.4 %all-to-all-start.1 = ((bf16[128,32,128]{2,1,0:T(8,128)(2,1)}), bf16[128,32,128]{2,1,0:T(8,128)(2,1)S(1)}, u32[]{:S(2)}, u32[]{:S(2)}) async-start(bf16[128,32,128]{2,1,0:T(8,128)(2,1)} %bitcast.19), calls=%async_computation.1 | async-start | bytes 2097152 | tf_op jit(solution)/shard_map/all_to_all | solution.py:351
  92.0 25.3 %copy-start.12 = (s32[19968]{0:T(1024)}, s32[19968]{0:T(1024)S(1)}, u32[]{:S(2)}) copy-start(s32[19968]{0:T(1024)S(1)} %reshape.105.ids) | copy-start | bytes 239620
  92.1 2.2 copy-start.3
  94.3 25.4 %copy-start.42 = (bf16[3,128,128]{2,1,0:T(8,128)(2,1)S(1)}, bf16[3,128,128]{2,1,0:T(8,128)(2,1)}, u32[]{:S(2)}) copy-start(bf16[3,128,128]{2,1,0:T(8,128)(2,1)} %param.12) | copy-start | bytes 294916
  94.3 26.0 %copy-start.40 = (s32[3,1,128,32]{2,3,1,0:T(8,128)S(1)}, s32[3,1,128,32]{2,3,1,0:T(8,128)}, u32[]{:S(2)}) copy-start(s32[3,1,128,32]{2,3,1,0:T(8,128)} %param.16) | copy-start | bytes 147460
  94.3 26.0 %copy-start.41 = (s32[3,1,128,32]{2,3,1,0:T(8,128)S(1)}, s32[3,1,128,32]{2,3,1,0:T(8,128)}, u32[]{:S(2)}) copy-start(s32[3,1,128,32]{2,3,1,0:T(8,128)} %param.15) | copy-start | bytes 147460
  94.3 26.1 %copy-start.13 = (f32[1,3456]{1,0:T(1,128)S(1)}, f32[1,3456]{1,0:T(1,128)}, u32[]{:S(2)}) copy-start(f32[1,3456]{1,0:T(1,128)} %reshape.120.weight) | copy-start | bytes 41476
  117.4 2.3 copy-start
  139.4 1.2 copy-start.4
  140.6 1.0 copy-start.7
  141.6 0.9 copy-start.16
  142.5 0.9 copy-start.18
  144.7 24.5 %copy-start.14 = (f32[1,3456]{1,0:T(1,128)S(1)}, f32[1,3456]{1,0:T(1,128)}, u32[]{:S(2)}) copy-start(f32[1,3456]{1,0:T(1,128)} %reshape.120.weight) | copy-start | bytes 41476
  144.7 24.5 %copy-start.15 = (bf16[128,128]{1,0:T(8,128)(2,1)S(1)}, bf16[128,128]{1,0:T(8,128)(2,1)}, u32[]{:S(2)}) copy-start(bf16[128,128]{1,0:T(8,128)(2,1)} %get-tuple-element.59.bottom) | copy-start | bytes 98308
  163.8 1.3 copy-start.5
  165.1 1.0 copy-start.9
  166.1 0.9 copy-start.20
  167.0 1.0 copy-start.22
  188.4 1.2 copy-start.6
  189.6 1.0 copy-start.11
  190.6 0.9 copy-start.24
  191.5 0.9 copy-start.26
  229.1 5.4 %collective-permute-start.1 = (bf16[64,128,128]{2,1,0:T(8,128)(2,1)}, bf16[64,128,128]{2,1,0:T(8,128)(2,1)S(1)}, u32[]{:S(2)}, u32[]{:S(2)}) collective-permute-start(bf16[64,128,128]{2,1,0:T(8,128)(2,1)} %get-tuple-element.52), channel_id=1, source_target_pairs={{0,1},{1,0},{2,3},{3,2},{4,5},{5,4},{6,7},{7,6},{8,9},{9,8},{10,11... | collective-permute-start | bytes 6291464 | tf_op jit(solution)/shard_map/ppermute | solution.py:439
  234.5 13.9 %copy-start.17 = (bf16[128,3456]{1,0:T(8,128)(2,1)S(1)}, bf16[128,3456]{1,0:T(8,128)(2,1)}, u32[]{:S(2)}) copy-start(bf16[128,3456]{1,0:T(8,128)(2,1)} %copy-done.16) | copy-start | bytes 2654212
  234.5 13.9 %copy-start.19 = (bf16[128,3456]{1,0:T(8,128)(2,1)S(1)}, bf16[128,3456]{1,0:T(8,128)(2,1)}, u32[]{:S(2)}) copy-start(bf16[128,3456]{1,0:T(8,128)(2,1)} %copy-done.18) | copy-start | bytes 2654212
  234.5 14.0 %copy-start.29 = (bf16[128,512]{1,0:T(8,128)(2,1)S(1)}, bf16[128,512]{1,0:T(8,128)(2,1)}, u32[]{:S(2)}) copy-start(bf16[128,512]{1,0:T(8,128)(2,1)} %copy-done.28) | copy-start | bytes 393220
  234.5 14.0 %copy-start.31 = (bf16[128,512]{1,0:T(8,128)(2,1)S(1)}, bf16[128,512]{1,0:T(8,128)(2,1)}, u32[]{:S(2)}) copy-start(bf16[128,512]{1,0:T(8,128)(2,1)} %copy-done.30) | copy-start | bytes 393220
  238.4 37.4 %all-to-all-start.5 = ((bf16[64,128,128]{2,1,0:T(8,128)(2,1)}), bf16[64,128,128]{2,1,0:T(8,128)(2,1)}, u32[]{:S(2)}, u32[]{:S(2)}) async-start(bf16[64,128,128]{2,1,0:T(8,128)(2,1)} %add_convert_fusion.1), calls=%async_computation.5 | async-start | bytes 4194304 | tf_op jit(solution)/shard_map/all_to_all | solution.py:441
  248.4 248.5 %all-gather.2.cloned.1.call-start = ((), (), s32[]{:S(2)}) async-start(), calls=%async_computation.9 | async-start | bytes 4227072 | tf_op jit(solution)/shard_map/all_gather | solution.py:445
  248.5 1.2 copy-start.21
  249.6 1.2 copy-start.23
  250.8 1.2 copy-start.25
  252.0 1.2 copy-start.27
  254.0 0.9 copy-start.35
  255.0 0.9 copy-start.37
  255.9 0.9 copy-start.39
  256.8 21.6 %copy-start.8 = (bf16[4096,128]{1,0:T(8,128)(2,1)S(1)}, bf16[4096,128]{1,0:T(8,128)(2,1)}, u32[]{:S(2)}) copy-start(bf16[4096,128]{1,0:T(8,128)(2,1)} %copy-done.7) | copy-start | bytes 3145732
  267.9 36.8 %copy-start.10 = (bf16[4096,128]{1,0:T(8,128)(2,1)S(1)}, bf16[4096,128]{1,0:T(8,128)(2,1)}, u32[]{:S(2)}) copy-start(bf16[4096,128]{1,0:T(8,128)(2,1)} %copy-done.9) | copy-start | bytes 3145732
  267.9 65.8 %collective-permute-start = (bf16[64,32,1024]{2,1,0:T(8,128)(2,1)}, bf16[64,32,1024]{2,1,0:T(8,128)(2,1)}, u32[]{:S(2)}, u32[]{:S(2)}) collective-permute-start(bf16[64,32,1024]{2,1,0:T(8,128)(2,1)} %get-tuple-element.44), channel_id=1, source_target_pairs={{0,1},{1,0},{2,3},{3,2},{4,5},{5,4},{6,7},{7,6},{8,9},{9,8},{10,11... | collective-permute-start | bytes 12582920 | tf_op jit(solution)/shard_map/ppermute | solution.py:419
  329.1 27.7 %all-to-all-start.6 = ((bf16[128,32,128]{2,1,0:T(8,128)(2,1)}), bf16[128,32,128]{2,1,0:T(8,128)(2,1)S(1)}, u32[]{:S(2)}, u32[]{:S(2)}) async-start(bf16[128,32,128]{2,1,0:T(8,128)(2,1)} %bitcast.115), calls=%async_computation.6 | async-start | bytes 2097152 | tf_op jit(solution)/shard_map/all_to_all | solution.py:395
  356.8 136.4 %all-to-all-start.4 = ((bf16[64,32,1024]{2,1,0:T(8,128)(2,1)}), bf16[64,32,1024]{2,1,0:T(8,128)(2,1)}, u32[]{:S(2)}, u32[]{:S(2)}) async-start(bf16[64,32,1024]{2,1,0:T(8,128)(2,1)} %add_convert_fusion), calls=%async_computation.4 | async-start | bytes 8388608 | tf_op jit(solution)/shard_map/all_to_all | solution.py:421
  (7 other events, 4.9 us)
Sparse Core Ops, SparseCore 0:
  278.5 82.7 all-gather.1

commit v2 on v1

--- a/solution.py
+++ b/solution.py
@@ -14,43 +14,50 @@
 MIB = 1024 * 1024
 SMEM = pl.BlockSpec(memory_space=pltpu.SMEM)
 VMEM = pl.BlockSpec(memory_space=pltpu.VMEM)
+HBM = pl.BlockSpec(memory_space=pltpu.HBM)
 NT = (((1,), (1,)), ((), ()))
 TN = (((0,), (0,)), ((), ()))
 
 
-def local_call(kernel, outs, in_specs, scratch, name, limit, flops, bytes_accessed):
+def local_call(
+    kernel, outs, in_specs, scratch, name, limit, flops, bytes_accessed, out_specs=None, aliases={}
+):
     return pl.pallas_call(
         kernel,
         out_shape=[jax.ShapeDtypeStruct(s, d) for s, d in outs],
         in_specs=in_specs,
-        out_specs=[VMEM] * len(outs),
+        out_specs=out_specs or [VMEM] * len(outs),
         scratch_shapes=scratch,
         compiler_params=pltpu.CompilerParams(vmem_limit_bytes=limit * MIB),
         cost_estimate=pl.CostEstimate(
             flops=flops, bytes_accessed=bytes_accessed, transcendentals=0
         ),
+        input_output_aliases=aliases,
         name=name,
     )
 
 
-def freq_kernel(blocks, samples, ids, table_ref, out, table):
+def freq_kernel(blocks, samples, ids, table_ref, *refs):
+    *outs, table = refs
     table[...] = table_ref[...].astype(f32)
     unroll = 32
-
-    def group(g, carry):
-        def some(k, carry):
-            for u in range(unroll):
-                s = k * unroll + u
-                first = ids[g * 2 * samples + s]
-                second = ids[g * 2 * samples + samples + s]
-                out[pl.ds(g * samples + s, 1), :] = (
-                    table[pl.ds(first, 1), :] + table[pl.ds(second, 1), :]
-                )
-            return carry
-
-        return lax.fori_loop(0, samples // unroll, some, carry)
-
-    lax.fori_loop(0, blocks, group, 0)
+    for m, out in enumerate(outs):
+        start = m * blocks * 2 * samples
+
+        def group(g, carry):
+            def some(k, carry):
+                for u in range(unroll):
+                    s = k * unroll + u
+                    first = ids[start + g * 2 * samples + s]
+                    second = ids[start + g * 2 * samples + samples + s]
+                    out[pl.ds(g * samples + s, 1), :] = (
+                        table[pl.ds(first, 1), :] + table[pl.ds(second, 1), :]
+                    )
+                return carry
+
+            return lax.fori_loop(0, samples // unroll, some, carry)
+
+        lax.fori_loop(0, blocks, group, 0)
 
 
 def lookup_kernel(peers, stride, start, cap, asked, table_ref, out, table, rows):
@@ -71,7 +78,7 @@
     cap,
     features,
     slot_start,
-    freq_start,
+    ret_start,
     loss_mult,
     slots,
     out_b,
@@ -83,26 +90,35 @@
     cross_v,
     bias,
     weight,
-    returned,
-    d_pooled,
-    x_zero,
-    hidden_out,
-    d_hidden_out,
-    gate_low,
-    grad_bw,
-    arrived,
-    acc0,
-    acc1,
-    acc2,
-    acc3,
-    gate,
+    *refs,
 ):
+    (
+        returned_hbm,
+        d_pooled_hbm,
+        x_zero_hbm,
+        hidden_hbm,
+        d_hidden_hbm,
+        gate_low_hbm,
+        grad_bw,
+        arrived,
+        acc0,
+        acc1,
+        acc2,
+        acc3,
+        gate,
+        returned,
+        x_zero,
+        hidden_out,
+        d_hidden_out,
+        gate_low,
+        sems,
+    ) = refs[-19:]
     samples, width = x_zero.shape
     emb = bottom.shape[1]
     n_slots = features * samples
     accs = (acc0, acc1, acc2, acc3)
     arrived[...] = fetched[...].astype(f32)
-    acc0[pl.ds(0, n_slots), :] = freq_part[pl.ds(freq_start, n_slots), :]
+    acc0[pl.ds(0, n_slots), :] = freq_part[...]
     for a in accs[1:]:
         a[...] = jnp.zeros_like(a)
 
@@ -127,6 +143,12 @@
 
     hidden = jnp.dot(x_zero[...], cross_u[...], preferred_element_type=f32).astype(bf16)
     hidden_out[...] = hidden
+    copies = [
+        pltpu.make_async_copy(x_zero, x_zero_hbm, sems.at[0]),
+        pltpu.make_async_copy(hidden_out, hidden_hbm, sems.at[1]),
+    ]
+    for copy in copies:
+        copy.start()
     chunk = 3 * emb
     chunks = width // chunk
     partial = jnp.zeros((samples, emb), f32)
@@ -152,6 +174,12 @@
         gate_low[...], cross_v[...], NT, preferred_element_type=f32
     ).astype(bf16)
     d_hidden_out[...] = d_hidden
+    later = [
+        pltpu.make_async_copy(gate_low, gate_low_hbm, sems.at[2]),
+        pltpu.make_async_copy(d_hidden_out, d_hidden_hbm, sems.at[3]),
+    ]
+    for copy in later:
+        copy.start()
     for k in range(chunks):
         cols = slice(k * chunk, (k + 1) * chunk)
         back = lax.dot_general(d_hidden, cross_u[cols, :], NT, preferred_element_type=f32)
@@ -159,10 +187,10 @@
         for j in range(3):
             f = 3 * k + j - 1
             if f >= 0:
-                block = d_input[:, j * emb : (j + 1) * emb]
-                d_pooled[f * samples : (f + 1) * samples, :] = block
-                acc0[f * samples : (f + 1) * samples, :] = block
+                acc0[f * samples : (f + 1) * samples, :] = d_input[:, j * emb : (j + 1) * emb]
     acc0[n_slots:, :] = jnp.zeros((acc0.shape[0] - n_slots, emb), f32)
+    pooled_copy = pltpu.make_async_copy(acc0.at[pl.ds(0, n_slots), :], d_pooled_hbm, sems.at[4])
+    pooled_copy.start()
 
     def take_peer(o, carry):
         for c in range(cap):
@@ -171,10 +199,20 @@
         return carry
 
     lax.fori_loop(0, peers, take_peer, 0)
-    returned[...] = arrived[...].astype(bf16)
-
-
-def dense_grad_kernel(peers, per, core, x0, x1, x2, g0, g1, g2, h0, h1, h2, e0, e1, e2, keep, send, total):
+    returned[...] = arrived[...].astype(bf16).reshape(peers, cap, emb)
+    returned_copy = pltpu.make_async_copy(
+        returned, returned_hbm.at[:, pl.ds(ret_start, cap), :], sems.at[5]
+    )
+    returned_copy.start()
+    for copy in copies + later:
+        copy.wait()
+    pooled_copy.wait()
+    returned_copy.wait()
+
+
+def dense_grad_kernel(
+    peers, per, core, columns, x0, x1, x2, g0, g1, g2, h0, h1, h2, e0, e1, e2, keep, send, total
+):
     width = x0.shape[1]
     rank = h0.shape[1]
     chunk = 128
@@ -200,11 +238,20 @@
             window = total[pl.ds(pl.multiple_of(base + (i * per - skip), 8), rows + 8), :]
             return window[skip : skip + rows]
 
+        spare = lax.broadcasted_iota(jnp.int32, (16, 128), 0) >= per - 16
         for i in range(4):
             first = block(2 * i)
             second = block(2 * i + 1)
-            keep[q * 4 + i] = jnp.where(even, first, second).astype(bf16)
-            send[q * 4 + i] = jnp.where(even, second, first).astype(bf16)
+            at = q * 4 + i
+            for ref, value, row in (
+                (keep, jnp.where(even, first, second), 2 * at + core[0]),
+                (send, jnp.where(even, second, first), 2 * at + 1 - core[0]),
+            ):
+                ref[at, 0:16, :] = value[0:16].astype(bf16)
+                ref[at, 16:32, 128:] = value[16:32, 128:].astype(bf16)
+                ref[at, 16:32, 0:128] = jnp.where(
+                    spare, columns[row], value[16:32, 0:128]
+                ).astype(bf16)
         return carry
 
     lax.fori_loop(0, peers // 8, pairs, 0)
@@ -250,12 +297,17 @@
     lax.fori_loop(0, keep.shape[0], block, 0)
 
 
-def owner_kernel(peers, stride, cap, asked, r0, r1, r2, out, rows, acc0, acc1, acc2, acc3):
+def owner_kernel(peers, stride, cap, asked, alone, pair, out, rows, acc0, acc1, acc2, acc3):
     accs = (acc0, acc1, acc2, acc3)
     for a in accs:
         a[...] = jnp.zeros_like(a)
-    for m, source in enumerate((r0, r1, r2)):
-        rows[...] = source[...].astype(f32)
+    emb = out.shape[1]
+    for m in range(3):
+        if m == 0:
+            rows[...] = alone[...].astype(f32)
+        else:
+            part = pair[:, (m - 1) * cap : m * cap, :]
+            rows[...] = part.astype(f32).reshape(peers * cap, emb)
 
         def peer(d, carry):
             for c in range(0, cap, 4):
@@ -318,25 +370,33 @@
     stride = -(-micro * cap // 128) * 128
     line = jnp.pad(line, ((0, 0), (0, stride - micro * cap)), constant_values=owned)
     asked = lax.all_to_all(line, "dev", split_axis=0, concat_axis=0, tiled=True).reshape(-1)
-    asked_row = jnp.minimum(asked, owned - 1)
-
-    (freq_part,) = local_call(
-        functools.partial(freq_kernel, micro * features, samples),
-        [((micro * n_slots, emb), f32)],
+
+    freq_part = local_call(
+        functools.partial(freq_kernel, features, samples),
+        [((n_slots, emb), f32)] * micro,
         [SMEM, VMEM],
         [pltpu.VMEM((freq_rows, emb), f32)],
         "freq_rows",
-        40,
+        62,
         0,
         50 * MIB,
     )(ids, freq_table)
 
+    asked, freq_part = lax.optimization_barrier((asked, freq_part))
+    asked_row = jnp.minimum(asked, owned - 1)
     weight = out_w.astype(f32).reshape(1, width)
     bias = cross_bias.reshape(1, width)
     label_cols = labels.astype(f32).reshape(micro, samples, 1)
     bias_b = out_b.reshape(1)
+
+    def exchange(rows, count):
+        return lax.all_to_all(
+            rows.reshape(devices, count, emb), "dev", split_axis=0, concat_axis=0, tiled=True
+        ).reshape(n_req * count // cap, emb)
+
     outs = []
     arrived = []
+    looked_all = []
     for m in range(micro):
         (looked,) = local_call(
             functools.partial(lookup_kernel, devices, stride, m * cap, cap),
@@ -348,9 +408,23 @@
             0,
             20 * MIB,
         )(asked_row, inf_table)
-        fetched = lax.all_to_all(
-            looked.reshape(devices, cap, emb), "dev", split_axis=0, concat_axis=0, tiled=True
-        ).reshape(n_req, emb)
+        asked_row, looked = lax.optimization_barrier((asked_row, looked))
+        looked_all.append(looked)
+    looked_all[1], looked_all[2] = lax.optimization_barrier((looked_all[1], looked_all[2]))
+    fetched = exchange(looked_all[0], cap)
+    later = exchange(looked_all[1], cap)
+    pair = None
+    for m in range(micro):
+        if m > 0:
+            fetched = later
+        if m == 1:
+            looked_all[2], outs[0][6] = lax.optimization_barrier((looked_all[2], outs[0][6]))
+            later = exchange(looked_all[2], cap)
+            fetched, outs[0][6] = lax.optimization_barrier((fetched, outs[0][6]))
+        if m == 2:
+            fetched, outs[1][6] = lax.optimization_barrier((fetched, outs[1][6]))
+            back, outs[1][6] = lax.optimization_barrier((outs[0][0], outs[1][6]))
+            arrived.append(exchange(back, cap))
         out = local_call(
             functools.partial(
                 micro_kernel,
@@ -358,11 +432,11 @@
                 cap,
                 features,
                 m * n_req,
-                m * n_slots,
+                cap if m == 2 else 0,
                 loss_mult,
             ),
             [
-                ((n_req, emb), bf16),
+                ((devices, cap if m == 0 else 2 * cap, emb), bf16),
                 ((n_slots, emb), f32),
                 ((samples, width), bf16),
                 ((samples, rank), bf16),
@@ -370,93 +444,103 @@
                 ((samples, width), bf16),
                 ((2, width), f32),
             ],
-            [SMEM, SMEM] + [VMEM] * 8,
+            [SMEM, SMEM] + [VMEM] * 8 + ([HBM] if m == 2 else []),
             [pltpu.VMEM((n_req, emb), f32)]
             + [pltpu.VMEM((n_slots + 8, emb), f32)] * 4
-            + [pltpu.VMEM((samples, width), f32)],
+            + [pltpu.VMEM((samples, width), f32)]
+            + [pltpu.VMEM((devices, cap, emb), bf16), pltpu.VMEM((samples, width), bf16)]
+            + [pltpu.VMEM((samples, rank), bf16)] * 2
+            + [pltpu.VMEM((samples, width), bf16), pltpu.SemaphoreType.DMA((6,))],
             f"micro{m}",
-            48,
+            62,
             6 * samples * width * rank,
             60 * MIB,
+            [HBM] * 6 + [VMEM],
+            {10: 0} if m == 2 else {},
         )(
             place,
             bias_b,
             fetched,
-            freq_part,
+            freq_part[m],
             bottom[m],
             label_cols[m],
             cross_u,
             cross_v,
             bias,
             weight,
+            *([outs[1][0]] if m == 2 else []),
         )
-        outs.append(out)
-        arrived.append(
-            lax.all_to_all(
-                out[0].reshape(devices, cap, emb), "dev", split_axis=0, concat_axis=0, tiled=True
-            ).reshape(n_req, emb)
-        )
+        outs.append(list(out))
+    arrived.append(exchange(outs[2][0], 2 * cap))
     d_pooled = [o[1] for o in outs]
-    grad_bw = lax.psum((outs[0][6] + outs[1][6]) + outs[2][6], "dev")
+    grad_bw = ((outs[0][6] + outs[1][6]) + outs[2][6]).reshape(2, devices, per)
+    columns = jnp.pad(
+        jnp.transpose(grad_bw, (1, 0, 2)), ((0, 0), (per - 16, 30 - per), (0, 128 - per))
+    )
 
     rows_pad = -(-per // 16) * 16
-    keep, send = local_call(
-        functools.partial(dense_grad_kernel, devices, per),
-        [((devices // 2, rows_pad, 2 * rank), bf16)] * 2,
-        [SMEM] + [VMEM] * 12,
-        [pltpu.VMEM((width + 16, 2 * rank), f32)],
-        "dense_grads",
-        48,
-        12 * samples * width * rank,
-        40 * MIB,
-    )(
-        core,
-        *[o[2] for o in outs],
-        *[o[5] for o in outs],
-        *[o[3] for o in outs],
-        *[o[4] for o in outs],
-    )
-    got = lax.ppermute(send, "dev", other_core)
-    both = (keep.astype(f32) + got.astype(f32)).astype(bf16)
-    parts = lax.all_to_all(
-        both, "dev", split_axis=0, concat_axis=0, axis_index_groups=same_core, tiled=True
-    )
-    dense = jnp.sum(parts.astype(f32), axis=0)[:per]
-    grad_u = dense[:, :rank]
-    grad_v = dense[:, rank:].T
-
     per_freq = freq_rows // devices
-    keep, send = local_call(
+    d_pooled, arrived[0] = lax.optimization_barrier((d_pooled, arrived[0]))
+    keep_f, send_f = local_call(
         functools.partial(freq_grad_kernel, features),
         [((devices // 2, per_freq, emb), bf16)] * 2,
         [SMEM, SMEM] + [VMEM] * 3,
         [pltpu.VMEM((freq_rows, emb), f32)] * 4,
         "freq_grads",
-        56,
+        62,
         0,
         120 * MIB,
     )(core, ids, *d_pooled)
+    send_f, arrived[1] = lax.optimization_barrier((send_f, arrived[1]))
+    got = lax.ppermute(send_f, "dev", other_core)
+    both_f = (keep_f.astype(f32) + got.astype(f32)).astype(bf16)
+    core_d, columns, both_f = lax.optimization_barrier((core, columns, both_f))
+    parts_f = lax.all_to_all(
+        both_f, "dev", split_axis=0, concat_axis=0, axis_index_groups=same_core, tiled=True
+    )
+    keep, send = local_call(
+        functools.partial(dense_grad_kernel, devices, per),
+        [((devices // 2, rows_pad, 2 * rank), bf16)] * 2,
+        [SMEM] + [VMEM] * 13,
+        [pltpu.VMEM((width + 16, 2 * rank), f32)],
+        "dense_grads",
+        62,
+        12 * samples * width * rank,
+        40 * MIB,
+    )(
+        core_d,
+        columns,
+        *[o[2] for o in outs],
+        *[o[5] for o in outs],
+        *[o[3] for o in outs],
+        *[o[4] for o in outs],
+    )
     got = lax.ppermute(send, "dev", other_core)
     both = (keep.astype(f32) + got.astype(f32)).astype(bf16)
+    both, parts_f = lax.optimization_barrier((both, parts_f))
     parts = lax.all_to_all(
         both, "dev", split_axis=0, concat_axis=0, axis_index_groups=same_core, tiled=True
     )
-    mine = jnp.sum(parts.astype(f32), axis=0).astype(bf16)
+    dense = jnp.sum(parts.astype(f32), axis=0)
+    grad_u = dense[:per, :rank]
+    grad_v = dense[:per, rank:].T
+    grad_b = dense[per, :per]
+    grad_w = dense[per + 1, :per]
+
+    mine = jnp.sum(parts_f.astype(f32), axis=0).astype(bf16)
     grad_freq = lax.all_gather(mine, "dev", tiled=True)
 
     (grad_inf,) = local_call(
         functools.partial(owner_kernel, devices, stride, cap),
         [((owned, emb), bf16)],
-        [SMEM] + [VMEM] * 3,
+        [SMEM] + [VMEM] * 2,
         [pltpu.VMEM((n_req, emb), f32)] + [pltpu.VMEM((owned + 8, emb), f32)] * 4,
         "owner_grads",
         32,
         0,
         60 * MIB,
-    )(asked, *arrived)
-
-    grad_b = lax.dynamic_slice_in_dim(grad_bw[0], me * per, per)
-    grad_w = lax.dynamic_slice_in_dim(grad_bw[1], me * per, per)
+    )(asked, arrived[0], arrived[1].reshape(devices, 2 * cap, emb))
+
     return (grad_u, grad_v, grad_b, grad_w, grad_freq, grad_inf)
 
 

time: 509 us -> 403 us (0.79)
  blocking collectives: 180 us -> 0 us
  waiting for transfers between devices: 51.7 us -> 102 us
  starting transfers between devices: 36.2 us -> 75.7 us
  local copies, waits for them, and re-layouts: 37.8 us -> 12.7 us
  Pallas kernels: 168 us -> 177 us
    psum x1 -> x0, blocking collectives: 109 us -> none  [on_device(): grad_bw = lax.psum(outs[0][6] + outs[1][6] + outs[2][6], 'dev')]
    all_to_all x3 -> x0, blocking collectives: 71.4 us -> none  [the longest x2 50.7 us: on_device(): lax.all_to_all(out[0].reshape(devices, cap, emb), 'dev', split_axis=0, co...]
    all_to_all x4 -> x7, starting transfers between devices: 18.5 us -> 66.7 us  [the longest x5 45.2 us: exchange(): lax.all_to_all(rows.reshape(devices, count, emb), 'dev', split_axis=0, co...]
    all_gather x1, waiting for transfers between devices: 0.01 us -> 45.2 us  [on_device(): grad_freq = lax.all_gather(mine, 'dev', tiled=True)]
    unnamed x93 -> x23, local copies, waits for them, and re-layouts: 33.9 us -> 3.79 us
    all_to_all x2 -> x1, waiting for transfers between devices: 7.3 us -> 28.6 us  [on_device(): lax.all_to_all(both, 'dev', split_axis=0, concat_axis=0, axis_index_group...]
    all_to_all x4 -> x7, waiting for transfers between devices: 40.3 us -> 25.2 us  [the longest x1 19.7 us: on_device(): lax.all_to_all(both_f, 'dev', split_axis=0, concat_axis=0, axis_index_gro...]
    all_to_all x2 -> x1, starting transfers between devices: 15.6 us -> 7.46 us  [on_device(): lax.all_to_all(both, 'dev', split_axis=0, concat_axis=0, axis_index_group...]
  transfers between devices with their start and end apart: 9 -> 11, of which waited for: 5 -> 5; matrix products, arithmetic and copies ran while one was open for 3% -> 5% of each run, Pallas kernels for 21% -> 39%
where the time goes in v2:
time: 403 us; the launch traced here: 402 us
  Pallas kernels  177 us (44%)
  waiting for transfers between devices  102 us (25%)
  starting transfers between devices  75.7 us (19%)
  other arithmetic  19.9 us (5%)
  between operations  15 us (4%)
  local copies, waits for them, and re-layouts  12.7 us (3%)
    pallas_call x3, Pallas kernels, on_device(): local_call(functools.partial(micro_kernel, devices, cap, features, m * n_...  60.1 us
    all_gather x1, waiting for transfers between devices, on_device(): grad_freq = lax.all_gather(mine, 'dev', tiled=True)  45.2 us
    all_to_all x5, starting transfers between devices, exchange(): lax.all_to_all(rows.reshape(devices, count, emb), 'dev', split_axis=0, co...  45.2 us
    pallas_call x1, Pallas kernels, on_device(): local_call(functools.partial(freq_grad_kernel, features), [((devices // 2...  35.3 us
    all_to_all x1, waiting for transfers between devices, on_device(): lax.all_to_all(both, 'dev', split_axis=0, concat_axis=0, axis_index_group...  28.6 us
    pallas_call x1, Pallas kernels, on_device(): local_call(functools.partial(freq_kernel, features, samples), [((n_slots,...  25.8 us
    pallas_call x1, Pallas kernels, on_device(): local_call(functools.partial(owner_kernel, devices, stride, cap), [((owne...  21.3 us
    pallas_call x3, Pallas kernels, on_device(): local_call(functools.partial(lookup_kernel, devices, stride, m * cap, cap...  20.2 us
  transfers between devices with their start and end apart: 11, of which 5 were waited for; matrix products, arithmetic and copies ran while one was open for 5% of the time, Pallas kernels for 39%

profile of v2, /device:TPU:1, one launch (start us, length us, event | category | flops | bytes accessed | tf_op | source)
XLA Modules:
  0.0 402.0 jit_solution(3555607544070484006)
XLA Ops:
  7.2 0.9 bitcast_select_fusion
  8.1 0.7 copy.53
  8.8 11.5 %all-to-all-start = ((s32[128,1,128]{2,1,0:T(1,128)}), s32[128,1,128]{2,1,0:T(1,128)S(1)}, u32[]{:S(2)}, u32[]{:S(2)}) async-start(s32[128,1,128]{2,1,0:T(1,128)} %copy.53), calls=%async_computation | async-start | bytes 131072 | tf_op jit(solution)/shard_map/all_to_all | solution.py:372
  20.3 1.6 reshape.93.ids
  21.9 25.8 %freq_rows.1 = (f32[3328,128]{1,0:T(8,128)}, f32[3328,128]{1,0:T(8,128)}, f32[3328,128]{1,0:T(8,128)}) custom-call(s32[19968]{0:T(1024)} %reshape.93.ids, bf16[16384,128]{1,0:T(8,128)(2,1)} %table_ref.4), custom_call_target="tpu_custom_call" | custom-call | bytes 52428800 | tf_op jit(solution)/shard_map/freq_rows/pallas_call | solution.py:374
  47.7 6.8 %lookup0.1 = bf16[4096,128]{1,0:T(8,128)(2,1)} custom-call(s32[16384]{0:T(1024)S(1)} %broadcast_minimum_fusion.asked, bf16[4096,128]{1,0:T(8,128)(2,1)S(1)} %copy-done), custom_call_target="tpu_custom_call" | custom-call | bytes 20971520 | tf_op jit(solution)/shard_map/lookup0/pallas_call | solution.py:401
  54.5 0.0 copy-start.3
  54.5 10.2 %all-to-all-start.2 = ((bf16[128,32,128]{2,1,0:T(8,128)(2,1)}), bf16[128,32,128]{2,1,0:T(8,128)(2,1)}, u32[]{:S(2)}, u32[]{:S(2)}) async-start(bf16[128,32,128]{2,1,0:T(8,128)(2,1)} %bitcast.22), calls=%async_computation.2 | async-start | bytes 2097152 | tf_op jit(solution)/shard_map/all_to_all | solution.py:393
  64.7 6.7 %lookup1.1 = bf16[4096,128]{1,0:T(8,128)(2,1)} custom-call(s32[16384]{0:T(1024)S(1)} %broadcast_minimum_fusion.asked, bf16[4096,128]{1,0:T(8,128)(2,1)S(1)} %copy-done), custom_call_target="tpu_custom_call" | custom-call | bytes 20971520 | tf_op jit(solution)/shard_map/lookup1/pallas_call | solution.py:401
  71.5 6.7 %lookup2.1 = bf16[4096,128]{1,0:T(8,128)(2,1)} custom-call(s32[16384]{0:T(1024)S(1)} %broadcast_minimum_fusion.asked, bf16[4096,128]{1,0:T(8,128)(2,1)S(1)} %copy-done), custom_call_target="tpu_custom_call" | custom-call | bytes 20971520 | tf_op jit(solution)/shard_map/lookup2/pallas_call | solution.py:401
  78.2 5.5 %all-to-all-done.2 = bf16[128,32,128]{2,1,0:T(8,128)(2,1)} async-done(((bf16[128,32,128]{2,1,0:T(8,128)(2,1)}), bf16[128,32,128]{2,1,0:T(8,128)(2,1)}, u32[]{:S(2)}, u32[]{:S(2)}) %all-to-all-start.2) | async-done | bytes 1048608 | tf_op jit(solution)/shard_map/all_to_all | solution.py:393
  83.7 4.6 %all-to-all-start.1 = ((bf16[128,32,128]{2,1,0:T(8,128)(2,1)}), bf16[128,32,128]{2,1,0:T(8,128)(2,1)S(1)}, u32[]{:S(2)}, u32[]{:S(2)}) async-start(bf16[128,32,128]{2,1,0:T(8,128)(2,1)} %bitcast.9), calls=%async_computation.1 | async-start | bytes 2097152 | tf_op jit(solution)/shard_map/all_to_all | solution.py:393
  88.3 0.7 copy.57.labels
  89.0 0.6 reshape.100.bias
  89.6 0.6 reshape.110.weight
  90.9 0.6 slice_bitcast_fusion.1
  91.6 0.7 fusion.2
  92.3 20.0 %micro0.1 = (bf16[128,32,128]{2,1,0:T(8,128)(2,1)}, f32[3328,128]{1,0:T(8,128)}, bf16[128,3456]{1,0:T(8,128)(2,1)}, bf16[128,512]{1,0:T(8,128)(2,1)}, bf16[128,5...) custom-call(s32[12288]{0:T(1024)} %bitcast.111, f32[1]{0:T(128)} %bitcast.104.out_b, ...), custom_call_target="tpu_custom_call" | custom-call | flops 1358954496 | bytes 62914560 | tf_op jit(solution)/shard_map/micro0/pallas_call | solution.py:428
  112.3 10.4 %all-to-all-start.3 = ((bf16[128,32,128]{2,1,0:T(8,128)(2,1)}), bf16[128,32,128]{2,1,0:T(8,128)(2,1)}, u32[]{:S(2)}, u32[]{:S(2)}) async-start(bf16[128,32,128]{2,1,0:T(8,128)(2,1)} %bitcast.26), calls=%async_computation.3 | async-start | bytes 2097152 | tf_op jit(solution)/shard_map/all_to_all | solution.py:393
  122.7 0.7 copy.58.labels
  123.4 20.0 %micro1.1 = (bf16[128,64,128]{2,1,0:T(8,128)(2,1)}, f32[3328,128]{1,0:T(8,128)}, bf16[128,3456]{1,0:T(8,128)(2,1)}, bf16[128,512]{1,0:T(8,128)(2,1)}, bf16[128,5...) custom-call(s32[12288]{0:T(1024)} %bitcast.112, f32[1]{0:T(128)} %bitcast.105.out_b, ...), custom_call_target="tpu_custom_call" | custom-call | flops 1358954496 | bytes 62914560 | tf_op jit(solution)/shard_map/micro1/pallas_call | solution.py:428
  143.5 9.8 %all-to-all-start.4 = ((bf16[128,32,128]{2,1,0:T(8,128)(2,1)}), bf16[128,32,128]{2,1,0:T(8,128)(2,1)S(1)}, u32[]{:S(2)}, u32[]{:S(2)}) async-start(bf16[128,32,128]{2,1,0:T(8,128)(2,1)} %get-tuple-element.93), calls=%async_computation.4 | async-start | bytes 2097152 | tf_op jit(solution)/shard_map/all_to_all | solution.py:393
  153.3 0.7 copy.59.labels
  154.0 20.0 %micro2.1 = (bf16[128,64,128]{2,1,0:T(8,128)(2,1)}, f32[3328,128]{1,0:T(8,128)}, bf16[128,3456]{1,0:T(8,128)(2,1)}, bf16[128,512]{1,0:T(8,128)(2,1)}, bf16[128,5...) custom-call(s32[12288]{0:T(1024)} %bitcast.113, ...), custom_call_target="tpu_custom_call", output_to_operand_aliasing={{0}: (10, {})} | custom-call | flops 1358954496 | bytes 62914560 | tf_op jit(solution)/shard_map/micro2/pallas_call | solution.py:428
  174.1 10.2 %all-to-all-start.5 = ((bf16[128,64,128]{2,1,0:T(8,128)(2,1)}), bf16[128,64,128]{2,1,0:T(8,128)(2,1)}, u32[]{:S(2)}, u32[]{:S(2)}) async-start(bf16[128,64,128]{2,1,0:T(8,128)(2,1)} %get-tuple-element.99), calls=%async_computation.5 | async-start | bytes 4194304 | tf_op jit(solution)/shard_map/all_to_all | solution.py:393
  184.4 35.3 %freq_grads.1 = (bf16[64,128,128]{2,1,0:T(8,128)(2,1)}, bf16[64,128,128]{2,1,0:T(8,128)(2,1)}) custom-call(s32[1]{0:T(128)} %bitcast.core, s32[19968]{0:T(1024)} %reshape.93.ids, f32[3328,128]{1,0:T(8,128)} %get-tuple-element.94.d0, f32[3328,128]{1,0:T(8,128)} %get-tuple-element.95.d1, f32[3328,128]{1,0:T(8,128)} %get-tuple-element.96.d2), custom_call_target="tpu_custom_call" | custom-call | bytes 125829120 | tf_op jit(solution)/shard_map/freq_grads/pallas_call | solution.py:484
  219.6 1.1 collective-permute-start
  220.8 0.2 reshape.105
  221.0 0.1 copy.64
  221.1 1.1 pad.9.columns
  222.2 2.7 collective-permute-done
  224.9 4.7 %add_convert_fusion.1 = bf16[64,128,128]{2,1,0:T(8,128)(2,1)} fusion(bf16[64,128,128]{2,1,0:T(8,128)(2,1)} %collective-permute-done, bf16[64,128,128]{2,1,0:T(8,128)(2,1)} %get-tuple-element.97), kind=kLoop, calls=%fused_computation.2 | loop fusion | flops 4194304 | bytes 6291456 | tf_op jit(solution)/shard_map/convert_element_type | solution.py:496
  229.6 14.4 %dense_grads.1 = (bf16[64,32,1024]{2,1,0:T(8,128)(2,1)}, bf16[64,32,1024]{2,1,0:T(8,128)(2,1)}) custom-call(s32[1]{0:T(128)} %bitcast.core, f32[128,16,128]{2,1,0:T(8,128)} %pad.9.columns, bf16[128,3456]{1,0:T(8,128)(2,1)} %get-tuple-element.103.x0, bf16[128,3456]{1,0:T(8,128)(2,1)} %get-tuple-element.104.x1, bf16[128,3456]{1,0:T(8,128)(2,1)} %get-tuple-element.105.x2, ...), custom_call_target="tpu_custom_call" | custom-call | flops 2717908992 | bytes 41943040 | tf_op jit(solution)/shard_map/dense_grads/pallas_call | solution.py:501
  244.0 0.3 collective-permute-start.1
  244.3 10.0 %all-to-all-start.6 = ((bf16[64,128,128]{2,1,0:T(8,128)(2,1)}), bf16[64,128,128]{2,1,0:T(8,128)(2,1)}, u32[]{:S(2)}, u32[]{:S(2)}) async-start(bf16[64,128,128]{2,1,0:T(8,128)(2,1)} %add_convert_fusion.1), calls=%async_computation.6 | async-start | bytes 4194304 | tf_op jit(solution)/shard_map/all_to_all | solution.py:498
  254.3 0.0 all-gather.2.cloned.1.call-start
  254.4 8.0 %add_convert_fusion = bf16[64,32,1024]{2,1,0:T(8,128)(2,1)} fusion(bf16[64,32,1024]{2,1,0:T(8,128)(2,1)} %collective-permute-done.1, bf16[64,32,1024]{2,1,0:T(8,128)(2,1)} %get-tuple-element.115), kind=kLoop, calls=%fused_computation.1 | loop fusion | flops 8388608 | bytes 12582912 | tf_op jit(solution)/shard_map/convert_element_type | solution.py:519
  262.4 19.7 %all-to-all-done.6 = bf16[64,128,128]{2,1,0:T(8,128)(2,1)} async-done(((bf16[64,128,128]{2,1,0:T(8,128)(2,1)}), bf16[64,128,128]{2,1,0:T(8,128)(2,1)}, u32[]{:S(2)}, u32[]{:S(2)}) %all-to-all-start.6) | async-done | bytes 2097184 | tf_op jit(solution)/shard_map/all_to_all | solution.py:498
  282.1 2.5 reduce_sum.22
  284.6 0.0 all-gather.2.cloned.1.call-update
  284.6 7.5 %all-to-all-start.7 = ((bf16[64,32,1024]{2,1,0:T(8,128)(2,1)}), bf16[64,32,1024]{2,1,0:T(8,128)(2,1)}, u32[]{:S(2)}, u32[]{:S(2)}) async-start(bf16[64,32,1024]{2,1,0:T(8,128)(2,1)} %add_convert_fusion), calls=%async_computation.7 | async-start | bytes 8388608 | tf_op jit(solution)/shard_map/all_to_all | solution.py:521
  292.1 21.3 %owner_grads.1 = bf16[4096,128]{1,0:T(8,128)(2,1)} custom-call(s32[16384]{0:T(1024)S(1)} %bitcast.109, bf16[4096,128]{1,0:T(8,128)(2,1)S(1)} %bitcast.107, bf16[128,64,128]{2,1,0:T(8,128)(2,1)} %bitcast.38.pair), custom_call_target="tpu_custom_call" | custom-call | bytes 62914560 | tf_op jit(solution)/shard_map/owner_grads/pallas_call | solution.py:533
  313.4 28.6 %all-to-all-done.7 = bf16[64,32,1024]{2,1,0:T(8,128)(2,1)} async-done(((bf16[64,32,1024]{2,1,0:T(8,128)(2,1)}), bf16[64,32,1024]{2,1,0:T(8,128)(2,1)}, u32[]{:S(2)}, u32[]{:S(2)}) %all-to-all-start.7) | async-done | bytes 4194336 | tf_op jit(solution)/shard_map/all_to_all | solution.py:521
  342.0 3.0 convert_reduce_fusion
  345.1 0.5 slice_bitcast_fusion.4
  345.6 0.7 slice_bitcast_fusion
  346.2 45.2 %all-gather.2.cloned.1.call-done = bf16[16384,128]{1,0:T(8,128)(2,1)} async-done(((bf16[128,128]{1,0:T(8,128)(2,1)}), bf16[16384,128]{1,0:T(8,128)(2,1)}) %all-gather.2.cloned.1.call-update) | async-done | bytes 4194320 | tf_op jit(solution)/shard_map/all_gather | solution.py:531
  391.5 3.7 copy.68
  (32 shorter events, 0.1 us)
Async XLA Ops:
  7.2 40.5 %copy-start = (bf16[4096,128]{1,0:T(8,128)(2,1)S(1)}, bf16[4096,128]{1,0:T(8,128)(2,1)}, u32[]{:S(2)}) copy-start(bf16[4096,128]{1,0:T(8,128)(2,1)} %table_ref.7) | copy-start | bytes 3145732
  8.8 38.8 %all-to-all-start = ((s32[128,1,128]{2,1,0:T(1,128)}), s32[128,1,128]{2,1,0:T(1,128)S(1)}, u32[]{:S(2)}, u32[]{:S(2)}) async-start(s32[128,1,128]{2,1,0:T(1,128)} %copy.53), calls=%async_computation | async-start | bytes 131072 | tf_op jit(solution)/shard_map/all_to_all | solution.py:372
  54.5 33.8 %copy-start.10 = (s32[3,128]{1,0:T(4,128)S(1)}, s32[3,128]{1,0:T(4,128)}, u32[]{:S(2)}) copy-start(s32[3,128]{1,0:T(4,128)} %param.13) | copy-start | bytes 4612
  54.5 34.6 %copy-start.8 = (f32[3456]{0:T(1024)S(1)}, f32[3456]{0:T(1024)}, u32[]{:S(2)}) copy-start(f32[3456]{0:T(1024)} %param.21) | copy-start | bytes 41476
  54.5 35.2 %copy-start.9 = (bf16[3456]{0:T(1024)(128)(2,1)S(1)}, bf16[3456]{0:T(1024)(128)(2,1)}, u32[]{:S(2)}) copy-start(bf16[3456]{0:T(1024)(128)(2,1)} %param.22) | copy-start | bytes 20740
  54.5 36.4 %copy-start.4 = (bf16[3,128,128]{2,1,0:T(8,128)(2,1)S(1)}, bf16[3,128,128]{2,1,0:T(8,128)(2,1)}, u32[]{:S(2)}) copy-start(bf16[3,128,128]{2,1,0:T(8,128)(2,1)} %param.12) | copy-start | bytes 294916
  54.5 37.1 %copy-start.2 = (s32[3,1,128,32]{2,3,1,0:T(8,128)S(1)}, s32[3,1,128,32]{2,3,1,0:T(8,128)}, u32[]{:S(2)}) copy-start(s32[3,1,128,32]{2,3,1,0:T(8,128)} %param.16) | copy-start | bytes 147460
  54.5 37.1 %copy-start.3 = (s32[3,1,128,32]{2,3,1,0:T(8,128)S(1)}, s32[3,1,128,32]{2,3,1,0:T(8,128)}, u32[]{:S(2)}) copy-start(s32[3,1,128,32]{2,3,1,0:T(8,128)} %param.15) | copy-start | bytes 147460
  54.5 29.2 %all-to-all-start.2 = ((bf16[128,32,128]{2,1,0:T(8,128)(2,1)}), bf16[128,32,128]{2,1,0:T(8,128)(2,1)}, u32[]{:S(2)}, u32[]{:S(2)}) async-start(bf16[128,32,128]{2,1,0:T(8,128)(2,1)} %bitcast.22), calls=%async_computation.2 | async-start | bytes 2097152 | tf_op jit(solution)/shard_map/all_to_all | solution.py:393
  83.7 28.6 %all-to-all-start.1 = ((bf16[128,32,128]{2,1,0:T(8,128)(2,1)}), bf16[128,32,128]{2,1,0:T(8,128)(2,1)S(1)}, u32[]{:S(2)}, u32[]{:S(2)}) async-start(bf16[128,32,128]{2,1,0:T(8,128)(2,1)} %bitcast.9), calls=%async_computation.1 | async-start | bytes 2097152 | tf_op jit(solution)/shard_map/all_to_all | solution.py:393
  112.3 11.1 %copy-start.1 = (bf16[128,32,128]{2,1,0:T(8,128)(2,1)}, bf16[128,32,128]{2,1,0:T(8,128)(2,1)S(1)}, u32[]{:S(2)}) copy-start(bf16[128,32,128]{2,1,0:T(8,128)(2,1)S(1)} %all-to-all-done.1) | copy-start | bytes 3145732
  112.3 31.2 %all-to-all-start.3 = ((bf16[128,32,128]{2,1,0:T(8,128)(2,1)}), bf16[128,32,128]{2,1,0:T(8,128)(2,1)}, u32[]{:S(2)}, u32[]{:S(2)}) async-start(bf16[128,32,128]{2,1,0:T(8,128)(2,1)} %bitcast.26), calls=%async_computation.3 | async-start | bytes 2097152 | tf_op jit(solution)/shard_map/all_to_all | solution.py:393
  143.5 30.6 %all-to-all-start.4 = ((bf16[128,32,128]{2,1,0:T(8,128)(2,1)}), bf16[128,32,128]{2,1,0:T(8,128)(2,1)S(1)}, u32[]{:S(2)}, u32[]{:S(2)}) async-start(bf16[128,32,128]{2,1,0:T(8,128)(2,1)} %get-tuple-element.93), calls=%async_computation.4 | async-start | bytes 2097152 | tf_op jit(solution)/shard_map/all_to_all | solution.py:393
  174.1 46.7 %copy-start.5 = (f32[2,3456]{1,0:T(2,128)S(1)}, f32[2,3456]{1,0:T(2,128)}, u32[]{:S(2)}) copy-start(f32[2,3456]{1,0:T(2,128)} %get-tuple-element.78) | copy-start | bytes 82948
  174.1 46.7 %copy-start.6 = (f32[2,3456]{1,0:T(2,128)S(1)}, f32[2,3456]{1,0:T(2,128)}, u32[]{:S(2)}) copy-start(f32[2,3456]{1,0:T(2,128)} %get-tuple-element.85) | copy-start | bytes 82948
  174.1 46.7 %copy-start.7 = (f32[2,3456]{1,0:T(2,128)S(1)}, f32[2,3456]{1,0:T(2,128)}, u32[]{:S(2)}) copy-start(f32[2,3456]{1,0:T(2,128)} %get-tuple-element.89) | copy-start | bytes 82948
  174.1 45.5 %all-to-all-start.5 = ((bf16[128,64,128]{2,1,0:T(8,128)(2,1)}), bf16[128,64,128]{2,1,0:T(8,128)(2,1)}, u32[]{:S(2)}, u32[]{:S(2)}) async-start(bf16[128,64,128]{2,1,0:T(8,128)(2,1)} %get-tuple-element.99), calls=%async_computation.5 | async-start | bytes 4194304 | tf_op jit(solution)/shard_map/all_to_all | solution.py:393
  219.6 5.3 %collective-permute-start = (bf16[64,128,128]{2,1,0:T(8,128)(2,1)}, bf16[64,128,128]{2,1,0:T(8,128)(2,1)}, u32[]{:S(2)}, u32[]{:S(2)}) collective-permute-start(bf16[64,128,128]{2,1,0:T(8,128)(2,1)} %get-tuple-element.100), channel_id=1, source_target_pairs={{0,1},{1,0},{2,3},{3,2},{4,5},{5,4},{6,7},{7,6},{8,9},{9,8},{10,11... | collective-permute-start | bytes 6291464 | tf_op jit(solution)/shard_map/ppermute | solution.py:495
  244.0 10.4 %collective-permute-start.1 = (bf16[64,32,1024]{2,1,0:T(8,128)(2,1)}, bf16[64,32,1024]{2,1,0:T(8,128)(2,1)}, u32[]{:S(2)}, u32[]{:S(2)}) collective-permute-start(bf16[64,32,1024]{2,1,0:T(8,128)(2,1)} %get-tuple-element.116), channel_id=1, source_target_pairs={{0,1},{1,0},{2,3},{3,2},{4,5},{5,4},{6,7},{7,6},{8,9},{9,8},{10,11... | collective-permute-start | bytes 12582920 | tf_op jit(solution)/shard_map/ppermute | solution.py:518
  244.3 37.8 %all-to-all-start.6 = ((bf16[64,128,128]{2,1,0:T(8,128)(2,1)}), bf16[64,128,128]{2,1,0:T(8,128)(2,1)}, u32[]{:S(2)}, u32[]{:S(2)}) async-start(bf16[64,128,128]{2,1,0:T(8,128)(2,1)} %add_convert_fusion.1), calls=%async_computation.6 | async-start | bytes 4194304 | tf_op jit(solution)/shard_map/all_to_all | solution.py:498
  254.3 137.1 %all-gather.2.cloned.1.call-start = ((), (), s32[]{:S(2)}) async-start(), calls=%async_computation.8 | async-start | bytes 4227072 | tf_op jit(solution)/shard_map/all_gather | solution.py:531
  284.6 57.4 %all-to-all-start.7 = ((bf16[64,32,1024]{2,1,0:T(8,128)(2,1)}), bf16[64,32,1024]{2,1,0:T(8,128)(2,1)}, u32[]{:S(2)}, u32[]{:S(2)}) async-start(bf16[64,32,1024]{2,1,0:T(8,128)(2,1)} %add_convert_fusion), calls=%async_computation.7 | async-start | bytes 8388608 | tf_op jit(solution)/shard_map/all_to_all | solution.py:521
Sparse Core Ops, SparseCore 0:
  284.8 106.6 all-gather.1

commit v3 on v2

--- a/solution.py
+++ b/solution.py
@@ -37,12 +37,12 @@
     )
 
 
-def freq_kernel(blocks, samples, ids, table_ref, *refs):
+def freq_kernel(blocks, samples, first_micro, ids, table_ref, *refs):
     *outs, table = refs
     table[...] = table_ref[...].astype(f32)
     unroll = 32
     for m, out in enumerate(outs):
-        start = m * blocks * 2 * samples
+        start = (first_micro + m) * blocks * 2 * samples
 
         def group(g, carry):
             def some(k, carry):
@@ -78,16 +78,17 @@
     cap,
     features,
     slot_start,
+    fetch_start,
     ret_start,
     loss_mult,
     slots,
     out_b,
-    fetched,
-    freq_part,
+    fetched_hbm,
+    freq_part_hbm,
     bottom,
     labels,
-    cross_u,
-    cross_v,
+    cross_u_hbm,
+    cross_v_hbm,
     bias,
     weight,
     *refs,
@@ -111,16 +112,30 @@
         hidden_out,
         d_hidden_out,
         gate_low,
+        cross_u,
+        cross_v,
         sems,
-    ) = refs[-19:]
+    ) = refs[-21:]
     samples, width = x_zero.shape
     emb = bottom.shape[1]
     n_slots = features * samples
     accs = (acc0, acc1, acc2, acc3)
-    arrived[...] = fetched[...].astype(f32)
-    acc0[pl.ds(0, n_slots), :] = freq_part[...]
+    loads = [
+        pltpu.make_async_copy(
+            fetched_hbm.at[:, pl.ds(fetch_start, cap), :], returned, sems.at[6]
+        ),
+        pltpu.make_async_copy(freq_part_hbm, acc0.at[pl.ds(0, n_slots), :], sems.at[7]),
+        pltpu.make_async_copy(cross_u_hbm, cross_u, sems.at[8]),
+        pltpu.make_async_copy(cross_v_hbm, cross_v, sems.at[9]),
+    ]
+    for load in loads:
+        load.start()
     for a in accs[1:]:
         a[...] = jnp.zeros_like(a)
+    acc0[n_slots:, :] = jnp.zeros((acc0.shape[0] - n_slots, emb), f32)
+    loads[0].wait()
+    arrived[...] = returned[...].astype(f32).reshape(peers * cap, emb)
+    loads[1].wait()
 
     def add_peer(o, carry):
         for c in range(0, cap, 4):
@@ -141,6 +156,8 @@
         total = (acc0[rows, :] + acc1[rows, :]) + (acc2[rows, :] + acc3[rows, :])
         x_zero[:, (f + 1) * emb : (f + 2) * emb] = total.astype(bf16)
 
+    loads[2].wait()
+    loads[3].wait()
     hidden = jnp.dot(x_zero[...], cross_u[...], preferred_element_type=f32).astype(bf16)
     hidden_out[...] = hidden
     copies = [
@@ -211,7 +228,7 @@
 
 
 def dense_grad_kernel(
-    peers, per, core, columns, x0, x1, x2, g0, g1, g2, h0, h1, h2, e0, e1, e2, keep, send, total
+    peers, per, columns, x0, x1, x2, g0, g1, g2, h0, h1, h2, e0, e1, e2, parts, total
 ):
     width = x0.shape[1]
     rank = h0.shape[1]
@@ -227,34 +244,24 @@
             g_all, h_all, TN, preferred_element_type=f32
         )
     total[width:, :] = jnp.zeros((total.shape[0] - width, 2 * rank), f32)
-    rows = keep.shape[1]
-    even = core[0] == 0
-
-    def pairs(q, carry):
+    rows = parts.shape[1]
+    spare = lax.broadcasted_iota(jnp.int32, (16, 128), 0) >= per - 16
+
+    def blocks(q, carry):
         base = q * 8 * per
-
-        def block(i):
+        for i in range(8):
             skip = i * per % 8
             window = total[pl.ds(pl.multiple_of(base + (i * per - skip), 8), rows + 8), :]
-            return window[skip : skip + rows]
-
-        spare = lax.broadcasted_iota(jnp.int32, (16, 128), 0) >= per - 16
-        for i in range(4):
-            first = block(2 * i)
-            second = block(2 * i + 1)
-            at = q * 4 + i
-            for ref, value, row in (
-                (keep, jnp.where(even, first, second), 2 * at + core[0]),
-                (send, jnp.where(even, second, first), 2 * at + 1 - core[0]),
-            ):
-                ref[at, 0:16, :] = value[0:16].astype(bf16)
-                ref[at, 16:32, 128:] = value[16:32, 128:].astype(bf16)
-                ref[at, 16:32, 0:128] = jnp.where(
-                    spare, columns[row], value[16:32, 0:128]
-                ).astype(bf16)
+            value = window[skip : skip + rows]
+            at = (i * 4 + q % 4) * 4 + q // 4
+            parts[at, 0:16, :] = value[0:16].astype(bf16)
+            parts[at, 16:32, 128:] = value[16:32, 128:].astype(bf16)
+            parts[at, 16:32, 0:128] = jnp.where(
+                spare, columns[q * 8 + i], value[16:32, 0:128]
+            ).astype(bf16)
         return carry
 
-    lax.fori_loop(0, peers // 8, pairs, 0)
+    lax.fori_loop(0, peers // 8, blocks, 0)
 
 
 def freq_grad_kernel(features, core, ids, d0, d1, d2, keep, send, acc0, acc1, acc2, acc3):
@@ -297,17 +304,14 @@
     lax.fori_loop(0, keep.shape[0], block, 0)
 
 
-def owner_kernel(peers, stride, cap, asked, alone, pair, out, rows, acc0, acc1, acc2, acc3):
+def owner_kernel(peers, stride, cap, asked, arrived, out, rows, acc0, acc1, acc2, acc3):
     accs = (acc0, acc1, acc2, acc3)
     for a in accs:
         a[...] = jnp.zeros_like(a)
     emb = out.shape[1]
     for m in range(3):
-        if m == 0:
-            rows[...] = alone[...].astype(f32)
-        else:
-            part = pair[:, (m - 1) * cap : m * cap, :]
-            rows[...] = part.astype(f32).reshape(peers * cap, emb)
+        part = arrived[:, m * cap : (m + 1) * cap, :]
+        rows[...] = part.astype(f32).reshape(peers * cap, emb)
 
         def peer(d, carry):
             for c in range(0, cap, 4):
@@ -371,18 +375,20 @@
     line = jnp.pad(line, ((0, 0), (0, stride - micro * cap)), constant_values=owned)
     asked = lax.all_to_all(line, "dev", split_axis=0, concat_axis=0, tiled=True).reshape(-1)
 
-    freq_part = local_call(
-        functools.partial(freq_kernel, features, samples),
-        [((n_slots, emb), f32)] * micro,
-        [SMEM, VMEM],
-        [pltpu.VMEM((freq_rows, emb), f32)],
-        "freq_rows",
-        62,
-        0,
-        50 * MIB,
-    )(ids, freq_table)
-
-    asked, freq_part = lax.optimization_barrier((asked, freq_part))
+    def freq_rows_of(first_micro, count):
+        return local_call(
+            functools.partial(freq_kernel, features, samples, first_micro),
+            [((n_slots, emb), f32)] * count,
+            [SMEM, VMEM],
+            [pltpu.VMEM((freq_rows, emb), f32)],
+            f"freq_rows{first_micro}",
+            62,
+            0,
+            (12 + 14 * count) * MIB,
+        )(ids, freq_table)
+
+    freq_part = list(freq_rows_of(0, 1))
+    asked, freq_part[0] = lax.optimization_barrier((asked, freq_part[0]))
     asked_row = jnp.minimum(asked, owned - 1)
     weight = out_w.astype(f32).reshape(1, width)
     bias = cross_bias.reshape(1, width)
@@ -395,36 +401,31 @@
         ).reshape(n_req * count // cap, emb)
 
     outs = []
-    arrived = []
-    looked_all = []
+
+    def lookup(start, count):
+        return local_call(
+            functools.partial(lookup_kernel, devices, stride, start, count),
+            [((devices * count, emb), bf16)],
+            [SMEM, VMEM],
+            [pltpu.VMEM((owned, emb), f32), pltpu.VMEM((devices * count, emb), f32)],
+            f"lookup{start}",
+            62,
+            0,
+            count * MIB * 5 // 8,
+        )(asked_row, inf_table)[0]
+
+    looked = lookup(0, cap)
+    asked_row, looked = lax.optimization_barrier((asked_row, looked))
+    looked_rest = lookup(cap, (micro - 1) * cap)
+    fetched = exchange(looked, cap)
+    looked_rest, fetched = lax.optimization_barrier((looked_rest, fetched))
+    fetched_rest = exchange(looked_rest, (micro - 1) * cap)
+    ids, looked_rest = lax.optimization_barrier((ids, looked_rest))
+    freq_part += freq_rows_of(1, micro - 1)
+    fetched, freq_part[1] = lax.optimization_barrier((fetched, freq_part[1]))
     for m in range(micro):
-        (looked,) = local_call(
-            functools.partial(lookup_kernel, devices, stride, m * cap, cap),
-            [((n_req, emb), bf16)],
-            [SMEM, VMEM],
-            [pltpu.VMEM((owned, emb), f32), pltpu.VMEM((n_req, emb), f32)],
-            f"lookup{m}",
-            24,
-            0,
-            20 * MIB,
-        )(asked_row, inf_table)
-        asked_row, looked = lax.optimization_barrier((asked_row, looked))
-        looked_all.append(looked)
-    looked_all[1], looked_all[2] = lax.optimization_barrier((looked_all[1], looked_all[2]))
-    fetched = exchange(looked_all[0], cap)
-    later = exchange(looked_all[1], cap)
-    pair = None
-    for m in range(micro):
-        if m > 0:
-            fetched = later
         if m == 1:
-            looked_all[2], outs[0][6] = lax.optimization_barrier((looked_all[2], outs[0][6]))
-            later = exchange(looked_all[2], cap)
-            fetched, outs[0][6] = lax.optimization_barrier((fetched, outs[0][6]))
-        if m == 2:
-            fetched, outs[1][6] = lax.optimization_barrier((fetched, outs[1][6]))
-            back, outs[1][6] = lax.optimization_barrier((outs[0][0], outs[1][6]))
-            arrived.append(exchange(back, cap))
+            fetched_rest, outs[0][6] = lax.optimization_barrier((fetched_rest, outs[0][6]))
         out = local_call(
             functools.partial(
                 micro_kernel,
@@ -432,11 +433,12 @@
                 cap,
                 features,
                 m * n_req,
-                cap if m == 2 else 0,
+                max(m - 1, 0) * cap,
+                m * cap,
                 loss_mult,
             ),
             [
-                ((devices, cap if m == 0 else 2 * cap, emb), bf16),
+                ((devices, micro * cap, emb), bf16),
                 ((n_slots, emb), f32),
                 ((samples, width), bf16),
                 ((samples, rank), bf16),
@@ -444,23 +446,25 @@
                 ((samples, width), bf16),
                 ((2, width), f32),
             ],
-            [SMEM, SMEM] + [VMEM] * 8 + ([HBM] if m == 2 else []),
+            [SMEM, SMEM, HBM, HBM, VMEM, VMEM, HBM, HBM, VMEM, VMEM] + ([HBM] if m else []),
             [pltpu.VMEM((n_req, emb), f32)]
             + [pltpu.VMEM((n_slots + 8, emb), f32)] * 4
             + [pltpu.VMEM((samples, width), f32)]
             + [pltpu.VMEM((devices, cap, emb), bf16), pltpu.VMEM((samples, width), bf16)]
             + [pltpu.VMEM((samples, rank), bf16)] * 2
-            + [pltpu.VMEM((samples, width), bf16), pltpu.SemaphoreType.DMA((6,))],
+            + [pltpu.VMEM((samples, width), bf16)]
+            + [pltpu.VMEM((width, rank), bf16), pltpu.VMEM((rank, width), bf16)]
+            + [pltpu.SemaphoreType.DMA((10,))],
             f"micro{m}",
             62,
             6 * samples * width * rank,
             60 * MIB,
             [HBM] * 6 + [VMEM],
-            {10: 0} if m == 2 else {},
+            {10: 0} if m else {},
         )(
             place,
             bias_b,
-            fetched,
+            (fetched_rest if m else fetched).reshape(devices, -1, emb),
             freq_part[m],
             bottom[m],
             label_cols[m],
@@ -468,10 +472,12 @@
             cross_v,
             bias,
             weight,
-            *([outs[1][0]] if m == 2 else []),
+            *([outs[m - 1][0]] if m else []),
         )
         outs.append(list(out))
-    arrived.append(exchange(outs[2][0], 2 * cap))
+        if m == 1:
+            place, outs[1][6] = lax.optimization_barrier((place, outs[1][6]))
+    arrived = exchange(outs[2][0], micro * cap)
     d_pooled = [o[1] for o in outs]
     grad_bw = ((outs[0][6] + outs[1][6]) + outs[2][6]).reshape(2, devices, per)
     columns = jnp.pad(
@@ -480,7 +486,36 @@
 
     rows_pad = -(-per // 16) * 16
     per_freq = freq_rows // devices
-    d_pooled, arrived[0] = lax.optimization_barrier((d_pooled, arrived[0]))
+    (dense,) = local_call(
+        functools.partial(dense_grad_kernel, devices, per),
+        [((devices, rows_pad, 2 * rank), bf16)],
+        [VMEM] * 13,
+        [pltpu.VMEM((width + 16, 2 * rank), f32)],
+        "dense_grads",
+        62,
+        12 * samples * width * rank,
+        40 * MIB,
+    )(
+        columns,
+        *[o[2] for o in outs],
+        *[o[5] for o in outs],
+        *[o[3] for o in outs],
+        *[o[4] for o in outs],
+    )
+    core, dense = lax.optimization_barrier((core, dense))
+    for step, size in ((1, 8), (8, 4), (32, 4)):
+        groups = [
+            [d + k * step for k in range(size)]
+            for d in range(devices)
+            if d // step % size == 0
+        ]
+        dense = lax.psum_scatter(dense, "dev", axis_index_groups=groups, tiled=True)
+    dense = dense.reshape(rows_pad, 2 * rank).astype(f32)
+    grad_u = dense[:per, :rank]
+    grad_v = dense[:per, rank:].T
+    grad_b = dense[per, :per]
+    grad_w = dense[per + 1, :per]
+
     keep_f, send_f = local_call(
         functools.partial(freq_grad_kernel, features),
         [((devices // 2, per_freq, emb), bf16)] * 2,
@@ -491,55 +526,36 @@
         0,
         120 * MIB,
     )(core, ids, *d_pooled)
-    send_f, arrived[1] = lax.optimization_barrier((send_f, arrived[1]))
+    send_f, arrived = lax.optimization_barrier((send_f, arrived))
     got = lax.ppermute(send_f, "dev", other_core)
-    both_f = (keep_f.astype(f32) + got.astype(f32)).astype(bf16)
-    core_d, columns, both_f = lax.optimization_barrier((core, columns, both_f))
-    parts_f = lax.all_to_all(
-        both_f, "dev", split_axis=0, concat_axis=0, axis_index_groups=same_core, tiled=True
-    )
-    keep, send = local_call(
-        functools.partial(dense_grad_kernel, devices, per),
-        [((devices // 2, rows_pad, 2 * rank), bf16)] * 2,
-        [SMEM] + [VMEM] * 13,
-        [pltpu.VMEM((width + 16, 2 * rank), f32)],
-        "dense_grads",
-        62,
-        12 * samples * width * rank,
-        40 * MIB,
-    )(
-        core_d,
-        columns,
-        *[o[2] for o in outs],
-        *[o[5] for o in outs],
-        *[o[3] for o in outs],
-        *[o[4] for o in outs],
-    )
-    got = lax.ppermute(send, "dev", other_core)
-    both = (keep.astype(f32) + got.astype(f32)).astype(bf16)
-    both, parts_f = lax.optimization_barrier((both, parts_f))
+    both = (keep_f.astype(f32) + got.astype(f32)).astype(bf16)
     parts = lax.all_to_all(
         both, "dev", split_axis=0, concat_axis=0, axis_index_groups=same_core, tiled=True
     )
-    dense = jnp.sum(parts.astype(f32), axis=0)
-    grad_u = dense[:per, :rank]
-    grad_v = dense[:per, rank:].T
-    grad_b = dense[per, :per]
-    grad_w = dense[per + 1, :per]
-
-    mine = jnp.sum(parts_f.astype(f32), axis=0).astype(bf16)
-    grad_freq = lax.all_gather(mine, "dev", tiled=True)
+    mine = jnp.sum(parts.astype(f32), axis=0).astype(bf16)
+    half = lax.all_to_all(
+        jnp.broadcast_to(mine[None], parts.shape),
+        "dev",
+        split_axis=0,
+        concat_axis=0,
+        axis_index_groups=same_core,
+        tiled=True,
+    )
+    rest = lax.ppermute(half, "dev", other_core)
+    grad_freq = jnp.where(
+        core[0] == 0, jnp.stack([half, rest], axis=1), jnp.stack([rest, half], axis=1)
+    ).reshape(freq_rows, emb)
 
     (grad_inf,) = local_call(
         functools.partial(owner_kernel, devices, stride, cap),
         [((owned, emb), bf16)],
-        [SMEM] + [VMEM] * 2,
+        [SMEM, VMEM],
         [pltpu.VMEM((n_req, emb), f32)] + [pltpu.VMEM((owned + 8, emb), f32)] * 4,
         "owner_grads",
         32,
         0,
         60 * MIB,
-    )(asked, arrived[0], arrived[1].reshape(devices, 2 * cap, emb))
+    )(asked, arrived.reshape(devices, micro * cap, emb))
 
     return (grad_u, grad_v, grad_b, grad_w, grad_freq, grad_inf)
 

time: 403 us -> 366 us (0.908)
  blocking collectives: 0 us -> 33.2 us
  starting transfers between devices: 75.7 us -> 46.9 us
  waiting for transfers between devices: 102 us -> 73.8 us
  other arithmetic: 19.9 us -> 11 us
    reduce_scatter x0 -> x3, waiting for transfers between devices: none -> 55.1 us  [on_device(): dense = lax.psum_scatter(dense, 'dev', axis_index_groups=groups, tiled=True)]
    all_to_all x2 -> x1, waiting for transfers between devices: 48.3 us -> 0.01 us  [on_device(): lax.all_to_all(jnp.broadcast_to(mine[None], parts.shape), 'dev', split_ax...]
    all_gather x1 -> x0, waiting for transfers between devices: 45.2 us -> none  [on_device(): grad_freq = lax.all_gather(mine, 'dev', tiled=True)]
    all_to_all x0 -> x1, blocking collectives: none -> 33.2 us  [on_device(): lax.all_to_all(both, 'dev', split_axis=0, concat_axis=0, axis_index_group...]
    all_to_all x5 -> x3, starting transfers between devices: 45.2 us -> 25.7 us  [exchange(): lax.all_to_all(rows.reshape(devices, count, emb), 'dev', split_axis=0, co...]
    all_to_all x2 -> x1, starting transfers between devices: 17.5 us -> 7.91 us  [on_device(): lax.all_to_all(jnp.broadcast_to(mine[None], parts.shape), 'dev', split_ax...]
    convert_element_type x2, other arithmetic: 12.7 us -> 3.29 us  [the longest x1 2.44 us: on_device(): both = (keep_f.astype(f32) + got.astype(f32)).astype(bf16)]
    all_to_all x5 -> x3, waiting for transfers between devices: 5.47 us -> 14.7 us  [exchange(): lax.all_to_all(rows.reshape(devices, count, emb), 'dev', split_axis=0, co...]
  transfers between devices with their start and end apart: 11 -> 10, of which waited for: 5 -> 5; matrix products, arithmetic and copies ran while one was open for 5% -> 4% of each run, Pallas kernels for 39% -> 32%
where the time goes in v3:
time: 366 us; the launch traced here: 364 us
  Pallas kernels  173 us (47%)
  waiting for transfers between devices  73.8 us (20%)
  starting transfers between devices  46.9 us (13%)
  blocking collectives  33.2 us (9%)
  between operations  14.6 us (4%)
  local copies, waits for them, and re-layouts  11.7 us (3%)
  other arithmetic  11 us (3%)
    pallas_call x3, Pallas kernels, on_device(): local_call(functools.partial(micro_kernel, devices, cap, features, m * n_...  56.9 us
    reduce_scatter x3, waiting for transfers between devices, on_device(): dense = lax.psum_scatter(dense, 'dev', axis_index_groups=groups, tiled=True)  55.1 us
    pallas_call x1, Pallas kernels, on_device(): local_call(functools.partial(freq_grad_kernel, features), [((devices // 2...  35.7 us
    all_to_all x1, blocking collectives, on_device(): lax.all_to_all(both, 'dev', split_axis=0, concat_axis=0, axis_index_group...  33.2 us
    pallas_call x2, Pallas kernels, freq_rows_of(): local_call(functools.partial(freq_kernel, features, samples, first_micro)...  29.1 us
    all_to_all x3, starting transfers between devices, exchange(): lax.all_to_all(rows.reshape(devices, count, emb), 'dev', split_axis=0, co...  25.7 us
    pallas_call x1, Pallas kernels, on_device(): local_call(functools.partial(owner_kernel, devices, stride, cap), [((owne...  21.6 us
    pallas_call x2, Pallas kernels, lookup(): local_call(functools.partial(lookup_kernel, devices, stride, start, count...  17.4 us
  transfers between devices with their start and end apart: 10, of which 5 were waited for; matrix products, arithmetic and copies ran while one was open for 4% of the time, Pallas kernels for 32%

profile of v3, /device:TPU:1, one launch (start us, length us, event | category | flops | bytes accessed | tf_op | source)
XLA Modules:
  0.0 364.5 jit_solution(2478035360197788302)
XLA Ops:
  7.2 0.8 bitcast_select_fusion
  8.0 0.7 copy.54
  8.7 11.5 %all-to-all-start = ((s32[128,1,128]{2,1,0:T(1,128)}), s32[128,1,128]{2,1,0:T(1,128)S(1)}, u32[]{:S(2)}, u32[]{:S(2)}) async-start(s32[128,1,128]{2,1,0:T(1,128)} %copy.54), calls=%async_computation | async-start | bytes 131072 | tf_op jit(solution)/shard_map/all_to_all | solution.py:376
  20.3 1.6 reshape.102.ids
  21.8 10.9 %freq_rows0.1.freq_part_hbm = f32[3328,128]{1,0:T(8,128)} custom-call(s32[19968]{0:T(1024)} %reshape.102.ids, bf16[16384,128]{1,0:T(8,128)(2,1)} %table_ref.7), custom_call_target="tpu_custom_call" | custom-call | bytes 27262976 | tf_op jit(solution)/shard_map/freq_rows0/pallas_call | solution.py:379
  32.8 0.6 broadcast_minimum_fusion.asked
  33.4 6.8 %lookup0.1 = bf16[4096,128]{1,0:T(8,128)(2,1)} custom-call(s32[16384]{0:T(1024)} %broadcast_minimum_fusion.asked, bf16[4096,128]{1,0:T(8,128)(2,1)} %table_ref.6), custom_call_target="tpu_custom_call" | custom-call | bytes 20971520 | tf_op jit(solution)/shard_map/lookup0/pallas_call | solution.py:406
  40.2 9.8 %all-to-all-start.1 = ((bf16[128,32,128]{2,1,0:T(8,128)(2,1)}), bf16[128,32,128]{2,1,0:T(8,128)(2,1)S(1)}, u32[]{:S(2)}, u32[]{:S(2)}) async-start(bf16[128,32,128]{2,1,0:T(8,128)(2,1)} %bitcast.118), calls=%async_computation.1 | async-start | bytes 2097152 | tf_op jit(solution)/shard_map/all_to_all | solution.py:399
  50.0 10.5 %lookup32.1 = bf16[8192,128]{1,0:T(8,128)(2,1)} custom-call(s32[16384]{0:T(1024)} %broadcast_minimum_fusion.asked, bf16[4096,128]{1,0:T(8,128)(2,1)} %table_ref.6), custom_call_target="tpu_custom_call" | custom-call | bytes 41943040 | tf_op jit(solution)/shard_map/lookup32/pallas_call | solution.py:406
  60.5 8.8 %all-to-all-done.1 = bf16[128,32,128]{2,1,0:T(8,128)(2,1)S(1)} async-done(((bf16[128,32,128]{2,1,0:T(8,128)(2,1)}), bf16[128,32,128]{2,1,0:T(8,128)(2,1)S(1)}, u32[]{:S(2)}, u32[]{:S(2)}) %all-to-all-start.1) | async-done | bytes 1048608 | tf_op jit(solution)/shard_map/all_to_all | solution.py:399
  69.3 0.9 copy-done
  70.3 5.7 %all-to-all-start.2 = ((bf16[128,64,128]{2,1,0:T(8,128)(2,1)}), bf16[128,64,128]{2,1,0:T(8,128)(2,1)}, u32[]{:S(2)}, u32[]{:S(2)}) async-start(bf16[128,64,128]{2,1,0:T(8,128)(2,1)} %bitcast.115), calls=%async_computation.2 | async-start | bytes 4194304 | tf_op jit(solution)/shard_map/all_to_all | solution.py:399
  75.9 0.2 reduce-scatter.4.cloned.1.call-start
  76.2 0.7 copy.58.labels
  76.9 0.6 reshape.110.bias
  77.5 0.6 reshape.118.weight
  78.8 0.7 copy.59.labels
  79.5 0.7 copy.60.labels
  80.3 0.7 slice_bitcast_fusion.1
  80.9 0.7 fusion.2
  81.6 18.2 %freq_rows1.1 = (f32[3328,128]{1,0:T(8,128)}, f32[3328,128]{1,0:T(8,128)}) custom-call(s32[19968]{0:T(1024)} %reshape.102.ids, bf16[16384,128]{1,0:T(8,128)(2,1)} %table_ref.7), custom_call_target="tpu_custom_call" | custom-call | bytes 41943040 | tf_op jit(solution)/shard_map/freq_rows1/pallas_call | solution.py:379
  99.9 18.9 %micro0.1 = (bf16[128,96,128]{2,1,0:T(8,128)(2,1)}, f32[3328,128]{1,0:T(8,128)}, bf16[128,3456]{1,0:T(8,128)(2,1)}, bf16[128,512]{1,0:T(8,128)(2,1)}, bf16[128,5...) custom-call(s32[12288]{0:T(1024)} %bitcast.119, f32[1]{0:T(128)} %bitcast.110.out_b, ...), custom_call_target="tpu_custom_call" | custom-call | flops 1358954496 | bytes 62914560 | tf_op jit(solution)/shard_map/micro0/pallas_call | solution.py:429
  118.7 18.9 %micro1.1 = (bf16[128,96,128]{2,1,0:T(8,128)(2,1)}, f32[3328,128]{1,0:T(8,128)}, bf16[128,3456]{1,0:T(8,128)(2,1)}, bf16[128,512]{1,0:T(8,128)(2,1)}, bf16[128,5...) custom-call(s32[12288]{0:T(1024)} %bitcast.120, ...), custom_call_target="tpu_custom_call", output_to_operand_aliasing={{0}: (10, {})} | custom-call | flops 1358954496 | bytes 62914560 | tf_op jit(solution)/shard_map/micro1/pallas_call | solution.py:429
  137.7 19.1 %micro2.1 = (bf16[128,96,128]{2,1,0:T(8,128)(2,1)}, f32[3328,128]{1,0:T(8,128)}, bf16[128,3456]{1,0:T(8,128)(2,1)}, bf16[128,512]{1,0:T(8,128)(2,1)}, bf16[128,5...) custom-call(s32[12288]{0:T(1024)} %bitcast.121, ...), custom_call_target="tpu_custom_call", output_to_operand_aliasing={{0}: (10, {})} | custom-call | flops 1358954496 | bytes 62914560 | tf_op jit(solution)/shard_map/micro2/pallas_call | solution.py:429
  156.8 0.8 add_add_fusion
  157.6 0.2 reshape.114
  157.8 0.1 copy.65
  157.9 1.1 pad.9.columns
  159.0 12.6 %dense_grads.1 = bf16[128,32,1024]{2,1,0:T(8,128)(2,1)} custom-call(f32[128,16,128]{2,1,0:T(8,128)} %pad.9.columns, bf16[128,3456]{1,0:T(8,128)(2,1)} %get-tuple-element.68.x0, bf16[128,3456]{1,0:T(8,128)(2,1)} %get-tuple-element.69.x1, bf16[128,3456]{1,0:T(8,128)(2,1)} %get-tuple-element.70.x2, bf16[128,3456]{1,0:T(8,128)(2,1)} %get-tuple-element.71.g0, ...), custom_call_target="tpu_custom_call" | custom-call | flops 2717908992 | bytes 41943040 | tf_op jit(solution)/shard_map/dense_grads/pallas_call | solution.py:489
  171.6 10.3 %all-to-all-start.3 = ((bf16[128,96,128]{2,1,0:T(8,128)(2,1)}), bf16[128,96,128]{2,1,0:T(8,128)(2,1)}, u32[]{:S(2)}, u32[]{:S(2)}) async-start(bf16[128,96,128]{2,1,0:T(8,128)(2,1)} %get-tuple-element.87), calls=%async_computation.6 | async-start | bytes 6291456 | tf_op jit(solution)/shard_map/all_to_all | solution.py:399
  181.9 35.7 %freq_grads.1 = (bf16[64,128,128]{2,1,0:T(8,128)(2,1)}, bf16[64,128,128]{2,1,0:T(8,128)(2,1)}) custom-call(s32[1]{0:T(128)} %bitcast.core, s32[19968]{0:T(1024)} %reshape.102.ids, f32[3328,128]{1,0:T(8,128)} %get-tuple-element.82.d0, f32[3328,128]{1,0:T(8,128)} %get-tuple-element.83.d1, f32[3328,128]{1,0:T(8,128)} %get-tuple-element.84.d2), custom_call_target="tpu_custom_call" | custom-call | bytes 125829120 | tf_op jit(solution)/shard_map/freq_grads/pallas_call | solution.py:519
  217.6 5.9 %all-to-all-done.3 = bf16[128,96,128]{2,1,0:T(8,128)(2,1)} async-done(((bf16[128,96,128]{2,1,0:T(8,128)(2,1)}), bf16[128,96,128]{2,1,0:T(8,128)(2,1)}, u32[]{:S(2)}, u32[]{:S(2)}) %all-to-all-start.3) | async-done | bytes 3145760 | tf_op jit(solution)/shard_map/all_to_all | solution.py:399
  223.5 1.1 collective-permute-start
  224.6 4.0 %collective-permute-done = bf16[64,128,128]{2,1,0:T(8,128)(2,1)S(1)} collective-permute-done((bf16[64,128,128]{2,1,0:T(8,128)(2,1)}, bf16[64,128,128]{2,1,0:T(8,128)(2,1)S(1)}, u32[]{:S(2)}, u32[]{:S(2)}) %collective-permute-start) | collective-permute-done | bytes 2097184 | tf_op jit(solution)/shard_map/ppermute | solution.py:530
  228.6 2.4 add_convert_fusion
  231.0 33.2 %all_to_all.34 = bf16[64,128,128]{2,1,0:T(8,128)(2,1)S(1)} all-to-all(bf16[64,128,128]{2,1,0:T(8,128)(2,1)S(1)} %add_convert_fusion), channel_id=1, replica_groups={{0,2,4,6,8,10,12,14,16,18,20,22,24,26,28,30,32,34,36,38,40,42,44,46,48,..., dimensions={0} | all-to-all | bytes 4194304 | tf_op jit(solution)/shard_map/all_to_all | solution.py:532
  264.2 0.3 reduce_sum.12
  264.5 1.8 broadcast_in_dim.6
  266.3 7.9 %all-to-all-start.5 = ((bf16[64,128,128]{2,1,0:T(8,128)(2,1)}), bf16[64,128,128]{2,1,0:T(8,128)(2,1)S(1)}, u32[]{:S(2)}, u32[]{:S(2)}) async-start(bf16[64,128,128]{2,1,0:T(8,128)(2,1)} %broadcast_in_dim.6), calls=%async_computation.8 | async-start | bytes 4194304 | tf_op jit(solution)/shard_map/all_to_all | solution.py:536
  274.2 0.0 reduce-scatter.6.cloned.1.call-start
  274.3 30.2 %reduce-scatter.4.cloned.1.call-done = bf16[16,32,1024]{2,1,0:T(8,128)(2,1)} async-done(((bf16[128,32,1024]{2,1,0:T(8,128)(2,1)}), bf16[16,32,1024]{2,1,0:T(8,128)(2,1)}) %reduce-scatter.4.cloned.1.call-update) | async-done | bytes 1048592 | tf_op jit(solution)/shard_map/reduce_scatter | solution.py:512
  304.5 0.3 collective-permute-start.1
  304.9 24.9 %reduce-scatter.6.cloned.1.call-done = bf16[4,32,1024]{2,1,0:T(8,128)(2,1)} async-done(((bf16[16,32,1024]{2,1,0:T(8,128)(2,1)}), bf16[4,32,1024]{2,1,0:T(8,128)(2,1)}) %reduce-scatter.6.cloned.1.call-update) | async-done | bytes 262160 | tf_op jit(solution)/shard_map/reduce_scatter | solution.py:512
  329.8 21.6 %owner_grads.1 = bf16[4096,128]{1,0:T(8,128)(2,1)} custom-call(s32[16384]{0:T(1024)S(1)} %bitcast.114, bf16[128,96,128]{2,1,0:T(8,128)(2,1)} %bitcast.43.arrived), custom_call_target="tpu_custom_call" | custom-call | bytes 62914560 | tf_op jit(solution)/shard_map/owner_grads/pallas_call | solution.py:549
  351.5 4.5 %maximum_select_fusion = bf16[64,2,128,128]{3,2,1,0:T(8,128)(2,1)} fusion(bf16[64,1,128,128]{3,2,1,0:T(8,128)(2,1)} %bitcast.41, bf16[64,1,128,128]{3,2,1,0:T(8,128)(2,1)S(1)} %bitcast.116, pred[]{:T(512)} %bitcast.38), kind=kLoop, calls=%fused_computation | loop fusion | flops 6291456 | bytes 8388609 | tf_op jit(solution)/shard_map/jit(_where)/select_n | solution.py:545
  355.9 0.8 bitcast_convert_fusion
  356.8 0.7 slice_bitcast_fusion
  357.4 0.5 slice_bitcast_fusion.4
  (29 shorter events, 0.2 us)
Async XLA Ops:
  8.7 24.0 %all-to-all-start = ((s32[128,1,128]{2,1,0:T(1,128)}), s32[128,1,128]{2,1,0:T(1,128)S(1)}, u32[]{:S(2)}, u32[]{:S(2)}) async-start(s32[128,1,128]{2,1,0:T(1,128)} %copy.54), calls=%async_computation | async-start | bytes 131072 | tf_op jit(solution)/shard_map/all_to_all | solution.py:376
  40.2 29.0 %all-to-all-start.1 = ((bf16[128,32,128]{2,1,0:T(8,128)(2,1)}), bf16[128,32,128]{2,1,0:T(8,128)(2,1)S(1)}, u32[]{:S(2)}, u32[]{:S(2)}) async-start(bf16[128,32,128]{2,1,0:T(8,128)(2,1)} %bitcast.118), calls=%async_computation.1 | async-start | bytes 2097152 | tf_op jit(solution)/shard_map/all_to_all | solution.py:399
  69.3 1.0 copy-start
  69.3 6.9 %copy-start.8 = (s32[3,128]{1,0:T(4,128)S(1)}, s32[3,128]{1,0:T(4,128)}, u32[]{:S(2)}) copy-start(s32[3,128]{1,0:T(4,128)} %param.13) | copy-start | bytes 4612
  69.3 7.6 %copy-start.6 = (f32[3456]{0:T(1024)S(1)}, f32[3456]{0:T(1024)}, u32[]{:S(2)}) copy-start(f32[3456]{0:T(1024)} %param.21) | copy-start | bytes 41476
  69.3 8.2 %copy-start.7 = (bf16[3456]{0:T(1024)(128)(2,1)S(1)}, bf16[3456]{0:T(1024)(128)(2,1)}, u32[]{:S(2)}) copy-start(bf16[3456]{0:T(1024)(128)(2,1)} %param.22) | copy-start | bytes 20740
  69.3 11.0 %copy-start.3 = (bf16[3,128,128]{2,1,0:T(8,128)(2,1)S(1)}, bf16[3,128,128]{2,1,0:T(8,128)(2,1)}, u32[]{:S(2)}) copy-start(bf16[3,128,128]{2,1,0:T(8,128)(2,1)} %param.12) | copy-start | bytes 294916
  69.3 11.6 %copy-start.1 = (s32[3,1,128,32]{2,3,1,0:T(8,128)S(1)}, s32[3,1,128,32]{2,3,1,0:T(8,128)}, u32[]{:S(2)}) copy-start(s32[3,1,128,32]{2,3,1,0:T(8,128)} %param.16) | copy-start | bytes 147460
  69.3 11.6 %copy-start.2 = (s32[3,1,128,32]{2,3,1,0:T(8,128)S(1)}, s32[3,1,128,32]{2,3,1,0:T(8,128)}, u32[]{:S(2)}) copy-start(s32[3,1,128,32]{2,3,1,0:T(8,128)} %param.15) | copy-start | bytes 147460
  70.3 48.5 %all-to-all-start.2 = ((bf16[128,64,128]{2,1,0:T(8,128)(2,1)}), bf16[128,64,128]{2,1,0:T(8,128)(2,1)}, u32[]{:S(2)}, u32[]{:S(2)}) async-start(bf16[128,64,128]{2,1,0:T(8,128)(2,1)} %bitcast.115), calls=%async_computation.2 | async-start | bytes 4194304 | tf_op jit(solution)/shard_map/all_to_all | solution.py:399
  75.9 228.5 %reduce-scatter.4.cloned.1.call-start = ((), (), s32[]{:S(2)}) async-start(), calls=%async_computation.9 | async-start | bytes 9437184 | tf_op jit(solution)/shard_map/reduce_scatter | solution.py:512
  137.7 19.2 %copy-start.4 = (f32[2,3456]{1,0:T(2,128)S(1)}, f32[2,3456]{1,0:T(2,128)}, u32[]{:S(2)}) copy-start(f32[2,3456]{1,0:T(2,128)} %get-tuple-element.58) | copy-start | bytes 82948
  137.7 19.2 %copy-start.5 = (f32[2,3456]{1,0:T(2,128)S(1)}, f32[2,3456]{1,0:T(2,128)}, u32[]{:S(2)}) copy-start(f32[2,3456]{1,0:T(2,128)} %get-tuple-element.63) | copy-start | bytes 82948
  171.6 51.9 %all-to-all-start.3 = ((bf16[128,96,128]{2,1,0:T(8,128)(2,1)}), bf16[128,96,128]{2,1,0:T(8,128)(2,1)}, u32[]{:S(2)}, u32[]{:S(2)}) async-start(bf16[128,96,128]{2,1,0:T(8,128)(2,1)} %get-tuple-element.87), calls=%async_computation.6 | async-start | bytes 6291456 | tf_op jit(solution)/shard_map/all_to_all | solution.py:399
  223.5 5.1 %collective-permute-start = (bf16[64,128,128]{2,1,0:T(8,128)(2,1)}, bf16[64,128,128]{2,1,0:T(8,128)(2,1)S(1)}, u32[]{:S(2)}, u32[]{:S(2)}) collective-permute-start(bf16[64,128,128]{2,1,0:T(8,128)(2,1)} %get-tuple-element.88), channel_id=1, source_target_pairs={{0,1},{1,0},{2,3},{3,2},{4,5},{5,4},{6,7},{7,6},{8,9},{9,8},{10,11... | collective-permute-start | bytes 6291464 | tf_op jit(solution)/shard_map/ppermute | solution.py:530
  266.3 38.2 %all-to-all-start.5 = ((bf16[64,128,128]{2,1,0:T(8,128)(2,1)}), bf16[64,128,128]{2,1,0:T(8,128)(2,1)S(1)}, u32[]{:S(2)}, u32[]{:S(2)}) async-start(bf16[64,128,128]{2,1,0:T(8,128)(2,1)} %broadcast_in_dim.6), calls=%async_computation.8 | async-start | bytes 4194304 | tf_op jit(solution)/shard_map/all_to_all | solution.py:536
  274.2 55.6 %reduce-scatter.6.cloned.1.call-start = ((), (), s32[]{:S(2)}) async-start(), calls=%async_computation.10 | async-start | bytes 1310720 | tf_op jit(solution)/shard_map/reduce_scatter | solution.py:512
  304.5 51.4 %reduce-scatter.8.cloned.1.call-start = ((), (), s32[]{:S(2)}) async-start(), calls=%async_computation.11 | async-start | bytes 327680 | tf_op jit(solution)/shard_map/reduce_scatter | solution.py:512
  304.5 46.9 %collective-permute-start.1 = (bf16[64,128,128]{2,1,0:T(8,128)(2,1)S(1)}, bf16[64,128,128]{2,1,0:T(8,128)(2,1)}, u32[]{:S(2)}, u32[]{:S(2)}) collective-permute-start(bf16[64,128,128]{2,1,0:T(8,128)(2,1)S(1)} %all-to-all-done.5), channel_id=1, source_target_pairs={{0,1},{1,0},{2,3},{3,2},{4,5},{5,4},{6,7},{7,6},{8,9},{9,8},{10,11... | collective-permute-start | bytes 6291464 | tf_op jit(solution)/shard_map/ppermute | solution.py:544
Sparse Core Ops, SparseCore 0:
  171.7 132.7 reduce-scatter.3
  306.9 22.9 reduce-scatter.5
  332.3 19.4 reduce-scatter.7

commit v4 on v3

--- a/solution.py
+++ b/solution.py
@@ -77,6 +77,7 @@
     peers,
     cap,
     features,
+    m,
     slot_start,
     fetch_start,
     ret_start,
@@ -117,7 +118,7 @@
         sems,
     ) = refs[-21:]
     samples, width = x_zero.shape
-    emb = bottom.shape[1]
+    emb = bottom.shape[2]
     n_slots = features * samples
     accs = (acc0, acc1, acc2, acc3)
     loads = [
@@ -150,7 +151,7 @@
 
     lax.fori_loop(0, peers, add_peer, 0)
 
-    x_zero[:, 0:emb] = bottom[...]
+    x_zero[:, 0:emb] = bottom[m]
     for f in range(features):
         rows = pl.ds(f * samples, samples)
         total = (acc0[rows, :] + acc1[rows, :]) + (acc2[rows, :] + acc3[rows, :])
@@ -178,7 +179,12 @@
         for j in range(3):
             partial = partial + scored[:, j * emb : (j + 1) * emb]
     logits = jnp.sum(partial, axis=1, keepdims=True) + out_b[0]
-    d_logit = (jax.nn.sigmoid(logits) - labels[...]) * loss_mult
+    square = (samples, samples)
+    diagonal = lax.broadcasted_iota(jnp.int32, square, 0) == lax.broadcasted_iota(
+        jnp.int32, square, 1
+    )
+    label = jnp.sum(jnp.where(diagonal, labels[m : m + 1, :], 0.0), axis=1, keepdims=True)
+    d_logit = (jax.nn.sigmoid(logits) - label) * loss_mult
     for k in range(chunks):
         cols = slice(k * chunk, (k + 1) * chunk)
         x_float = x_zero[:, cols].astype(f32)
@@ -228,7 +234,7 @@
 
 
 def dense_grad_kernel(
-    peers, per, columns, x0, x1, x2, g0, g1, g2, h0, h1, h2, e0, e1, e2, parts, total
+    peers, per, columns, x0, x1, x2, g0, g1, g2, h0, h1, h2, e0, e1, e2, parts_hbm, total, parts, sem
 ):
     width = x0.shape[1]
     rank = h0.shape[1]
@@ -244,7 +250,7 @@
             g_all, h_all, TN, preferred_element_type=f32
         )
     total[width:, :] = jnp.zeros((total.shape[0] - width, 2 * rank), f32)
-    rows = parts.shape[1]
+    rows = parts.shape[2]
     spare = lax.broadcasted_iota(jnp.int32, (16, 128), 0) >= per - 16
 
     def blocks(q, carry):
@@ -253,24 +259,43 @@
             skip = i * per % 8
             window = total[pl.ds(pl.multiple_of(base + (i * per - skip), 8), rows + 8), :]
             value = window[skip : skip + rows]
-            at = (i * 4 + q % 4) * 4 + q // 4
-            parts[at, 0:16, :] = value[0:16].astype(bf16)
-            parts[at, 16:32, 128:] = value[16:32, 128:].astype(bf16)
-            parts[at, 16:32, 0:128] = jnp.where(
+            parts[q, i, 0:16, :] = value[0:16].astype(bf16)
+            parts[q, i, 16:32, 128:] = value[16:32, 128:].astype(bf16)
+            parts[q, i, 16:32, 0:128] = jnp.where(
                 spare, columns[q * 8 + i], value[16:32, 0:128]
             ).astype(bf16)
+        pltpu.make_async_copy(
+            parts.at[q], parts_hbm.at[:, q % 4 * 4 + q // 4], sem.at[q]
+        ).start()
         return carry
 
     lax.fori_loop(0, peers // 8, blocks, 0)
 
-
-def freq_grad_kernel(features, core, ids, d0, d1, d2, keep, send, acc0, acc1, acc2, acc3):
+    def ends(q, carry):
+        pltpu.make_async_copy(
+            parts.at[q], parts_hbm.at[:, q % 4 * 4 + q // 4], sem.at[q]
+        ).wait()
+        return carry
+
+    lax.fori_loop(0, peers // 8, ends, 0)
+
+
+def freq_grad_kernel(
+    features, core, ids, d0, d1, d2, keep, send, acc0, acc1, acc2, acc3, buf0, buf1, buf2, sems
+):
     accs = (acc0, acc1, acc2, acc3)
     samples = d0.shape[0] // features
+    loads = [
+        pltpu.make_async_copy(d, buf, sems.at[k])
+        for k, (d, buf) in enumerate(((d0, buf0), (d1, buf1), (d2, buf2)))
+    ]
+    for load in loads:
+        load.start()
     for a in accs:
         a[...] = jnp.zeros_like(a)
-    unroll = 32
-    for m, source in enumerate((d0, d1, d2)):
+    unroll = 64
+    for m, source in enumerate((buf0, buf1, buf2)):
+        loads[m].wait()
         start = m * features * 2 * samples
 
         def feature(f, carry):
@@ -304,13 +329,13 @@
     lax.fori_loop(0, keep.shape[0], block, 0)
 
 
-def owner_kernel(peers, stride, cap, asked, arrived, out, rows, acc0, acc1, acc2, acc3):
+def owner_kernel(peers, stride, cap, asked, first, last, out, rows, acc0, acc1, acc2, acc3):
     accs = (acc0, acc1, acc2, acc3)
     for a in accs:
         a[...] = jnp.zeros_like(a)
     emb = out.shape[1]
     for m in range(3):
-        part = arrived[:, m * cap : (m + 1) * cap, :]
+        part = last[...] if m == 2 else first[:, m * cap : (m + 1) * cap, :]
         rows[...] = part.astype(f32).reshape(peers * cap, emb)
 
         def peer(d, carry):
@@ -392,7 +417,7 @@
     asked_row = jnp.minimum(asked, owned - 1)
     weight = out_w.astype(f32).reshape(1, width)
     bias = cross_bias.reshape(1, width)
-    label_cols = labels.astype(f32).reshape(micro, samples, 1)
+    label_rows = labels.astype(f32)
     bias_b = out_b.reshape(1)
 
     def exchange(rows, count):
@@ -418,27 +443,35 @@
     asked_row, looked = lax.optimization_barrier((asked_row, looked))
     looked_rest = lookup(cap, (micro - 1) * cap)
     fetched = exchange(looked, cap)
-    looked_rest, fetched = lax.optimization_barrier((looked_rest, fetched))
+    ids, looked_rest = lax.optimization_barrier((ids, looked_rest))
+    freq_part += freq_rows_of(1, 1)
+    small = (place, weight, bias, label_rows, bias_b)
+    looked_rest, fetched, freq_part[1], small = lax.optimization_barrier(
+        (looked_rest, fetched, freq_part[1], small)
+    )
+    place, weight, bias, label_rows, bias_b = small
     fetched_rest = exchange(looked_rest, (micro - 1) * cap)
-    ids, looked_rest = lax.optimization_barrier((ids, looked_rest))
-    freq_part += freq_rows_of(1, micro - 1)
-    fetched, freq_part[1] = lax.optimization_barrier((fetched, freq_part[1]))
+    ids, freq_part[1] = lax.optimization_barrier((ids, freq_part[1]))
+    freq_part += freq_rows_of(2, 1)
     for m in range(micro):
         if m == 1:
-            fetched_rest, outs[0][6] = lax.optimization_barrier((fetched_rest, outs[0][6]))
+            fetched_rest, outs[0][6], freq_part[2] = lax.optimization_barrier(
+                (fetched_rest, outs[0][6], freq_part[2])
+            )
         out = local_call(
             functools.partial(
                 micro_kernel,
                 devices,
                 cap,
                 features,
+                m,
                 m * n_req,
                 max(m - 1, 0) * cap,
-                m * cap,
+                cap if m == 1 else 0,
                 loss_mult,
             ),
             [
-                ((devices, micro * cap, emb), bf16),
+                ((devices, cap if m == 2 else 2 * cap, emb), bf16),
                 ((n_slots, emb), f32),
                 ((samples, width), bf16),
                 ((samples, rank), bf16),
@@ -446,7 +479,7 @@
                 ((samples, width), bf16),
                 ((2, width), f32),
             ],
-            [SMEM, SMEM, HBM, HBM, VMEM, VMEM, HBM, HBM, VMEM, VMEM] + ([HBM] if m else []),
+            [SMEM, SMEM, HBM, HBM, VMEM, VMEM, HBM, HBM, VMEM, VMEM] + ([HBM] if m == 1 else []),
             [pltpu.VMEM((n_req, emb), f32)]
             + [pltpu.VMEM((n_slots + 8, emb), f32)] * 4
             + [pltpu.VMEM((samples, width), f32)]
@@ -460,24 +493,26 @@
             6 * samples * width * rank,
             60 * MIB,
             [HBM] * 6 + [VMEM],
-            {10: 0} if m else {},
+            {10: 0} if m == 1 else {},
         )(
             place,
             bias_b,
             (fetched_rest if m else fetched).reshape(devices, -1, emb),
             freq_part[m],
-            bottom[m],
-            label_cols[m],
+            bottom,
+            label_rows,
             cross_u,
             cross_v,
             bias,
             weight,
-            *([outs[m - 1][0]] if m else []),
+            *([outs[0][0]] if m == 1 else []),
         )
         outs.append(list(out))
         if m == 1:
             place, outs[1][6] = lax.optimization_barrier((place, outs[1][6]))
-    arrived = exchange(outs[2][0], micro * cap)
+    arrived_first = exchange(outs[1][0], 2 * cap)
+    outs[2][0], arrived_first = lax.optimization_barrier((outs[2][0], arrived_first))
+    arrived_last = exchange(outs[2][0], cap)
     d_pooled = [o[1] for o in outs]
     grad_bw = ((outs[0][6] + outs[1][6]) + outs[2][6]).reshape(2, devices, per)
     columns = jnp.pad(
@@ -488,13 +523,18 @@
     per_freq = freq_rows // devices
     (dense,) = local_call(
         functools.partial(dense_grad_kernel, devices, per),
-        [((devices, rows_pad, 2 * rank), bf16)],
+        [((8, devices // 8, rows_pad, 2 * rank), bf16)],
         [VMEM] * 13,
-        [pltpu.VMEM((width + 16, 2 * rank), f32)],
+        [
+            pltpu.VMEM((width + 16, 2 * rank), f32),
+            pltpu.VMEM((devices // 8, 8, rows_pad, 2 * rank), bf16),
+            pltpu.SemaphoreType.DMA((devices // 8,)),
+        ],
         "dense_grads",
         62,
         12 * samples * width * rank,
         40 * MIB,
+        [HBM],
     )(
         columns,
         *[o[2] for o in outs],
@@ -502,7 +542,8 @@
         *[o[3] for o in outs],
         *[o[4] for o in outs],
     )
-    core, dense = lax.optimization_barrier((core, dense))
+    core, dense, arrived_first = lax.optimization_barrier((core, dense, arrived_first))
+    dense = dense.reshape(devices, rows_pad, 2 * rank)
     for step, size in ((1, 8), (8, 4), (32, 4)):
         groups = [
             [d + k * step for k in range(size)]
@@ -519,19 +560,37 @@
     keep_f, send_f = local_call(
         functools.partial(freq_grad_kernel, features),
         [((devices // 2, per_freq, emb), bf16)] * 2,
-        [SMEM, SMEM] + [VMEM] * 3,
-        [pltpu.VMEM((freq_rows, emb), f32)] * 4,
+        [SMEM, SMEM] + [HBM] * 3,
+        [pltpu.VMEM((freq_rows, emb), f32)] * 4
+        + [pltpu.VMEM((n_slots, emb), f32)] * 3
+        + [pltpu.SemaphoreType.DMA((3,))],
         "freq_grads",
         62,
         0,
         120 * MIB,
     )(core, ids, *d_pooled)
-    send_f, arrived = lax.optimization_barrier((send_f, arrived))
+    send_f, arrived_last = lax.optimization_barrier((send_f, arrived_last))
     got = lax.ppermute(send_f, "dev", other_core)
     both = (keep_f.astype(f32) + got.astype(f32)).astype(bf16)
     parts = lax.all_to_all(
         both, "dev", split_axis=0, concat_axis=0, axis_index_groups=same_core, tiled=True
     )
+    (grad_inf,) = local_call(
+        functools.partial(owner_kernel, devices, stride, cap),
+        [((owned, emb), bf16)],
+        [SMEM, VMEM, VMEM],
+        [pltpu.VMEM((n_req, emb), f32)] + [pltpu.VMEM((owned + 8, emb), f32)] * 4,
+        "owner_grads",
+        32,
+        0,
+        60 * MIB,
+    )(
+        asked,
+        arrived_first.reshape(devices, 2 * cap, emb),
+        arrived_last.reshape(devices, cap, emb),
+    )
+
+    parts, grad_inf = lax.optimization_barrier((parts, grad_inf))
     mine = jnp.sum(parts.astype(f32), axis=0).astype(bf16)
     half = lax.all_to_all(
         jnp.broadcast_to(mine[None], parts.shape),
@@ -545,17 +604,6 @@
     grad_freq = jnp.where(
         core[0] == 0, jnp.stack([half, rest], axis=1), jnp.stack([rest, half], axis=1)
     ).reshape(freq_rows, emb)
-
-    (grad_inf,) = local_call(
-        functools.partial(owner_kernel, devices, stride, cap),
-        [((owned, emb), bf16)],
-        [SMEM, VMEM],
-        [pltpu.VMEM((n_req, emb), f32)] + [pltpu.VMEM((owned + 8, emb), f32)] * 4,
-        "owner_grads",
-        32,
-        0,
-        60 * MIB,
-    )(asked, arrived.reshape(devices, micro * cap, emb))
 
     return (grad_u, grad_v, grad_b, grad_w, grad_freq, grad_inf)
 

time: 366 us -> 348 us (0.951)
  blocking collectives: 33.2 us -> 0 us
  starting transfers between devices: 46.9 us -> 74.3 us
  waiting for transfers between devices: 73.8 us -> 59.2 us
    all_to_all x1 -> x0, blocking collectives: 33.2 us -> none  [on_device(): lax.all_to_all(both, 'dev', split_axis=0, concat_axis=0, axis_index_group...]
    reduce_scatter x3, waiting for transfers between devices: 55.1 us -> 22.3 us  [on_device(): dense = lax.psum_scatter(dense, 'dev', axis_index_groups=groups, tiled=True)]
    all_to_all x1, waiting for transfers between devices: 0.01 us -> 25.8 us  [on_device(): lax.all_to_all(jnp.broadcast_to(mine[None], parts.shape), 'dev', split_ax...]
    all_to_all x3 -> x4, waiting for transfers between devices: 14.7 us -> 0.01 us  [exchange(): lax.all_to_all(rows.reshape(devices, count, emb), 'dev', split_axis=0, co...]
    all_to_all x3 -> x4, starting transfers between devices: 25.7 us -> 39.9 us  [exchange(): lax.all_to_all(rows.reshape(devices, count, emb), 'dev', split_axis=0, co...]
    all_to_all x0 -> x1, starting transfers between devices: none -> 10 us  [on_device(): lax.all_to_all(both, 'dev', split_axis=0, concat_axis=0, axis_index_group...]
    all_to_all x0 -> x1, waiting for transfers between devices: none -> 6.39 us  [on_device(): lax.all_to_all(both, 'dev', split_axis=0, concat_axis=0, axis_index_group...]
    ppermute x1, starting transfers between devices: 0.33 us -> 4.02 us  [on_device(): rest = lax.ppermute(half, 'dev', other_core)]
  transfers between devices with their start and end apart: 10 -> 12, of which waited for: 5 -> 5; matrix products, arithmetic and copies ran while one was open for 4% -> 5% of each run, Pallas kernels for 32% -> 43%
where the time goes in v4:
time: 348 us; the launch traced here: 346 us
  Pallas kernels  174 us (50%)
  starting transfers between devices  74.3 us (21%)
  waiting for transfers between devices  59.2 us (17%)
  between operations  14.6 us (4%)
  other arithmetic  14.5 us (4%)
  local copies, waits for them, and re-layouts  8.89 us (3%)
    pallas_call x3, Pallas kernels, on_device(): local_call(functools.partial(micro_kernel, devices, cap, features, m, m *...  57.7 us
    all_to_all x4, starting transfers between devices, exchange(): lax.all_to_all(rows.reshape(devices, count, emb), 'dev', split_axis=0, co...  39.9 us
    pallas_call x1, Pallas kernels, on_device(): local_call(functools.partial(freq_grad_kernel, features), [((devices // 2...  34.7 us
    pallas_call x3, Pallas kernels, freq_rows_of(): local_call(functools.partial(freq_kernel, features, samples, first_micro)...  32.5 us
    all_to_all x1, waiting for transfers between devices, on_device(): lax.all_to_all(jnp.broadcast_to(mine[None], parts.shape), 'dev', split_ax...  25.8 us
    reduce_scatter x3, waiting for transfers between devices, on_device(): dense = lax.psum_scatter(dense, 'dev', axis_index_groups=groups, tiled=True)  22.3 us
    pallas_call x1, Pallas kernels, on_device(): local_call(functools.partial(owner_kernel, devices, stride, cap), [((owne...  21 us
    pallas_call x2, Pallas kernels, lookup(): local_call(functools.partial(lookup_kernel, devices, stride, start, count...  17.5 us
  transfers between devices with their start and end apart: 12, of which 5 were waited for; matrix products, arithmetic and copies ran while one was open for 5% of the time, Pallas kernels for 43%

profile of v4, /device:TPU:1, one launch (start us, length us, event | category | flops | bytes accessed | tf_op | source)
XLA Modules:
  0.0 345.5 jit_solution(17077037669393159293)
XLA Ops:
  7.2 0.8 bitcast_select_fusion
  8.0 0.7 copy.44
  8.7 11.5 %all-to-all-start = ((s32[128,1,128]{2,1,0:T(1,128)}), s32[128,1,128]{2,1,0:T(1,128)S(1)}, u32[]{:S(2)}, u32[]{:S(2)}) async-start(s32[128,1,128]{2,1,0:T(1,128)} %copy.44), calls=%async_computation | async-start | bytes 131072 | tf_op jit(solution)/shard_map/all_to_all | solution.py:401
  20.3 1.6 reshape.103.ids
  21.8 10.9 %freq_rows0.1.freq_part_hbm = f32[3328,128]{1,0:T(8,128)} custom-call(s32[19968]{0:T(1024)} %reshape.103.ids, bf16[16384,128]{1,0:T(8,128)(2,1)} %table_ref.9), custom_call_target="tpu_custom_call" | custom-call | bytes 27262976 | tf_op jit(solution)/shard_map/freq_rows0/pallas_call | solution.py:404
  32.7 0.6 broadcast_minimum_fusion.asked
  33.3 7.0 %lookup0.1 = bf16[4096,128]{1,0:T(8,128)(2,1)} custom-call(s32[16384]{0:T(1024)} %broadcast_minimum_fusion.asked, bf16[4096,128]{1,0:T(8,128)(2,1)} %table_ref.7), custom_call_target="tpu_custom_call" | custom-call | bytes 20971520 | tf_op jit(solution)/shard_map/lookup0/pallas_call | solution.py:431
  40.3 9.8 %all-to-all-start.1 = ((bf16[128,32,128]{2,1,0:T(8,128)(2,1)}), bf16[128,32,128]{2,1,0:T(8,128)(2,1)S(1)}, u32[]{:S(2)}, u32[]{:S(2)}) async-start(bf16[128,32,128]{2,1,0:T(8,128)(2,1)} %bitcast.110), calls=%async_computation.1 | async-start | bytes 2097152 | tf_op jit(solution)/shard_map/all_to_all | solution.py:424
  50.1 0.6 reshape.111.bias
  50.7 0.6 reshape.124.weight
  51.3 0.6 convert_element_type.23.labels
  51.9 0.7 fusion.2
  52.6 10.5 %lookup32.1 = bf16[8192,128]{1,0:T(8,128)(2,1)} custom-call(s32[16384]{0:T(1024)} %broadcast_minimum_fusion.asked, bf16[4096,128]{1,0:T(8,128)(2,1)} %table_ref.7), custom_call_target="tpu_custom_call" | custom-call | bytes 41943040 | tf_op jit(solution)/shard_map/lookup32/pallas_call | solution.py:431
  63.1 10.8 %freq_rows1.1.freq_part_hbm = f32[3328,128]{1,0:T(8,128)} custom-call(s32[19968]{0:T(1024)} %reshape.103.ids, bf16[16384,128]{1,0:T(8,128)(2,1)} %table_ref.9), custom_call_target="tpu_custom_call" | custom-call | bytes 27262976 | tf_op jit(solution)/shard_map/freq_rows1/pallas_call | solution.py:404
  74.0 1.0 copy-done
  74.9 10.2 %all-to-all-start.2 = ((bf16[128,64,128]{2,1,0:T(8,128)(2,1)}), bf16[128,64,128]{2,1,0:T(8,128)(2,1)}, u32[]{:S(2)}, u32[]{:S(2)}) async-start(bf16[128,64,128]{2,1,0:T(8,128)(2,1)} %bitcast.107), calls=%async_computation.2 | async-start | bytes 4194304 | tf_op jit(solution)/shard_map/all_to_all | solution.py:424
  85.8 10.8 %freq_rows2.1.freq_part_hbm = f32[3328,128]{1,0:T(8,128)} custom-call(s32[19968]{0:T(1024)} %reshape.103.ids, bf16[16384,128]{1,0:T(8,128)(2,1)} %table_ref.9), custom_call_target="tpu_custom_call" | custom-call | bytes 27262976 | tf_op jit(solution)/shard_map/freq_rows2/pallas_call | solution.py:404
  96.7 19.2 %micro0.1 = (bf16[128,64,128]{2,1,0:T(8,128)(2,1)}, f32[3328,128]{1,0:T(8,128)}, bf16[128,3456]{1,0:T(8,128)(2,1)}, bf16[128,512]{1,0:T(8,128)(2,1)}, bf16[128,5...) custom-call(s32[12288]{0:T(1024)} %bitcast.111, f32[1]{0:T(128)} %bitcast.101.out_b, ...), custom_call_target="tpu_custom_call" | custom-call | flops 1358954496 | bytes 62914560 | tf_op jit(solution)/shard_map/micro0/pallas_call | solution.py:461
  115.9 19.3 %micro1.1 = (bf16[128,64,128]{2,1,0:T(8,128)(2,1)}, f32[3328,128]{1,0:T(8,128)}, bf16[128,3456]{1,0:T(8,128)(2,1)}, bf16[128,512]{1,0:T(8,128)(2,1)}, bf16[128,5...) custom-call(s32[12288]{0:T(1024)} %bitcast.112, ...), custom_call_target="tpu_custom_call", output_to_operand_aliasing={{0}: (10, {})} | custom-call | flops 1358954496 | bytes 62914560 | tf_op jit(solution)/shard_map/micro1/pallas_call | solution.py:461
  135.2 10.2 %all-to-all-start.3 = ((bf16[128,64,128]{2,1,0:T(8,128)(2,1)}), bf16[128,64,128]{2,1,0:T(8,128)(2,1)}, u32[]{:S(2)}, u32[]{:S(2)}) async-start(bf16[128,64,128]{2,1,0:T(8,128)(2,1)} %get-tuple-element.97), calls=%async_computation.3 | async-start | bytes 4194304 | tf_op jit(solution)/shard_map/all_to_all | solution.py:424
  145.4 0.3 reduce-scatter.4.cloned.1.call-start
  145.7 19.2 %micro2.1 = (bf16[128,32,128]{2,1,0:T(8,128)(2,1)}, f32[3328,128]{1,0:T(8,128)}, bf16[128,3456]{1,0:T(8,128)(2,1)}, bf16[128,512]{1,0:T(8,128)(2,1)}, bf16[128,5...) custom-call(s32[12288]{0:T(1024)} %bitcast.113, f32[1]{0:T(128)} %bitcast.103.out_b, ...), custom_call_target="tpu_custom_call" | custom-call | flops 1358954496 | bytes 62914560 | tf_op jit(solution)/shard_map/micro2/pallas_call | solution.py:461
  165.0 0.8 add_add_fusion
  165.7 0.2 reshape.117
  165.9 0.1 copy.52
  166.1 1.1 pad.9.columns
  167.1 10.3 %dense_grads.1 = bf16[8,16,32,1024]{3,2,1,0:T(8,128)(2,1)} custom-call(f32[128,16,128]{2,1,0:T(8,128)} %pad.9.columns, bf16[128,3456]{1,0:T(8,128)(2,1)} %get-tuple-element.84.x0, bf16[128,3456]{1,0:T(8,128)(2,1)} %get-tuple-element.85.x1, bf16[128,3456]{1,0:T(8,128)(2,1)} %get-tuple-element.86.x2, bf16[128,3456]{1,0:T(8,128)(2,1)} %get-tuple-element.87.g0, ...), custom_call_target="tpu_custom_call" | custom-call | flops 2717908992 | bytes 41943040 | tf_op jit(solution)/shard_map/dense_grads/pallas_call | solution.py:524
  177.5 9.8 %all-to-all-start.4 = ((bf16[128,32,128]{2,1,0:T(8,128)(2,1)}), bf16[128,32,128]{2,1,0:T(8,128)(2,1)S(1)}, u32[]{:S(2)}, u32[]{:S(2)}) async-start(bf16[128,32,128]{2,1,0:T(8,128)(2,1)} %get-tuple-element.106), calls=%async_computation.7 | async-start | bytes 2097152 | tf_op jit(solution)/shard_map/all_to_all | solution.py:424
  187.2 34.7 %freq_grads.1 = (bf16[64,128,128]{2,1,0:T(8,128)(2,1)}, bf16[64,128,128]{2,1,0:T(8,128)(2,1)}) custom-call(s32[1]{0:T(128)} %bitcast.core, s32[19968]{0:T(1024)} %reshape.103.ids, f32[3328,128]{1,0:T(8,128)} %get-tuple-element.101.d0, f32[3328,128]{1,0:T(8,128)} %get-tuple-element.102.d1, f32[3328,128]{1,0:T(8,128)} %get-tuple-element.103.d2), custom_call_target="tpu_custom_call" | custom-call | bytes 125829120 | tf_op jit(solution)/shard_map/freq_grads/pallas_call | solution.py:560
  222.0 1.4 collective-permute-start
  223.4 4.0 %collective-permute-done = bf16[64,128,128]{2,1,0:T(8,128)(2,1)S(1)} collective-permute-done((bf16[64,128,128]{2,1,0:T(8,128)(2,1)}, bf16[64,128,128]{2,1,0:T(8,128)(2,1)S(1)}, u32[]{:S(2)}, u32[]{:S(2)}) %collective-permute-start) | collective-permute-done | bytes 2097184 | tf_op jit(solution)/shard_map/ppermute | solution.py:573
  227.4 3.8 %add_convert_fusion = bf16[64,128,128]{2,1,0:T(8,128)(2,1)} fusion(bf16[64,128,128]{2,1,0:T(8,128)(2,1)S(1)} %collective-permute-done, bf16[64,128,128]{2,1,0:T(8,128)(2,1)} %get-tuple-element.104), kind=kLoop, calls=%fused_computation.1 | loop fusion | flops 4194304 | bytes 6291456 | tf_op jit(solution)/shard_map/convert_element_type | solution.py:574
  231.2 10.0 %all-to-all-start.5 = ((bf16[64,128,128]{2,1,0:T(8,128)(2,1)}), bf16[64,128,128]{2,1,0:T(8,128)(2,1)}, u32[]{:S(2)}, u32[]{:S(2)}) async-start(bf16[64,128,128]{2,1,0:T(8,128)(2,1)} %add_convert_fusion), calls=%async_computation.8 | async-start | bytes 4194304 | tf_op jit(solution)/shard_map/all_to_all | solution.py:575
  241.2 21.0 %owner_grads.1 = bf16[4096,128]{1,0:T(8,128)(2,1)} custom-call(s32[16384]{0:T(1024)S(1)} %bitcast.105, bf16[128,64,128]{2,1,0:T(8,128)(2,1)} %bitcast.36.first, bf16[128,32,128]{2,1,0:T(8,128)(2,1)S(1)} %all-to-all-done.4), custom_call_target="tpu_custom_call" | custom-call | bytes 62914560 | tf_op jit(solution)/shard_map/owner_grads/pallas_call | solution.py:578
  262.3 6.4 %all-to-all-done.5 = bf16[64,128,128]{2,1,0:T(8,128)(2,1)} async-done(((bf16[64,128,128]{2,1,0:T(8,128)(2,1)}), bf16[64,128,128]{2,1,0:T(8,128)(2,1)}, u32[]{:S(2)}, u32[]{:S(2)}) %all-to-all-start.5) | async-done | bytes 2097184 | tf_op jit(solution)/shard_map/all_to_all | solution.py:575
  268.7 1.9 reduce_sum.12
  270.6 1.8 broadcast_in_dim.6
  272.4 7.1 %all-to-all-start.6 = ((bf16[64,128,128]{2,1,0:T(8,128)(2,1)}), bf16[64,128,128]{2,1,0:T(8,128)(2,1)S(1)}, u32[]{:S(2)}, u32[]{:S(2)}) async-start(bf16[64,128,128]{2,1,0:T(8,128)(2,1)} %broadcast_in_dim.6), calls=%async_computation.9 | async-start | bytes 4194304 | tf_op jit(solution)/shard_map/all_to_all | solution.py:595
  279.5 0.0 reduce-scatter.6.cloned.1.call-start
  279.6 0.7 reduce-scatter.6.cloned.1.call-update
  280.3 25.8 %all-to-all-done.6 = bf16[64,128,128]{2,1,0:T(8,128)(2,1)S(1)} async-done(((bf16[64,128,128]{2,1,0:T(8,128)(2,1)}), bf16[64,128,128]{2,1,0:T(8,128)(2,1)S(1)}, u32[]{:S(2)}, u32[]{:S(2)}) %all-to-all-start.6) | async-done | bytes 2097184 | tf_op jit(solution)/shard_map/all_to_all | solution.py:595
  306.1 4.0 %collective-permute-start.1 = (bf16[64,128,128]{2,1,0:T(8,128)(2,1)S(1)}, bf16[64,128,128]{2,1,0:T(8,128)(2,1)}, u32[]{:S(2)}, u32[]{:S(2)}) collective-permute-start(bf16[64,128,128]{2,1,0:T(8,128)(2,1)S(1)} %all-to-all-done.6), channel_id=1, source_target_pairs={{0,1},{1,0},{2,3},{3,2},{4,5},{5,4},{6,7},{7,6},{8,9},{9,8},{10,11... | collective-permute-start | bytes 6291464 | tf_op jit(solution)/shard_map/ppermute | solution.py:603
  310.1 5.2 %reduce-scatter.6.cloned.1.call-done = bf16[4,32,1024]{2,1,0:T(8,128)(2,1)} async-done(((bf16[16,32,1024]{2,1,0:T(8,128)(2,1)}), bf16[4,32,1024]{2,1,0:T(8,128)(2,1)}) %reduce-scatter.6.cloned.1.call-update) | async-done | bytes 262160 | tf_op jit(solution)/shard_map/reduce_scatter | solution.py:553
  315.4 4.5 %maximum_select_fusion = bf16[64,2,128,128]{3,2,1,0:T(8,128)(2,1)} fusion(bf16[64,1,128,128]{3,2,1,0:T(8,128)(2,1)} %bitcast.39, bf16[64,1,128,128]{3,2,1,0:T(8,128)(2,1)S(1)} %bitcast.108, pred[]{:T(512)} %bitcast.34), kind=kLoop, calls=%fused_computation | loop fusion | flops 6291456 | bytes 8388609 | tf_op jit(solution)/shard_map/jit(_where)/select_n | solution.py:604
  319.9 17.1 %reduce-scatter.8.cloned.1.call-done = bf16[1,32,1024]{2,1,0:T(8,128)(2,1)} async-done(((bf16[4,32,1024]{2,1,0:T(8,128)(2,1)}), bf16[1,32,1024]{2,1,0:T(8,128)(2,1)}) %reduce-scatter.8.cloned.1.call-update) | async-done | bytes 65552 | tf_op jit(solution)/shard_map/reduce_scatter | solution.py:553
  336.9 0.8 bitcast_convert_fusion
  337.8 0.7 slice_bitcast_fusion
  338.5 0.5 slice_bitcast_fusion.1
  (26 shorter events, 0.1 us)
Async XLA Ops:
  8.7 23.9 %all-to-all-start = ((s32[128,1,128]{2,1,0:T(1,128)}), s32[128,1,128]{2,1,0:T(1,128)S(1)}, u32[]{:S(2)}, u32[]{:S(2)}) async-start(s32[128,1,128]{2,1,0:T(1,128)} %copy.44), calls=%async_computation | async-start | bytes 131072 | tf_op jit(solution)/shard_map/all_to_all | solution.py:401
  33.3 16.8 %copy-start.5 = (f32[3456]{0:T(1024)S(1)}, f32[3456]{0:T(1024)}, u32[]{:S(2)}) copy-start(f32[3456]{0:T(1024)} %param.21) | copy-start | bytes 41476
  33.3 17.4 %copy-start.6 = (bf16[3456]{0:T(1024)(128)(2,1)S(1)}, bf16[3456]{0:T(1024)(128)(2,1)}, u32[]{:S(2)}) copy-start(bf16[3456]{0:T(1024)(128)(2,1)} %param.22) | copy-start | bytes 20740
  33.3 18.0 %copy-start.7 = (s32[3,128]{1,0:T(4,128)S(1)}, s32[3,128]{1,0:T(4,128)}, u32[]{:S(2)}) copy-start(s32[3,128]{1,0:T(4,128)} %param.13) | copy-start | bytes 4612
  33.3 18.6 %copy-start.1 = (s32[3,1,128,32]{2,3,1,0:T(8,128)S(1)}, s32[3,1,128,32]{2,3,1,0:T(8,128)}, u32[]{:S(2)}) copy-start(s32[3,1,128,32]{2,3,1,0:T(8,128)} %param.16) | copy-start | bytes 147460
  33.3 18.6 %copy-start.2 = (s32[3,1,128,32]{2,3,1,0:T(8,128)S(1)}, s32[3,1,128,32]{2,3,1,0:T(8,128)}, u32[]{:S(2)}) copy-start(s32[3,1,128,32]{2,3,1,0:T(8,128)} %param.15) | copy-start | bytes 147460
  40.3 33.7 %all-to-all-start.1 = ((bf16[128,32,128]{2,1,0:T(8,128)(2,1)}), bf16[128,32,128]{2,1,0:T(8,128)(2,1)S(1)}, u32[]{:S(2)}, u32[]{:S(2)}) async-start(bf16[128,32,128]{2,1,0:T(8,128)(2,1)} %bitcast.110), calls=%async_computation.1 | async-start | bytes 2097152 | tf_op jit(solution)/shard_map/all_to_all | solution.py:424
  74.0 1.0 copy-start
  74.9 40.9 %all-to-all-start.2 = ((bf16[128,64,128]{2,1,0:T(8,128)(2,1)}), bf16[128,64,128]{2,1,0:T(8,128)(2,1)}, u32[]{:S(2)}, u32[]{:S(2)}) async-start(bf16[128,64,128]{2,1,0:T(8,128)(2,1)} %bitcast.107), calls=%async_computation.2 | async-start | bytes 4194304 | tf_op jit(solution)/shard_map/all_to_all | solution.py:424
  135.2 42.2 %all-to-all-start.3 = ((bf16[128,64,128]{2,1,0:T(8,128)(2,1)}), bf16[128,64,128]{2,1,0:T(8,128)(2,1)}, u32[]{:S(2)}, u32[]{:S(2)}) async-start(bf16[128,64,128]{2,1,0:T(8,128)(2,1)} %get-tuple-element.97), calls=%async_computation.3 | async-start | bytes 4194304 | tf_op jit(solution)/shard_map/all_to_all | solution.py:424
  145.4 134.1 %reduce-scatter.4.cloned.1.call-start = ((), (), s32[]{:S(2)}) async-start(), calls=%async_computation.10 | async-start | bytes 9437184 | tf_op jit(solution)/shard_map/reduce_scatter | solution.py:553
  145.7 19.2 %copy-start.3 = (f32[2,3456]{1,0:T(2,128)S(1)}, f32[2,3456]{1,0:T(2,128)}, u32[]{:S(2)}) copy-start(f32[2,3456]{1,0:T(2,128)} %get-tuple-element.75) | copy-start | bytes 82948
  145.7 19.2 %copy-start.4 = (f32[2,3456]{1,0:T(2,128)S(1)}, f32[2,3456]{1,0:T(2,128)}, u32[]{:S(2)}) copy-start(f32[2,3456]{1,0:T(2,128)} %get-tuple-element.80) | copy-start | bytes 82948
  177.5 44.5 %all-to-all-start.4 = ((bf16[128,32,128]{2,1,0:T(8,128)(2,1)}), bf16[128,32,128]{2,1,0:T(8,128)(2,1)S(1)}, u32[]{:S(2)}, u32[]{:S(2)}) async-start(bf16[128,32,128]{2,1,0:T(8,128)(2,1)} %get-tuple-element.106), calls=%async_computation.7 | async-start | bytes 2097152 | tf_op jit(solution)/shard_map/all_to_all | solution.py:424
  222.0 5.4 %collective-permute-start = (bf16[64,128,128]{2,1,0:T(8,128)(2,1)}, bf16[64,128,128]{2,1,0:T(8,128)(2,1)S(1)}, u32[]{:S(2)}, u32[]{:S(2)}) collective-permute-start(bf16[64,128,128]{2,1,0:T(8,128)(2,1)} %get-tuple-element.107), channel_id=1, source_target_pairs={{0,1},{1,0},{2,3},{3,2},{4,5},{5,4},{6,7},{7,6},{8,9},{9,8},{10,11... | collective-permute-start | bytes 6291464 | tf_op jit(solution)/shard_map/ppermute | solution.py:573
  231.2 37.5 %all-to-all-start.5 = ((bf16[64,128,128]{2,1,0:T(8,128)(2,1)}), bf16[64,128,128]{2,1,0:T(8,128)(2,1)}, u32[]{:S(2)}, u32[]{:S(2)}) async-start(bf16[64,128,128]{2,1,0:T(8,128)(2,1)} %add_convert_fusion), calls=%async_computation.8 | async-start | bytes 4194304 | tf_op jit(solution)/shard_map/all_to_all | solution.py:575
  272.4 33.7 %all-to-all-start.6 = ((bf16[64,128,128]{2,1,0:T(8,128)(2,1)}), bf16[64,128,128]{2,1,0:T(8,128)(2,1)S(1)}, u32[]{:S(2)}, u32[]{:S(2)}) async-start(bf16[64,128,128]{2,1,0:T(8,128)(2,1)} %broadcast_in_dim.6), calls=%async_computation.9 | async-start | bytes 4194304 | tf_op jit(solution)/shard_map/all_to_all | solution.py:595
  279.5 35.9 %reduce-scatter.6.cloned.1.call-start = ((), (), s32[]{:S(2)}) async-start(), calls=%async_computation.11 | async-start | bytes 1310720 | tf_op jit(solution)/shard_map/reduce_scatter | solution.py:553
  280.2 56.7 %reduce-scatter.8.cloned.1.call-start = ((), (), s32[]{:S(2)}) async-start(), calls=%async_computation.12 | async-start | bytes 327680 | tf_op jit(solution)/shard_map/reduce_scatter | solution.py:553
  306.1 9.3 %collective-permute-start.1 = (bf16[64,128,128]{2,1,0:T(8,128)(2,1)S(1)}, bf16[64,128,128]{2,1,0:T(8,128)(2,1)}, u32[]{:S(2)}, u32[]{:S(2)}) collective-permute-start(bf16[64,128,128]{2,1,0:T(8,128)(2,1)S(1)} %all-to-all-done.6), channel_id=1, source_target_pairs={{0,1},{1,0},{2,3},{3,2},{4,5},{5,4},{6,7},{7,6},{8,9},{9,8},{10,11... | collective-permute-start | bytes 6291464 | tf_op jit(solution)/shard_map/ppermute | solution.py:603
Sparse Core Ops, SparseCore 0:
  177.6 64.1 reduce-scatter.3
  282.7 32.5 reduce-scatter.5
  317.9 19.0 reduce-scatter.7

commit v5 on v4

--- a/solution.py
+++ b/solution.py
@@ -17,6 +17,12 @@
 HBM = pl.BlockSpec(memory_space=pltpu.HBM)
 NT = (((1,), (1,)), ((), ()))
 TN = (((0,), (0,)), ((), ()))
+
+
+def tree_sum(terms):
+    while len(terms) > 1:
+        terms = [sum(terms[k : k + 2][1:], terms[k]) for k in range(0, len(terms), 2)]
+    return terms[0]
 
 
 def local_call(
@@ -103,10 +109,7 @@
         gate_low_hbm,
         grad_bw,
         arrived,
-        acc0,
-        acc1,
-        acc2,
-        acc3,
+        *accs,
         gate,
         returned,
         x_zero,
@@ -116,11 +119,12 @@
         cross_u,
         cross_v,
         sems,
-    ) = refs[-21:]
+    ) = refs[-25:]
+    acc0 = accs[0]
     samples, width = x_zero.shape
     emb = bottom.shape[2]
     n_slots = features * samples
-    accs = (acc0, acc1, acc2, acc3)
+    ways = len(accs)
     loads = [
         pltpu.make_async_copy(
             fetched_hbm.at[:, pl.ds(fetch_start, cap), :], returned, sems.at[6]
@@ -139,13 +143,13 @@
     loads[1].wait()
 
     def add_peer(o, carry):
-        for c in range(0, cap, 4):
-            at = [slots[slot_start + (c + j) * peers + o] for j in range(4)]
+        for c in range(0, cap, ways):
+            at = [slots[slot_start + (c + j) * peers + o] for j in range(ways)]
             new = [
                 accs[j][pl.ds(at[j], 1), :] + arrived[pl.ds(o * cap + c + j, 1), :]
-                for j in range(4)
+                for j in range(ways)
             ]
-            for j in range(4):
+            for j in range(ways):
                 accs[j][pl.ds(at[j], 1), :] = new[j]
         return carry
 
@@ -154,7 +158,7 @@
     x_zero[:, 0:emb] = bottom[m]
     for f in range(features):
         rows = pl.ds(f * samples, samples)
-        total = (acc0[rows, :] + acc1[rows, :]) + (acc2[rows, :] + acc3[rows, :])
+        total = tree_sum([a[rows, :] for a in accs])
         x_zero[:, (f + 1) * emb : (f + 2) * emb] = total.astype(bf16)
 
     loads[2].wait()
@@ -281,9 +285,10 @@
 
 
 def freq_grad_kernel(
-    features, core, ids, d0, d1, d2, keep, send, acc0, acc1, acc2, acc3, buf0, buf1, buf2, sems
+    features, core, ids, d0, d1, d2, keep, send, *scratch
 ):
-    accs = (acc0, acc1, acc2, acc3)
+    *accs, buf0, buf1, buf2, sems = scratch
+    pairs = len(accs) // 2
     samples = d0.shape[0] // features
     loads = [
         pltpu.make_async_copy(d, buf, sems.at[k])
@@ -293,27 +298,23 @@
         load.start()
     for a in accs:
         a[...] = jnp.zeros_like(a)
-    unroll = 64
     for m, source in enumerate((buf0, buf1, buf2)):
         loads[m].wait()
         start = m * features * 2 * samples
 
         def feature(f, carry):
-            def some(k, carry):
-                for u in range(0, unroll, 2):
-                    s = k * unroll + u
-                    at = [
-                        ids[start + (2 * f + h) * samples + s + j]
-                        for j in range(2)
-                        for h in range(2)
-                    ]
-                    value = [source[pl.ds(f * samples + s + j, 1), :] for j in range(2)]
-                    new = [accs[j][pl.ds(at[j], 1), :] + value[j // 2] for j in range(4)]
-                    for j in range(4):
-                        accs[j][pl.ds(at[j], 1), :] = new[j]
-                return carry
-
-            return lax.fori_loop(0, samples // unroll, some, carry)
+            base = f * samples
+            first = start + f * 2 * samples
+            for s in range(0, samples, pairs):
+                count = min(pairs, samples - s)
+                at = [
+                    ids[first + h * samples + s + j] for j in range(count) for h in range(2)
+                ]
+                value = [source[pl.ds(base + s + j, 1), :] for j in range(count)]
+                new = [accs[j][pl.ds(at[j], 1), :] + value[j // 2] for j in range(2 * count)]
+                for j in range(2 * count):
+                    accs[j][pl.ds(at[j], 1), :] = new[j]
+            return carry
 
         lax.fori_loop(0, features, feature, 0)
     rows = 128
@@ -322,15 +323,31 @@
     def block(q, carry):
         for ref, parity in ((keep, mine), (send, 1 - mine)):
             at = pl.ds(pl.multiple_of((2 * q + parity) * rows, rows), rows)
-            total = (acc0[at, :] + acc1[at, :]) + (acc2[at, :] + acc3[at, :])
-            ref[q] = total.astype(bf16)
+            ref[q] = tree_sum([a[at, :] for a in accs]).astype(bf16)
         return carry
 
     lax.fori_loop(0, keep.shape[0], block, 0)
 
 
-def owner_kernel(peers, stride, cap, asked, first, last, out, rows, acc0, acc1, acc2, acc3):
-    accs = (acc0, acc1, acc2, acc3)
+def spread_kernel(parts, out):
+    total = parts[0].astype(f32)
+    for k in range(1, parts.shape[0]):
+        total = total + parts[k].astype(f32)
+    total = total.astype(bf16)
+    for k in range(parts.shape[0]):
+        out[k] = total
+
+
+def place_kernel(other, core, half, *refs):
+    out, sem = refs[-2:]
+    at = core[0] if other == 0 else 1 - core[0]
+    copy = pltpu.make_async_copy(half, out.at[:, at], sem)
+    copy.start()
+    copy.wait()
+
+
+def owner_kernel(peers, stride, cap, asked, first, last, out, rows, *accs):
+    ways = len(accs)
     for a in accs:
         a[...] = jnp.zeros_like(a)
     emb = out.shape[1]
@@ -339,19 +356,19 @@
         rows[...] = part.astype(f32).reshape(peers * cap, emb)
 
         def peer(d, carry):
-            for c in range(0, cap, 4):
-                at = [asked[d * stride + m * cap + c + j] for j in range(4)]
+            for c in range(0, cap, ways):
+                at = [asked[d * stride + m * cap + c + j] for j in range(ways)]
                 new = [
                     accs[j][pl.ds(at[j], 1), :] + rows[pl.ds(d * cap + c + j, 1), :]
-                    for j in range(4)
+                    for j in range(ways)
                 ]
-                for j in range(4):
+                for j in range(ways):
                     accs[j][pl.ds(at[j], 1), :] = new[j]
             return carry
 
         lax.fori_loop(0, peers, peer, 0)
     at = slice(0, out.shape[0])
-    out[...] = ((acc0[at, :] + acc1[at, :]) + (acc2[at, :] + acc3[at, :])).astype(bf16)
+    out[...] = tree_sum([a[at, :] for a in accs]).astype(bf16)
 
 
 def on_device(
@@ -419,6 +436,15 @@
     bias = cross_bias.reshape(1, width)
     label_rows = labels.astype(f32)
     bias_b = out_b.reshape(1)
+
+    def axis_sum(blocks, step):
+        at = me // step % 4
+        total = lax.dynamic_index_in_dim(blocks, at, 0, keepdims=False).astype(f32)
+        for k in range(1, 4):
+            block = lax.dynamic_index_in_dim(blocks, (at + k) % 4, 0, keepdims=False)
+            to = [(d, d + ((d // step % 4 + k) % 4 - d // step % 4) * step) for d in range(devices)]
+            total = total + lax.ppermute(block, "dev", to).astype(f32)
+        return total
 
     def exchange(rows, count):
         return lax.all_to_all(
@@ -481,7 +507,7 @@
             ],
             [SMEM, SMEM, HBM, HBM, VMEM, VMEM, HBM, HBM, VMEM, VMEM] + ([HBM] if m == 1 else []),
             [pltpu.VMEM((n_req, emb), f32)]
-            + [pltpu.VMEM((n_slots + 8, emb), f32)] * 4
+            + [pltpu.VMEM((n_slots + 8, emb), f32)] * 8
             + [pltpu.VMEM((samples, width), f32)]
             + [pltpu.VMEM((devices, cap, emb), bf16), pltpu.VMEM((samples, width), bf16)]
             + [pltpu.VMEM((samples, rank), bf16)] * 2
@@ -544,24 +570,15 @@
     )
     core, dense, arrived_first = lax.optimization_barrier((core, dense, arrived_first))
     dense = dense.reshape(devices, rows_pad, 2 * rank)
-    for step, size in ((1, 8), (8, 4), (32, 4)):
-        groups = [
-            [d + k * step for k in range(size)]
-            for d in range(devices)
-            if d // step % size == 0
-        ]
-        dense = lax.psum_scatter(dense, "dev", axis_index_groups=groups, tiled=True)
-    dense = dense.reshape(rows_pad, 2 * rank).astype(f32)
-    grad_u = dense[:per, :rank]
-    grad_v = dense[:per, rank:].T
-    grad_b = dense[per, :per]
-    grad_w = dense[per + 1, :per]
-
+    near = [list(range(d, d + 8)) for d in range(0, devices, 8)]
+    dense = lax.psum_scatter(dense, "dev", axis_index_groups=near, tiled=True)
+    dense = axis_sum(dense.reshape(4, 4, rows_pad, 2 * rank), 8).astype(bf16)
+    dense = axis_sum(dense, 32)
     keep_f, send_f = local_call(
         functools.partial(freq_grad_kernel, features),
         [((devices // 2, per_freq, emb), bf16)] * 2,
         [SMEM, SMEM] + [HBM] * 3,
-        [pltpu.VMEM((freq_rows, emb), f32)] * 4
+        [pltpu.VMEM((freq_rows, emb), f32)] * 6
         + [pltpu.VMEM((n_slots, emb), f32)] * 3
         + [pltpu.SemaphoreType.DMA((3,))],
         "freq_grads",
@@ -579,9 +596,9 @@
         functools.partial(owner_kernel, devices, stride, cap),
         [((owned, emb), bf16)],
         [SMEM, VMEM, VMEM],
-        [pltpu.VMEM((n_req, emb), f32)] + [pltpu.VMEM((owned + 8, emb), f32)] * 4,
+        [pltpu.VMEM((n_req, emb), f32)] + [pltpu.VMEM((owned + 8, emb), f32)] * 8,
         "owner_grads",
-        32,
+        62,
         0,
         60 * MIB,
     )(
@@ -591,20 +608,51 @@
     )
 
     parts, grad_inf = lax.optimization_barrier((parts, grad_inf))
-    mine = jnp.sum(parts.astype(f32), axis=0).astype(bf16)
+    (spread,) = local_call(
+        spread_kernel,
+        [(parts.shape, bf16)],
+        [VMEM],
+        [],
+        "spread",
+        62,
+        0,
+        4 * MIB,
+    )(parts)
     half = lax.all_to_all(
-        jnp.broadcast_to(mine[None], parts.shape),
-        "dev",
-        split_axis=0,
-        concat_axis=0,
-        axis_index_groups=same_core,
-        tiled=True,
-    )
+        spread, "dev", split_axis=0, concat_axis=0, axis_index_groups=same_core, tiled=True
+    )
+    half, dense = lax.optimization_barrier((half, dense))
     rest = lax.ppermute(half, "dev", other_core)
-    grad_freq = jnp.where(
-        core[0] == 0, jnp.stack([half, rest], axis=1), jnp.stack([rest, half], axis=1)
-    ).reshape(freq_rows, emb)
-
+    full = (devices // 2, 2, per_freq, emb)
+    (placed,) = local_call(
+        functools.partial(place_kernel, 0),
+        [(full, bf16)],
+        [SMEM, HBM],
+        [pltpu.SemaphoreType.DMA],
+        "place_own",
+        62,
+        0,
+        4 * MIB,
+        [HBM],
+    )(core, half)
+    (placed,) = local_call(
+        functools.partial(place_kernel, 1),
+        [(full, bf16)],
+        [SMEM, HBM, HBM],
+        [pltpu.SemaphoreType.DMA],
+        "place_other",
+        62,
+        0,
+        4 * MIB,
+        [HBM],
+        {2: 0},
+    )(core, rest, placed)
+    grad_freq = placed.reshape(freq_rows, emb)
+
+    grad_u = dense[:per, :rank]
+    grad_v = dense[:per, rank:].T
+    grad_b = dense[per, :per]
+    grad_w = dense[per + 1, :per]
     return (grad_u, grad_v, grad_b, grad_w, grad_freq, grad_inf)
 
 

time: 348 us -> 461 us (1.32)
  Pallas kernels: 174 us -> 292 us
  waiting for transfers between devices: 59.2 us -> 50.5 us
  starting transfers between devices: 74.3 us -> 81.4 us
  other arithmetic: 14.5 us -> 8.47 us
    pallas_call x0 -> x3, Pallas kernels: none -> 133 us  [the longest x1 64.6 us: on_device(): local_call(functools.partial(place_kernel, 1), [(full, bf16)], [SMEM, HBM...]
    ppermute x0 -> x6, waiting for transfers between devices: none -> 35.5 us  [axis_sum(): total = total + lax.ppermute(block, 'dev', to).astype(f32)]
    all_to_all x1, waiting for transfers between devices: 25.8 us -> 0.01 us  [on_device(): lax.all_to_all(spread, 'dev', split_axis=0, concat_axis=0, axis_index_gro...]
    reduce_scatter x3 -> x1, waiting for transfers between devices: 22.3 us -> 0.02 us  [on_device(): dense = lax.psum_scatter(dense, 'dev', axis_index_groups=near, tiled=True)]
    ppermute x0 -> x6, starting transfers between devices: none -> 7.55 us  [axis_sum(): total = total + lax.ppermute(block, 'dev', to).astype(f32)]
    pallas_call x1, Pallas kernels: 34.7 us -> 27.7 us  [on_device(): local_call(functools.partial(freq_grad_kernel, features), [((devices // 2...]
  transfers between devices with their start and end apart: 12 -> 16, of which waited for: 5 -> 9; matrix products, arithmetic and copies ran while one was open for 5% -> 3% of each run, Pallas kernels for 43% -> 44%
where the time goes in v5:
time: 461 us; the launch traced here: 456 us
  Pallas kernels  292 us (63%)
  starting transfers between devices  81.4 us (18%)
  waiting for transfers between devices  50.5 us (11%)
  between operations  15.5 us (3%)
  other arithmetic  8.47 us (2%)
  local copies, waits for them, and re-layouts  8.31 us (2%)
    pallas_call x1, Pallas kernels, on_device(): local_call(functools.partial(place_kernel, 1), [(full, bf16)], [SMEM, HBM...  64.6 us
    pallas_call x1, Pallas kernels, on_device(): local_call(functools.partial(place_kernel, 0), [(full, bf16)], [SMEM, HBM...  64.6 us
    pallas_call x3, Pallas kernels, on_device(): local_call(functools.partial(micro_kernel, devices, cap, features, m, m *...  53.7 us
    all_to_all x4, starting transfers between devices, exchange(): lax.all_to_all(rows.reshape(devices, count, emb), 'dev', split_axis=0, co...  40.1 us
    ppermute x6, waiting for transfers between devices, axis_sum(): total = total + lax.ppermute(block, 'dev', to).astype(f32)  35.5 us
    pallas_call x3, Pallas kernels, freq_rows_of(): local_call(functools.partial(freq_kernel, features, samples, first_micro)...  32.5 us
    pallas_call x1, Pallas kernels, on_device(): local_call(functools.partial(freq_grad_kernel, features), [((devices // 2...  27.7 us
    pallas_call x2, Pallas kernels, lookup(): local_call(functools.partial(lookup_kernel, devices, stride, start, count...  17.5 us
  transfers between devices with their start and end apart: 16, of which 9 were waited for; matrix products, arithmetic and copies ran while one was open for 3% of the time, Pallas kernels for 44%

profile of v5, /device:TPU:1, one launch (start us, length us, event | category | flops | bytes accessed | tf_op | source)
XLA Modules:
  0.0 455.7 jit_solution(11279444037445151704)
XLA Ops:
  7.2 0.8 bitcast_select_fusion
  8.0 0.7 copy.45
  8.7 11.5 %all-to-all-start = ((s32[128,1,128]{2,1,0:T(1,128)}), s32[128,1,128]{2,1,0:T(1,128)S(1)}, u32[]{:S(2)}, u32[]{:S(2)}) async-start(s32[128,1,128]{2,1,0:T(1,128)} %copy.45), calls=%async_computation | async-start | bytes 131072 | tf_op jit(solution)/shard_map/all_to_all | solution.py:418
  20.3 1.6 reshape.102.ids
  21.8 10.8 %freq_rows0.1.freq_part_hbm = f32[3328,128]{1,0:T(8,128)} custom-call(s32[19968]{0:T(1024)} %reshape.102.ids, bf16[16384,128]{1,0:T(8,128)(2,1)} %table_ref.9), custom_call_target="tpu_custom_call" | custom-call | bytes 27262976 | tf_op jit(solution)/shard_map/freq_rows0/pallas_call | solution.py:421
  32.6 0.6 broadcast_minimum_fusion.asked
  33.3 7.0 %lookup0.1 = bf16[4096,128]{1,0:T(8,128)(2,1)} custom-call(s32[16384]{0:T(1024)} %broadcast_minimum_fusion.asked, bf16[4096,128]{1,0:T(8,128)(2,1)} %table_ref.7), custom_call_target="tpu_custom_call" | custom-call | bytes 20971520 | tf_op jit(solution)/shard_map/lookup0/pallas_call | solution.py:457
  40.3 9.8 %all-to-all-start.1 = ((bf16[128,32,128]{2,1,0:T(8,128)(2,1)}), bf16[128,32,128]{2,1,0:T(8,128)(2,1)S(1)}, u32[]{:S(2)}, u32[]{:S(2)}) async-start(bf16[128,32,128]{2,1,0:T(8,128)(2,1)} %bitcast.120), calls=%async_computation.1 | async-start | bytes 2097152 | tf_op jit(solution)/shard_map/all_to_all | solution.py:450
  50.1 0.6 reshape.125.weight
  50.7 0.6 reshape.110.bias
  51.3 0.6 convert_element_type.48.labels
  51.9 0.7 fusion.7
  52.6 10.5 %lookup32.1 = bf16[8192,128]{1,0:T(8,128)(2,1)} custom-call(s32[16384]{0:T(1024)} %broadcast_minimum_fusion.asked, bf16[4096,128]{1,0:T(8,128)(2,1)} %table_ref.7), custom_call_target="tpu_custom_call" | custom-call | bytes 41943040 | tf_op jit(solution)/shard_map/lookup32/pallas_call | solution.py:457
  63.1 10.8 %freq_rows1.1.freq_part_hbm = f32[3328,128]{1,0:T(8,128)} custom-call(s32[19968]{0:T(1024)} %reshape.102.ids, bf16[16384,128]{1,0:T(8,128)(2,1)} %table_ref.9), custom_call_target="tpu_custom_call" | custom-call | bytes 27262976 | tf_op jit(solution)/shard_map/freq_rows1/pallas_call | solution.py:421
  74.0 1.0 copy-done.1
  74.9 10.6 %all-to-all-start.2 = ((bf16[128,64,128]{2,1,0:T(8,128)(2,1)}), bf16[128,64,128]{2,1,0:T(8,128)(2,1)}, u32[]{:S(2)}, u32[]{:S(2)}) async-start(bf16[128,64,128]{2,1,0:T(8,128)(2,1)} %bitcast.119), calls=%async_computation.2 | async-start | bytes 4194304 | tf_op jit(solution)/shard_map/all_to_all | solution.py:450
  86.2 10.8 %freq_rows2.1.freq_part_hbm = f32[3328,128]{1,0:T(8,128)} custom-call(s32[19968]{0:T(1024)} %reshape.102.ids, bf16[16384,128]{1,0:T(8,128)(2,1)} %table_ref.9), custom_call_target="tpu_custom_call" | custom-call | bytes 27262976 | tf_op jit(solution)/shard_map/freq_rows2/pallas_call | solution.py:421
  97.0 17.9 %micro0.1 = (bf16[128,64,128]{2,1,0:T(8,128)(2,1)}, f32[3328,128]{1,0:T(8,128)}, bf16[128,3456]{1,0:T(8,128)(2,1)}, bf16[128,512]{1,0:T(8,128)(2,1)}, bf16[128,5...) custom-call(s32[12288]{0:T(1024)} %bitcast.123, f32[1]{0:T(128)} %bitcast.114.out_b, ...), custom_call_target="tpu_custom_call" | custom-call | flops 1358954496 | bytes 62914560 | tf_op jit(solution)/shard_map/micro0/pallas_call | solution.py:487
  115.5 17.9 %micro1.1 = (bf16[128,64,128]{2,1,0:T(8,128)(2,1)}, f32[3328,128]{1,0:T(8,128)}, bf16[128,3456]{1,0:T(8,128)(2,1)}, bf16[128,512]{1,0:T(8,128)(2,1)}, bf16[128,5...) custom-call(s32[12288]{0:T(1024)} %bitcast.124, ...), custom_call_target="tpu_custom_call", output_to_operand_aliasing={{0}: (10, {})} | custom-call | flops 1358954496 | bytes 62914560 | tf_op jit(solution)/shard_map/micro1/pallas_call | solution.py:487
  133.4 9.7 %all-to-all-start.3 = ((bf16[128,64,128]{2,1,0:T(8,128)(2,1)}), bf16[128,64,128]{2,1,0:T(8,128)(2,1)}, u32[]{:S(2)}, u32[]{:S(2)}) async-start(bf16[128,64,128]{2,1,0:T(8,128)(2,1)} %get-tuple-element.99), calls=%async_computation.3 | async-start | bytes 4194304 | tf_op jit(solution)/shard_map/all_to_all | solution.py:450
  143.4 17.8 %micro2.1 = (bf16[128,32,128]{2,1,0:T(8,128)(2,1)}, f32[3328,128]{1,0:T(8,128)}, bf16[128,3456]{1,0:T(8,128)(2,1)}, bf16[128,512]{1,0:T(8,128)(2,1)}, bf16[128,5...) custom-call(s32[12288]{0:T(1024)} %bitcast.125, f32[1]{0:T(128)} %bitcast.116.out_b, ...), custom_call_target="tpu_custom_call" | custom-call | flops 1358954496 | bytes 62914560 | tf_op jit(solution)/shard_map/micro2/pallas_call | solution.py:487
  161.3 0.8 add_add_fusion
  162.4 1.1 pad.9.columns
  163.4 10.4 %dense_grads.1 = bf16[8,16,32,1024]{3,2,1,0:T(8,128)(2,1)} custom-call(f32[128,16,128]{2,1,0:T(8,128)} %pad.9.columns, bf16[128,3456]{1,0:T(8,128)(2,1)} %get-tuple-element.86.x0, bf16[128,3456]{1,0:T(8,128)(2,1)} %get-tuple-element.87.x1, bf16[128,3456]{1,0:T(8,128)(2,1)} %get-tuple-element.88.x2, bf16[128,3456]{1,0:T(8,128)(2,1)} %get-tuple-element.89.g0, ...), custom_call_target="tpu_custom_call" | custom-call | flops 2717908992 | bytes 41943040 | tf_op jit(solution)/shard_map/dense_grads/pallas_call | solution.py:550
  173.9 10.1 %all-to-all-start.4 = ((bf16[128,32,128]{2,1,0:T(8,128)(2,1)}), bf16[128,32,128]{2,1,0:T(8,128)(2,1)S(1)}, u32[]{:S(2)}, u32[]{:S(2)}) async-start(bf16[128,32,128]{2,1,0:T(8,128)(2,1)} %get-tuple-element.107), calls=%async_computation.4 | async-start | bytes 2097152 | tf_op jit(solution)/shard_map/all_to_all | solution.py:450
  184.0 27.7 %freq_grads.1 = (bf16[64,128,128]{2,1,0:T(8,128)(2,1)}, bf16[64,128,128]{2,1,0:T(8,128)(2,1)}) custom-call(s32[1]{0:T(128)} %bitcast.core, s32[19968]{0:T(1024)} %reshape.102.ids, f32[3328,128]{1,0:T(8,128)} %get-tuple-element.102.d0, f32[3328,128]{1,0:T(8,128)} %get-tuple-element.103.d1, f32[3328,128]{1,0:T(8,128)} %get-tuple-element.104.d2), custom_call_target="tpu_custom_call" | custom-call | bytes 125829120 | tf_op jit(solution)/shard_map/freq_grads/pallas_call | solution.py:577
  211.7 1.0 collective-permute-start
  212.8 4.0 collective-permute-done
  216.8 3.8 add_convert_fusion
  220.6 10.3 %all-to-all-start.5 = ((bf16[64,128,128]{2,1,0:T(8,128)(2,1)}), bf16[64,128,128]{2,1,0:T(8,128)(2,1)}, u32[]{:S(2)}, u32[]{:S(2)}) async-start(bf16[64,128,128]{2,1,0:T(8,128)(2,1)} %add_convert_fusion), calls=%async_computation.5 | async-start | bytes 4194304 | tf_op jit(solution)/shard_map/all_to_all | solution.py:592
  230.9 17.1 %owner_grads.1 = bf16[4096,128]{1,0:T(8,128)(2,1)} custom-call(s32[16384]{0:T(1024)} %bitcast.127, bf16[128,64,128]{2,1,0:T(8,128)(2,1)} %bitcast.29.first, bf16[128,32,128]{2,1,0:T(8,128)(2,1)} %copy-done), custom_call_target="tpu_custom_call" | custom-call | bytes 62914560 | tf_op jit(solution)/shard_map/owner_grads/pallas_call | solution.py:595
  248.0 10.4 %all-to-all-done.5.parts = bf16[64,128,128]{2,1,0:T(8,128)(2,1)} async-done(((bf16[64,128,128]{2,1,0:T(8,128)(2,1)}), bf16[64,128,128]{2,1,0:T(8,128)(2,1)}, u32[]{:S(2)}, u32[]{:S(2)}) %all-to-all-start.5) | async-done | bytes 2097184 | tf_op jit(solution)/shard_map/all_to_all | solution.py:592
  258.4 3.4 spread.1
  261.8 8.0 %all-to-all-start.6 = ((bf16[64,128,128]{2,1,0:T(8,128)(2,1)}), bf16[64,128,128]{2,1,0:T(8,128)(2,1)}, u32[]{:S(2)}, u32[]{:S(2)}) async-start(bf16[64,128,128]{2,1,0:T(8,128)(2,1)} %spread.1), calls=%async_computation.6 | async-start | bytes 4194304 | tf_op jit(solution)/shard_map/all_to_all | solution.py:621
  269.9 1.2 dynamic-slice_bitcast_fusion.2
  271.1 2.2 collective-permute-start.3
  273.9 0.6 collective-permute-start.1
  274.5 24.3 %collective-permute-done.3 = bf16[4,32,1024]{2,1,0:T(8,128)(2,1)S(1)} collective-permute-done((bf16[4,32,1024]{2,1,0:T(8,128)(2,1)S(1)}, bf16[4,32,1024]{2,1,0:T(8,128)(2,1)S(1)}, u32[]{:S(2)}, u32[]{:S(2)}) %collective-permute-start.3) | collective-permute-done | bytes 262176 | tf_op jit(solution)/shard_map/ppermute | solution.py:446
  298.8 1.1 collective-permute-done.2
  299.8 5.9 %collective-permute-done.1 = bf16[4,32,1024]{2,1,0:T(8,128)(2,1)S(1)} collective-permute-done((bf16[4,32,1024]{2,1,0:T(8,128)(2,1)S(1)}, bf16[4,32,1024]{2,1,0:T(8,128)(2,1)S(1)}, u32[]{:S(2)}, u32[]{:S(2)}) %collective-permute-start.1) | collective-permute-done | bytes 262176 | tf_op jit(solution)/shard_map/ppermute | solution.py:446
  305.8 1.1 fusion.2
  306.9 3.3 collective-permute-start.6
  310.3 0.8 collective-permute-start.4
  311.5 3.4 collective-permute-done.5
  315.4 2.5 collective-permute-start.7
  317.9 64.6 %place_own.1.refs_0_ = bf16[64,2,128,128]{3,2,1,0:T(8,128)(2,1)} custom-call(s32[1]{0:T(128)} %bitcast.core, bf16[64,128,128]{2,1,0:T(8,128)(2,1)} %all-to-all-done.6.half), custom_call_target="tpu_custom_call" | custom-call | bytes 4194304 | tf_op jit(solution)/shard_map/place_own/pallas_call | solution.py:627
  383.1 0.7 slice_bitcast_fusion
  383.8 64.6 %place_other.1 = bf16[64,2,128,128]{3,2,1,0:T(8,128)(2,1)} custom-call(s32[1]{0:T(128)} %bitcast.core, bf16[64,128,128]{2,1,0:T(8,128)(2,1)} %collective-permute-done.7.half, bf16[64,2,128,128]{3,2,1,0:T(8,128)(2,1)} %place_own.1.refs_0_), custom_call_target="tpu_custom_call", output_to_operand_aliasing={{}: (2, {})} | custom-call | bytes 4194304 | tf_op jit(solution)/shard_map/place_other/pallas_call | solution.py:638
  (39 shorter events, 3.4 us)
Async XLA Ops:
  8.7 23.9 %all-to-all-start = ((s32[128,1,128]{2,1,0:T(1,128)}), s32[128,1,128]{2,1,0:T(1,128)S(1)}, u32[]{:S(2)}, u32[]{:S(2)}) async-start(s32[128,1,128]{2,1,0:T(1,128)} %copy.45), calls=%async_computation | async-start | bytes 131072 | tf_op jit(solution)/shard_map/all_to_all | solution.py:418
  32.6 7.7 %copy-start.2 = (s32[128,1,128]{2,1,0:T(1,128)}, s32[128,1,128]{2,1,0:T(1,128)S(1)}, u32[]{:S(2)}) copy-start(s32[128,1,128]{2,1,0:T(1,128)S(1)} %all-to-all-done) | copy-start | bytes 196612
  33.3 16.8 %copy-start.8 = (bf16[3456]{0:T(1024)(128)(2,1)S(1)}, bf16[3456]{0:T(1024)(128)(2,1)}, u32[]{:S(2)}) copy-start(bf16[3456]{0:T(1024)(128)(2,1)} %param.22) | copy-start | bytes 20740
  33.3 17.4 %copy-start.7 = (f32[3456]{0:T(1024)S(1)}, f32[3456]{0:T(1024)}, u32[]{:S(2)}) copy-start(f32[3456]{0:T(1024)} %param.21) | copy-start | bytes 41476
  33.3 18.0 %copy-start.9 = (s32[3,128]{1,0:T(4,128)S(1)}, s32[3,128]{1,0:T(4,128)}, u32[]{:S(2)}) copy-start(s32[3,128]{1,0:T(4,128)} %param.13) | copy-start | bytes 4612
  33.3 18.6 %copy-start.3 = (s32[3,1,128,32]{2,3,1,0:T(8,128)S(1)}, s32[3,1,128,32]{2,3,1,0:T(8,128)}, u32[]{:S(2)}) copy-start(s32[3,1,128,32]{2,3,1,0:T(8,128)} %param.16) | copy-start | bytes 147460
  33.3 18.6 %copy-start.4 = (s32[3,1,128,32]{2,3,1,0:T(8,128)S(1)}, s32[3,1,128,32]{2,3,1,0:T(8,128)}, u32[]{:S(2)}) copy-start(s32[3,1,128,32]{2,3,1,0:T(8,128)} %param.15) | copy-start | bytes 147460
  40.3 33.7 %all-to-all-start.1 = ((bf16[128,32,128]{2,1,0:T(8,128)(2,1)}), bf16[128,32,128]{2,1,0:T(8,128)(2,1)S(1)}, u32[]{:S(2)}, u32[]{:S(2)}) async-start(bf16[128,32,128]{2,1,0:T(8,128)(2,1)} %bitcast.120), calls=%async_computation.1 | async-start | bytes 2097152 | tf_op jit(solution)/shard_map/all_to_all | solution.py:450
  74.0 1.0 copy-start.1
  74.9 40.6 %all-to-all-start.2 = ((bf16[128,64,128]{2,1,0:T(8,128)(2,1)}), bf16[128,64,128]{2,1,0:T(8,128)(2,1)}, u32[]{:S(2)}, u32[]{:S(2)}) async-start(bf16[128,64,128]{2,1,0:T(8,128)(2,1)} %bitcast.119), calls=%async_computation.2 | async-start | bytes 4194304 | tf_op jit(solution)/shard_map/all_to_all | solution.py:450
  133.4 40.4 %all-to-all-start.3 = ((bf16[128,64,128]{2,1,0:T(8,128)(2,1)}), bf16[128,64,128]{2,1,0:T(8,128)(2,1)}, u32[]{:S(2)}, u32[]{:S(2)}) async-start(bf16[128,64,128]{2,1,0:T(8,128)(2,1)} %get-tuple-element.99), calls=%async_computation.3 | async-start | bytes 4194304 | tf_op jit(solution)/shard_map/all_to_all | solution.py:450
  143.1 126.8 %reduce-scatter.2.cloned.1.call-start = ((), (), s32[]{:S(2)}) async-start(), calls=%async_computation.8 | async-start | bytes 9437184 | tf_op jit(solution)/shard_map/reduce_scatter | solution.py:574
  143.4 17.9 %copy-start.5 = (f32[2,3456]{1,0:T(2,128)S(1)}, f32[2,3456]{1,0:T(2,128)}, u32[]{:S(2)}) copy-start(f32[2,3456]{1,0:T(2,128)} %get-tuple-element.77) | copy-start | bytes 82948
  143.4 17.9 %copy-start.6 = (f32[2,3456]{1,0:T(2,128)S(1)}, f32[2,3456]{1,0:T(2,128)}, u32[]{:S(2)}) copy-start(f32[2,3456]{1,0:T(2,128)} %get-tuple-element.82) | copy-start | bytes 82948
  173.9 37.9 %all-to-all-start.4 = ((bf16[128,32,128]{2,1,0:T(8,128)(2,1)}), bf16[128,32,128]{2,1,0:T(8,128)(2,1)S(1)}, u32[]{:S(2)}, u32[]{:S(2)}) async-start(bf16[128,32,128]{2,1,0:T(8,128)(2,1)} %get-tuple-element.107), calls=%async_computation.4 | async-start | bytes 2097152 | tf_op jit(solution)/shard_map/all_to_all | solution.py:450
  211.7 8.9 %copy-start = (bf16[128,32,128]{2,1,0:T(8,128)(2,1)}, bf16[128,32,128]{2,1,0:T(8,128)(2,1)S(1)}, u32[]{:S(2)}) copy-start(bf16[128,32,128]{2,1,0:T(8,128)(2,1)S(1)} %all-to-all-done.4) | copy-start | bytes 3145732
  211.7 5.0 %collective-permute-start = (bf16[64,128,128]{2,1,0:T(8,128)(2,1)}, bf16[64,128,128]{2,1,0:T(8,128)(2,1)S(1)}, u32[]{:S(2)}, u32[]{:S(2)}) collective-permute-start(bf16[64,128,128]{2,1,0:T(8,128)(2,1)} %get-tuple-element.108), channel_id=1, source_target_pairs={{0,1},{1,0},{2,3},{3,2},{4,5},{5,4},{6,7},{7,6},{8,9},{9,8},{10,11... | collective-permute-start | bytes 6291464 | tf_op jit(solution)/shard_map/ppermute | solution.py:590
  220.6 37.8 %all-to-all-start.5 = ((bf16[64,128,128]{2,1,0:T(8,128)(2,1)}), bf16[64,128,128]{2,1,0:T(8,128)(2,1)}, u32[]{:S(2)}, u32[]{:S(2)}) async-start(bf16[64,128,128]{2,1,0:T(8,128)(2,1)} %add_convert_fusion), calls=%async_computation.5 | async-start | bytes 4194304 | tf_op jit(solution)/shard_map/all_to_all | solution.py:592
  261.8 53.6 %all-to-all-start.6 = ((bf16[64,128,128]{2,1,0:T(8,128)(2,1)}), bf16[64,128,128]{2,1,0:T(8,128)(2,1)}, u32[]{:S(2)}, u32[]{:S(2)}) async-start(bf16[64,128,128]{2,1,0:T(8,128)(2,1)} %spread.1), calls=%async_computation.6 | async-start | bytes 4194304 | tf_op jit(solution)/shard_map/all_to_all | solution.py:621
  271.1 27.6 %collective-permute-start.3 = (bf16[4,32,1024]{2,1,0:T(8,128)(2,1)S(1)}, bf16[4,32,1024]{2,1,0:T(8,128)(2,1)S(1)}, u32[]{:S(2)}, u32[]{:S(2)}) collective-permute-start(bf16[4,32,1024]{2,1,0:T(8,128)(2,1)S(1)} %get-tuple-element.117), channel_id=1, source_target_pairs={{0,24},{1,25},{2,26},{3,27},{4,28},{5,29},{6,30},{7,31},{8,0},{9,1... | collective-permute-start | bytes 786440 | tf_op jit(solution)/shard_map/ppermute | solution.py:446
  273.3 26.5 %collective-permute-start.2 = (bf16[4,32,1024]{2,1,0:T(8,128)(2,1)S(1)}, bf16[4,32,1024]{2,1,0:T(8,128)(2,1)S(1)}, u32[]{:S(2)}, u32[]{:S(2)}) collective-permute-start(bf16[4,32,1024]{2,1,0:T(8,128)(2,1)S(1)} %get-tuple-element.118), channel_id=1, source_target_pairs={{0,16},{1,17},{2,18},{3,19},{4,20},{5,21},{6,22},{7,23},{8,24},{9,... | collective-permute-start | bytes 786440 | tf_op jit(solution)/shard_map/ppermute | solution.py:446
  273.9 31.8 %collective-permute-start.1 = (bf16[4,32,1024]{2,1,0:T(8,128)(2,1)S(1)}, bf16[4,32,1024]{2,1,0:T(8,128)(2,1)S(1)}, u32[]{:S(2)}, u32[]{:S(2)}) collective-permute-start(bf16[4,32,1024]{2,1,0:T(8,128)(2,1)S(1)} %get-tuple-element.116), channel_id=1, source_target_pairs={{0,8},{1,9},{2,10},{3,11},{4,12},{5,13},{6,14},{7,15},{8,16},{9,17... | collective-permute-start | bytes 786440 | tf_op jit(solution)/shard_map/ppermute | solution.py:446
  306.9 4.6 %collective-permute-start.6 = (bf16[32,1024]{1,0:T(8,128)(2,1)S(1)}, bf16[32,1024]{1,0:T(8,128)(2,1)S(1)}, u32[]{:S(2)}, u32[]{:S(2)}) collective-permute-start(bf16[32,1024]{1,0:T(8,128)(2,1)S(1)} %get-tuple-element.120), channel_id=1, source_target_pairs={{0,96},{1,97},{2,98},{3,99},{4,100},{5,101},{6,102},{7,103},{8,104... | collective-permute-start | bytes 196616 | tf_op jit(solution)/shard_map/ppermute | solution.py:446
  310.2 4.7 %collective-permute-start.5 = (bf16[32,1024]{1,0:T(8,128)(2,1)S(1)}, bf16[32,1024]{1,0:T(8,128)(2,1)S(1)}, u32[]{:S(2)}, u32[]{:S(2)}) collective-permute-start(bf16[32,1024]{1,0:T(8,128)(2,1)S(1)} %get-tuple-element.121), channel_id=1, source_target_pairs={{0,64},{1,65},{2,66},{3,67},{4,68},{5,69},{6,70},{7,71},{8,72},{9,... | collective-permute-start | bytes 196616 | tf_op jit(solution)/shard_map/ppermute | solution.py:446
  310.3 5.0 %collective-permute-start.4 = (bf16[32,1024]{1,0:T(8,128)(2,1)S(1)}, bf16[32,1024]{1,0:T(8,128)(2,1)S(1)}, u32[]{:S(2)}, u32[]{:S(2)}) collective-permute-start(bf16[32,1024]{1,0:T(8,128)(2,1)S(1)} %get-tuple-element.119), channel_id=1, source_target_pairs={{0,32},{1,33},{2,34},{3,35},{4,36},{5,37},{6,38},{7,39},{8,40},{9,... | collective-permute-start | bytes 196616 | tf_op jit(solution)/shard_map/ppermute | solution.py:446
  315.4 68.4 %collective-permute-start.7 = (bf16[64,128,128]{2,1,0:T(8,128)(2,1)}, bf16[64,128,128]{2,1,0:T(8,128)(2,1)}, u32[]{:S(2)}, u32[]{:S(2)}) collective-permute-start(bf16[64,128,128]{2,1,0:T(8,128)(2,1)} %all-to-all-done.6.half), channel_id=1, source_target_pairs={{0,1},{1,0},{2,3},{3,2},{4,5},{5,4},{6,7},{7,6},{8,9},{9,8},{10,11... | collective-permute-start | bytes 6291464 | tf_op jit(solution)/shard_map/ppermute | solution.py:625
Sparse Core Ops, SparseCore 0:
  174.0 86.5 reduce-scatter.1

commit v6 on v5

--- a/solution.py
+++ b/solution.py
@@ -44,9 +44,19 @@
 
 
 def freq_kernel(blocks, samples, first_micro, ids, table_ref, *refs):
-    *outs, table = refs
-    table[...] = table_ref[...].astype(f32)
-    unroll = 32
+    *outs, table, low, sems = refs
+    pieces = sems.shape[0]
+    size = table.shape[0] // pieces
+    loads = []
+    for k in range(pieces):
+        at = pl.ds(k * size, size)
+        loads.append(pltpu.make_async_copy(table_ref.at[at, :], low.at[at, :], sems.at[k]))
+        loads[k].start()
+    for k in range(pieces):
+        at = slice(k * size, (k + 1) * size)
+        loads[k].wait()
+        table[at, :] = low[at, :].astype(f32)
+    unroll = 64
     for m, out in enumerate(outs):
         start = (first_micro + m) * blocks * 2 * samples
 
@@ -421,8 +431,12 @@
         return local_call(
             functools.partial(freq_kernel, features, samples, first_micro),
             [((n_slots, emb), f32)] * count,
-            [SMEM, VMEM],
-            [pltpu.VMEM((freq_rows, emb), f32)],
+            [SMEM, HBM],
+            [
+                pltpu.VMEM((freq_rows, emb), f32),
+                pltpu.VMEM((freq_rows, emb), bf16),
+                pltpu.SemaphoreType.DMA((8,)),
+            ],
             f"freq_rows{first_micro}",
             62,
             0,
@@ -627,10 +641,10 @@
     (placed,) = local_call(
         functools.partial(place_kernel, 0),
         [(full, bf16)],
-        [SMEM, HBM],
+        [SMEM, VMEM],
         [pltpu.SemaphoreType.DMA],
         "place_own",
-        62,
+        40,
         0,
         4 * MIB,
         [HBM],
@@ -638,10 +652,10 @@
     (placed,) = local_call(
         functools.partial(place_kernel, 1),
         [(full, bf16)],
-        [SMEM, HBM, HBM],
+        [SMEM, VMEM, HBM],
         [pltpu.SemaphoreType.DMA],
         "place_other",
-        62,
+        40,
         0,
         4 * MIB,
         [HBM],

time: 461 us -> 340 us (0.74)
  Pallas kernels: 292 us -> 168 us
    pallas_call x2, Pallas kernels: 129 us -> 2.65 us  [the longest x1 1.33 us: on_device(): local_call(functools.partial(place_kernel, 0), [(full, bf16)], [SMEM, VME...]
  transfers between devices with their start and end apart: 16 -> 16, of which waited for: 9 -> 9; matrix products, arithmetic and copies ran while one was open for 3% -> 4% of each run, Pallas kernels for 44% -> 43%
where the time goes in v6:
time: 340 us; the launch traced here: 334 us
  Pallas kernels  168 us (49%)
  starting transfers between devices  81.8 us (24%)
  waiting for transfers between devices  51.4 us (15%)
  between operations  15.6 us (5%)
  other arithmetic  8.54 us (3%)
  local copies, waits for them, and re-layouts  8.3 us (2%)
    pallas_call x3, Pallas kernels, on_device(): local_call(functools.partial(micro_kernel, devices, cap, features, m, m *...  53.7 us
    all_to_all x4, starting transfers between devices, exchange(): lax.all_to_all(rows.reshape(devices, count, emb), 'dev', split_axis=0, co...  40.7 us
    pallas_call x3, Pallas kernels, freq_rows_of(): local_call(functools.partial(freq_kernel, features, samples, first_micro)...  36.1 us
    ppermute x6, waiting for transfers between devices, axis_sum(): total = total + lax.ppermute(block, 'dev', to).astype(f32)  35.7 us
    pallas_call x1, Pallas kernels, on_device(): local_call(functools.partial(freq_grad_kernel, features), [((devices // 2...  27.7 us
    pallas_call x2, Pallas kernels, lookup(): local_call(functools.partial(lookup_kernel, devices, stride, start, count...  17.5 us
    pallas_call x1, Pallas kernels, on_device(): local_call(functools.partial(owner_kernel, devices, stride, cap), [((owne...  17.1 us
    all_to_all x1, starting transfers between devices, on_device(): lax.all_to_all(line, 'dev', split_axis=0, concat_axis=0, tiled=True)  11.5 us
  transfers between devices with their start and end apart: 16, of which 9 were waited for; matrix products, arithmetic and copies ran while one was open for 4% of the time, Pallas kernels for 43%

profile of v6, /device:TPU:1, one launch (start us, length us, event | category | flops | bytes accessed | tf_op | source)
XLA Modules:
  0.0 334.1 jit_solution(14672745610475199572)
XLA Ops:
  7.2 0.8 bitcast_select_fusion
  8.0 0.7 copy.45
  8.7 11.5 %all-to-all-start = ((s32[128,1,128]{2,1,0:T(1,128)}), s32[128,1,128]{2,1,0:T(1,128)S(1)}, u32[]{:S(2)}, u32[]{:S(2)}) async-start(s32[128,1,128]{2,1,0:T(1,128)} %copy.45), calls=%async_computation | async-start | bytes 131072 | tf_op jit(solution)/shard_map/all_to_all | solution.py:428
  20.3 1.6 reshape.102.ids
  21.8 12.0 %freq_rows0.1.freq_part_hbm = f32[3328,128]{1,0:T(8,128)} custom-call(s32[19968]{0:T(1024)} %reshape.102.ids, bf16[16384,128]{1,0:T(8,128)(2,1)} %table_ref.9), custom_call_target="tpu_custom_call" | custom-call | bytes 27262976 | tf_op jit(solution)/shard_map/freq_rows0/pallas_call | solution.py:431
  33.9 0.6 broadcast_minimum_fusion.asked
  34.5 7.0 %lookup0.1 = bf16[4096,128]{1,0:T(8,128)(2,1)} custom-call(s32[16384]{0:T(1024)} %broadcast_minimum_fusion.asked, bf16[4096,128]{1,0:T(8,128)(2,1)} %table_ref.7), custom_call_target="tpu_custom_call" | custom-call | bytes 20971520 | tf_op jit(solution)/shard_map/lookup0/pallas_call | solution.py:471
  41.5 9.8 %all-to-all-start.1 = ((bf16[128,32,128]{2,1,0:T(8,128)(2,1)}), bf16[128,32,128]{2,1,0:T(8,128)(2,1)S(1)}, u32[]{:S(2)}, u32[]{:S(2)}) async-start(bf16[128,32,128]{2,1,0:T(8,128)(2,1)} %bitcast.120), calls=%async_computation.1 | async-start | bytes 2097152 | tf_op jit(solution)/shard_map/all_to_all | solution.py:464
  51.3 0.6 reshape.125.weight
  51.9 0.6 reshape.110.bias
  52.5 0.6 convert_element_type.48.labels
  53.1 0.7 fusion.7
  53.8 10.5 %lookup32.1 = bf16[8192,128]{1,0:T(8,128)(2,1)} custom-call(s32[16384]{0:T(1024)} %broadcast_minimum_fusion.asked, bf16[4096,128]{1,0:T(8,128)(2,1)} %table_ref.7), custom_call_target="tpu_custom_call" | custom-call | bytes 41943040 | tf_op jit(solution)/shard_map/lookup32/pallas_call | solution.py:471
  64.3 12.0 %freq_rows1.1.freq_part_hbm = f32[3328,128]{1,0:T(8,128)} custom-call(s32[19968]{0:T(1024)} %reshape.102.ids, bf16[16384,128]{1,0:T(8,128)(2,1)} %table_ref.9), custom_call_target="tpu_custom_call" | custom-call | bytes 27262976 | tf_op jit(solution)/shard_map/freq_rows1/pallas_call | solution.py:431
  76.4 1.0 copy-done.1
  77.3 10.6 %all-to-all-start.2 = ((bf16[128,64,128]{2,1,0:T(8,128)(2,1)}), bf16[128,64,128]{2,1,0:T(8,128)(2,1)}, u32[]{:S(2)}, u32[]{:S(2)}) async-start(bf16[128,64,128]{2,1,0:T(8,128)(2,1)} %bitcast.119), calls=%async_computation.2 | async-start | bytes 4194304 | tf_op jit(solution)/shard_map/all_to_all | solution.py:464
  88.6 12.0 %freq_rows2.1.freq_part_hbm = f32[3328,128]{1,0:T(8,128)} custom-call(s32[19968]{0:T(1024)} %reshape.102.ids, bf16[16384,128]{1,0:T(8,128)(2,1)} %table_ref.9), custom_call_target="tpu_custom_call" | custom-call | bytes 27262976 | tf_op jit(solution)/shard_map/freq_rows2/pallas_call | solution.py:431
  100.6 17.9 %micro0.1 = (bf16[128,64,128]{2,1,0:T(8,128)(2,1)}, f32[3328,128]{1,0:T(8,128)}, bf16[128,3456]{1,0:T(8,128)(2,1)}, bf16[128,512]{1,0:T(8,128)(2,1)}, bf16[128,5...) custom-call(s32[12288]{0:T(1024)} %bitcast.123, f32[1]{0:T(128)} %bitcast.114.out_b, ...), custom_call_target="tpu_custom_call" | custom-call | flops 1358954496 | bytes 62914560 | tf_op jit(solution)/shard_map/micro0/pallas_call | solution.py:501
  118.5 17.9 %micro1.1 = (bf16[128,64,128]{2,1,0:T(8,128)(2,1)}, f32[3328,128]{1,0:T(8,128)}, bf16[128,3456]{1,0:T(8,128)(2,1)}, bf16[128,512]{1,0:T(8,128)(2,1)}, bf16[128,5...) custom-call(s32[12288]{0:T(1024)} %bitcast.124, ...), custom_call_target="tpu_custom_call", output_to_operand_aliasing={{0}: (10, {})} | custom-call | flops 1358954496 | bytes 62914560 | tf_op jit(solution)/shard_map/micro1/pallas_call | solution.py:501
  136.5 10.2 %all-to-all-start.3 = ((bf16[128,64,128]{2,1,0:T(8,128)(2,1)}), bf16[128,64,128]{2,1,0:T(8,128)(2,1)}, u32[]{:S(2)}, u32[]{:S(2)}) async-start(bf16[128,64,128]{2,1,0:T(8,128)(2,1)} %get-tuple-element.99), calls=%async_computation.3 | async-start | bytes 4194304 | tf_op jit(solution)/shard_map/all_to_all | solution.py:464
  147.0 17.8 %micro2.1 = (bf16[128,32,128]{2,1,0:T(8,128)(2,1)}, f32[3328,128]{1,0:T(8,128)}, bf16[128,3456]{1,0:T(8,128)(2,1)}, bf16[128,512]{1,0:T(8,128)(2,1)}, bf16[128,5...) custom-call(s32[12288]{0:T(1024)} %bitcast.125, f32[1]{0:T(128)} %bitcast.116.out_b, ...), custom_call_target="tpu_custom_call" | custom-call | flops 1358954496 | bytes 62914560 | tf_op jit(solution)/shard_map/micro2/pallas_call | solution.py:501
  164.9 0.8 add_add_fusion
  166.0 1.1 pad.9.columns
  167.0 10.4 %dense_grads.1 = bf16[8,16,32,1024]{3,2,1,0:T(8,128)(2,1)} custom-call(f32[128,16,128]{2,1,0:T(8,128)} %pad.9.columns, bf16[128,3456]{1,0:T(8,128)(2,1)} %get-tuple-element.86.x0, bf16[128,3456]{1,0:T(8,128)(2,1)} %get-tuple-element.87.x1, bf16[128,3456]{1,0:T(8,128)(2,1)} %get-tuple-element.88.x2, bf16[128,3456]{1,0:T(8,128)(2,1)} %get-tuple-element.89.g0, ...), custom_call_target="tpu_custom_call" | custom-call | flops 2717908992 | bytes 41943040 | tf_op jit(solution)/shard_map/dense_grads/pallas_call | solution.py:564
  177.5 10.1 %all-to-all-start.4 = ((bf16[128,32,128]{2,1,0:T(8,128)(2,1)}), bf16[128,32,128]{2,1,0:T(8,128)(2,1)S(1)}, u32[]{:S(2)}, u32[]{:S(2)}) async-start(bf16[128,32,128]{2,1,0:T(8,128)(2,1)} %get-tuple-element.107), calls=%async_computation.4 | async-start | bytes 2097152 | tf_op jit(solution)/shard_map/all_to_all | solution.py:464
  187.6 27.7 %freq_grads.1 = (bf16[64,128,128]{2,1,0:T(8,128)(2,1)}, bf16[64,128,128]{2,1,0:T(8,128)(2,1)}) custom-call(s32[1]{0:T(128)} %bitcast.core, s32[19968]{0:T(1024)} %reshape.102.ids, f32[3328,128]{1,0:T(8,128)} %get-tuple-element.102.d0, f32[3328,128]{1,0:T(8,128)} %get-tuple-element.103.d1, f32[3328,128]{1,0:T(8,128)} %get-tuple-element.104.d2), custom_call_target="tpu_custom_call" | custom-call | bytes 125829120 | tf_op jit(solution)/shard_map/freq_grads/pallas_call | solution.py:591
  215.3 1.0 collective-permute-start
  216.4 4.0 %collective-permute-done = bf16[64,128,128]{2,1,0:T(8,128)(2,1)S(1)} collective-permute-done((bf16[64,128,128]{2,1,0:T(8,128)(2,1)}, bf16[64,128,128]{2,1,0:T(8,128)(2,1)S(1)}, u32[]{:S(2)}, u32[]{:S(2)}) %collective-permute-start) | collective-permute-done | bytes 2097184 | tf_op jit(solution)/shard_map/ppermute | solution.py:604
  220.4 3.8 %add_convert_fusion = bf16[64,128,128]{2,1,0:T(8,128)(2,1)} fusion(bf16[64,128,128]{2,1,0:T(8,128)(2,1)S(1)} %collective-permute-done, bf16[64,128,128]{2,1,0:T(8,128)(2,1)} %get-tuple-element.105), kind=kLoop, calls=%fused_computation | loop fusion | flops 4194304 | bytes 6291456 | tf_op jit(solution)/shard_map/convert_element_type | solution.py:605
  224.2 10.3 %all-to-all-start.5 = ((bf16[64,128,128]{2,1,0:T(8,128)(2,1)}), bf16[64,128,128]{2,1,0:T(8,128)(2,1)}, u32[]{:S(2)}, u32[]{:S(2)}) async-start(bf16[64,128,128]{2,1,0:T(8,128)(2,1)} %add_convert_fusion), calls=%async_computation.5 | async-start | bytes 4194304 | tf_op jit(solution)/shard_map/all_to_all | solution.py:606
  234.5 17.1 %owner_grads.1 = bf16[4096,128]{1,0:T(8,128)(2,1)} custom-call(s32[16384]{0:T(1024)} %bitcast.127, bf16[128,64,128]{2,1,0:T(8,128)(2,1)} %bitcast.29.first, bf16[128,32,128]{2,1,0:T(8,128)(2,1)} %copy-done), custom_call_target="tpu_custom_call" | custom-call | bytes 62914560 | tf_op jit(solution)/shard_map/owner_grads/pallas_call | solution.py:609
  251.6 10.4 %all-to-all-done.5.parts = bf16[64,128,128]{2,1,0:T(8,128)(2,1)} async-done(((bf16[64,128,128]{2,1,0:T(8,128)(2,1)}), bf16[64,128,128]{2,1,0:T(8,128)(2,1)}, u32[]{:S(2)}, u32[]{:S(2)}) %all-to-all-start.5) | async-done | bytes 2097184 | tf_op jit(solution)/shard_map/all_to_all | solution.py:606
  262.0 3.4 %spread.1 = bf16[64,128,128]{2,1,0:T(8,128)(2,1)} custom-call(bf16[64,128,128]{2,1,0:T(8,128)(2,1)} %all-to-all-done.5.parts), custom_call_target="tpu_custom_call" | custom-call | bytes 4194304 | tf_op jit(solution)/shard_map/spread/pallas_call | solution.py:625
  265.4 7.7 %all-to-all-start.6 = ((bf16[64,128,128]{2,1,0:T(8,128)(2,1)}), bf16[64,128,128]{2,1,0:T(8,128)(2,1)S(1)}, u32[]{:S(2)}, u32[]{:S(2)}) async-start(bf16[64,128,128]{2,1,0:T(8,128)(2,1)} %spread.1), calls=%async_computation.6 | async-start | bytes 4194304 | tf_op jit(solution)/shard_map/all_to_all | solution.py:635
  273.3 1.2 dynamic-slice_bitcast_fusion.2
  274.5 2.3 collective-permute-start.3
  277.9 24.4 %collective-permute-done.3 = bf16[4,32,1024]{2,1,0:T(8,128)(2,1)S(1)} collective-permute-done((bf16[4,32,1024]{2,1,0:T(8,128)(2,1)S(1)}, bf16[4,32,1024]{2,1,0:T(8,128)(2,1)S(1)}, u32[]{:S(2)}, u32[]{:S(2)}) %collective-permute-start.3) | collective-permute-done | bytes 262176 | tf_op jit(solution)/shard_map/ppermute | solution.py:460
  302.3 1.1 collective-permute-done.2
  303.4 6.0 %collective-permute-done.1 = bf16[4,32,1024]{2,1,0:T(8,128)(2,1)} collective-permute-done((bf16[4,32,1024]{2,1,0:T(8,128)(2,1)S(1)}, bf16[4,32,1024]{2,1,0:T(8,128)(2,1)}, u32[]{:S(2)}, u32[]{:S(2)}) %collective-permute-start.1) | collective-permute-done | bytes 262176 | tf_op jit(solution)/shard_map/ppermute | solution.py:460
  309.4 1.2 fusion.2
  310.6 3.3 collective-permute-start.6
  314.1 0.8 collective-permute-start.4
  315.2 3.4 %collective-permute-done.5 = bf16[32,1024]{1,0:T(8,128)(2,1)S(1)} collective-permute-done((bf16[32,1024]{1,0:T(8,128)(2,1)S(1)}, bf16[32,1024]{1,0:T(8,128)(2,1)S(1)}, u32[]{:S(2)}, u32[]{:S(2)}) %collective-permute-start.5) | collective-permute-done | bytes 65568 | tf_op jit(solution)/shard_map/ppermute | solution.py:460
  319.2 2.5 collective-permute-start.7
  321.7 1.3 place_own.1.refs_0_
  323.5 0.7 slice_bitcast_fusion
  324.2 1.3 collective-permute-done.7.half
  325.5 1.3 place_other.1
  (39 shorter events, 3.5 us)
Async XLA Ops:
  8.7 25.1 %all-to-all-start = ((s32[128,1,128]{2,1,0:T(1,128)}), s32[128,1,128]{2,1,0:T(1,128)S(1)}, u32[]{:S(2)}, u32[]{:S(2)}) async-start(s32[128,1,128]{2,1,0:T(1,128)} %copy.45), calls=%async_computation | async-start | bytes 131072 | tf_op jit(solution)/shard_map/all_to_all | solution.py:428
  33.8 7.7 %copy-start.2 = (s32[128,1,128]{2,1,0:T(1,128)}, s32[128,1,128]{2,1,0:T(1,128)S(1)}, u32[]{:S(2)}) copy-start(s32[128,1,128]{2,1,0:T(1,128)S(1)} %all-to-all-done) | copy-start | bytes 196612
  34.5 16.8 %copy-start.8 = (bf16[3456]{0:T(1024)(128)(2,1)S(1)}, bf16[3456]{0:T(1024)(128)(2,1)}, u32[]{:S(2)}) copy-start(bf16[3456]{0:T(1024)(128)(2,1)} %param.22) | copy-start | bytes 20740
  34.5 17.4 %copy-start.7 = (f32[3456]{0:T(1024)S(1)}, f32[3456]{0:T(1024)}, u32[]{:S(2)}) copy-start(f32[3456]{0:T(1024)} %param.21) | copy-start | bytes 41476
  34.5 18.0 %copy-start.9 = (s32[3,128]{1,0:T(4,128)S(1)}, s32[3,128]{1,0:T(4,128)}, u32[]{:S(2)}) copy-start(s32[3,128]{1,0:T(4,128)} %param.13) | copy-start | bytes 4612
  34.5 18.6 %copy-start.3 = (s32[3,1,128,32]{2,3,1,0:T(8,128)S(1)}, s32[3,1,128,32]{2,3,1,0:T(8,128)}, u32[]{:S(2)}) copy-start(s32[3,1,128,32]{2,3,1,0:T(8,128)} %param.16) | copy-start | bytes 147460
  34.5 18.6 %copy-start.4 = (s32[3,1,128,32]{2,3,1,0:T(8,128)S(1)}, s32[3,1,128,32]{2,3,1,0:T(8,128)}, u32[]{:S(2)}) copy-start(s32[3,1,128,32]{2,3,1,0:T(8,128)} %param.15) | copy-start | bytes 147460
  41.5 34.8 %all-to-all-start.1 = ((bf16[128,32,128]{2,1,0:T(8,128)(2,1)}), bf16[128,32,128]{2,1,0:T(8,128)(2,1)S(1)}, u32[]{:S(2)}, u32[]{:S(2)}) async-start(bf16[128,32,128]{2,1,0:T(8,128)(2,1)} %bitcast.120), calls=%async_computation.1 | async-start | bytes 2097152 | tf_op jit(solution)/shard_map/all_to_all | solution.py:464
  76.4 1.0 copy-start.1
  77.3 41.2 %all-to-all-start.2 = ((bf16[128,64,128]{2,1,0:T(8,128)(2,1)}), bf16[128,64,128]{2,1,0:T(8,128)(2,1)}, u32[]{:S(2)}, u32[]{:S(2)}) async-start(bf16[128,64,128]{2,1,0:T(8,128)(2,1)} %bitcast.119), calls=%async_computation.2 | async-start | bytes 4194304 | tf_op jit(solution)/shard_map/all_to_all | solution.py:464
  136.5 41.0 %all-to-all-start.3 = ((bf16[128,64,128]{2,1,0:T(8,128)(2,1)}), bf16[128,64,128]{2,1,0:T(8,128)(2,1)}, u32[]{:S(2)}, u32[]{:S(2)}) async-start(bf16[128,64,128]{2,1,0:T(8,128)(2,1)} %get-tuple-element.99), calls=%async_computation.3 | async-start | bytes 4194304 | tf_op jit(solution)/shard_map/all_to_all | solution.py:464
  146.7 126.6 %reduce-scatter.2.cloned.1.call-start = ((), (), s32[]{:S(2)}) async-start(), calls=%async_computation.8 | async-start | bytes 9437184 | tf_op jit(solution)/shard_map/reduce_scatter | solution.py:588
  147.0 17.9 %copy-start.5 = (f32[2,3456]{1,0:T(2,128)S(1)}, f32[2,3456]{1,0:T(2,128)}, u32[]{:S(2)}) copy-start(f32[2,3456]{1,0:T(2,128)} %get-tuple-element.77) | copy-start | bytes 82948
  147.0 17.9 %copy-start.6 = (f32[2,3456]{1,0:T(2,128)S(1)}, f32[2,3456]{1,0:T(2,128)}, u32[]{:S(2)}) copy-start(f32[2,3456]{1,0:T(2,128)} %get-tuple-element.82) | copy-start | bytes 82948
  177.5 37.9 %all-to-all-start.4 = ((bf16[128,32,128]{2,1,0:T(8,128)(2,1)}), bf16[128,32,128]{2,1,0:T(8,128)(2,1)S(1)}, u32[]{:S(2)}, u32[]{:S(2)}) async-start(bf16[128,32,128]{2,1,0:T(8,128)(2,1)} %get-tuple-element.107), calls=%async_computation.4 | async-start | bytes 2097152 | tf_op jit(solution)/shard_map/all_to_all | solution.py:464
  215.3 8.9 %copy-start = (bf16[128,32,128]{2,1,0:T(8,128)(2,1)}, bf16[128,32,128]{2,1,0:T(8,128)(2,1)S(1)}, u32[]{:S(2)}) copy-start(bf16[128,32,128]{2,1,0:T(8,128)(2,1)S(1)} %all-to-all-done.4) | copy-start | bytes 3145732
  215.3 5.0 %collective-permute-start = (bf16[64,128,128]{2,1,0:T(8,128)(2,1)}, bf16[64,128,128]{2,1,0:T(8,128)(2,1)S(1)}, u32[]{:S(2)}, u32[]{:S(2)}) collective-permute-start(bf16[64,128,128]{2,1,0:T(8,128)(2,1)} %get-tuple-element.108), channel_id=1, source_target_pairs={{0,1},{1,0},{2,3},{3,2},{4,5},{5,4},{6,7},{7,6},{8,9},{9,8},{10,11... | collective-permute-start | bytes 6291464 | tf_op jit(solution)/shard_map/ppermute | solution.py:604
  224.2 37.8 %all-to-all-start.5 = ((bf16[64,128,128]{2,1,0:T(8,128)(2,1)}), bf16[64,128,128]{2,1,0:T(8,128)(2,1)}, u32[]{:S(2)}, u32[]{:S(2)}) async-start(bf16[64,128,128]{2,1,0:T(8,128)(2,1)} %add_convert_fusion), calls=%async_computation.5 | async-start | bytes 4194304 | tf_op jit(solution)/shard_map/all_to_all | solution.py:606
  265.4 53.8 %all-to-all-start.6 = ((bf16[64,128,128]{2,1,0:T(8,128)(2,1)}), bf16[64,128,128]{2,1,0:T(8,128)(2,1)S(1)}, u32[]{:S(2)}, u32[]{:S(2)}) async-start(bf16[64,128,128]{2,1,0:T(8,128)(2,1)} %spread.1), calls=%async_computation.6 | async-start | bytes 4194304 | tf_op jit(solution)/shard_map/all_to_all | solution.py:635
  274.5 27.8 %collective-permute-start.3 = (bf16[4,32,1024]{2,1,0:T(8,128)(2,1)S(1)}, bf16[4,32,1024]{2,1,0:T(8,128)(2,1)S(1)}, u32[]{:S(2)}, u32[]{:S(2)}) collective-permute-start(bf16[4,32,1024]{2,1,0:T(8,128)(2,1)S(1)} %get-tuple-element.117), channel_id=1, source_target_pairs={{0,24},{1,25},{2,26},{3,27},{4,28},{5,29},{6,30},{7,31},{8,0},{9,1... | collective-permute-start | bytes 786440 | tf_op jit(solution)/shard_map/ppermute | solution.py:460
  276.8 26.6 %collective-permute-start.2 = (bf16[4,32,1024]{2,1,0:T(8,128)(2,1)S(1)}, bf16[4,32,1024]{2,1,0:T(8,128)(2,1)S(1)}, u32[]{:S(2)}, u32[]{:S(2)}) collective-permute-start(bf16[4,32,1024]{2,1,0:T(8,128)(2,1)S(1)} %get-tuple-element.118), channel_id=1, source_target_pairs={{0,16},{1,17},{2,18},{3,19},{4,20},{5,21},{6,22},{7,23},{8,24},{9,... | collective-permute-start | bytes 786440 | tf_op jit(solution)/shard_map/ppermute | solution.py:460
  277.3 32.0 %collective-permute-start.1 = (bf16[4,32,1024]{2,1,0:T(8,128)(2,1)S(1)}, bf16[4,32,1024]{2,1,0:T(8,128)(2,1)}, u32[]{:S(2)}, u32[]{:S(2)}) collective-permute-start(bf16[4,32,1024]{2,1,0:T(8,128)(2,1)S(1)} %get-tuple-element.116), channel_id=1, source_target_pairs={{0,8},{1,9},{2,10},{3,11},{4,12},{5,13},{6,14},{7,15},{8,16},{9,17... | collective-permute-start | bytes 786440 | tf_op jit(solution)/shard_map/ppermute | solution.py:460
  310.6 4.6 %collective-permute-start.6 = (bf16[32,1024]{1,0:T(8,128)(2,1)S(1)}, bf16[32,1024]{1,0:T(8,128)(2,1)S(1)}, u32[]{:S(2)}, u32[]{:S(2)}) collective-permute-start(bf16[32,1024]{1,0:T(8,128)(2,1)S(1)} %get-tuple-element.120), channel_id=1, source_target_pairs={{0,96},{1,97},{2,98},{3,99},{4,100},{5,101},{6,102},{7,103},{8,104... | collective-permute-start | bytes 196616 | tf_op jit(solution)/shard_map/ppermute | solution.py:460
  313.9 4.7 %collective-permute-start.5 = (bf16[32,1024]{1,0:T(8,128)(2,1)S(1)}, bf16[32,1024]{1,0:T(8,128)(2,1)S(1)}, u32[]{:S(2)}, u32[]{:S(2)}) collective-permute-start(bf16[32,1024]{1,0:T(8,128)(2,1)S(1)} %get-tuple-element.121), channel_id=1, source_target_pairs={{0,64},{1,65},{2,66},{3,67},{4,68},{5,69},{6,70},{7,71},{8,72},{9,... | collective-permute-start | bytes 196616 | tf_op jit(solution)/shard_map/ppermute | solution.py:460
  314.1 5.0 %collective-permute-start.4 = (bf16[32,1024]{1,0:T(8,128)(2,1)S(1)}, bf16[32,1024]{1,0:T(8,128)(2,1)S(1)}, u32[]{:S(2)}, u32[]{:S(2)}) collective-permute-start(bf16[32,1024]{1,0:T(8,128)(2,1)S(1)} %get-tuple-element.119), channel_id=1, source_target_pairs={{0,32},{1,33},{2,34},{3,35},{4,36},{5,37},{6,38},{7,39},{8,40},{9,... | collective-permute-start | bytes 196616 | tf_op jit(solution)/shard_map/ppermute | solution.py:460
  319.2 6.3 %collective-permute-start.7 = (bf16[64,128,128]{2,1,0:T(8,128)(2,1)S(1)}, bf16[64,128,128]{2,1,0:T(8,128)(2,1)S(1)}, u32[]{:S(2)}, u32[]{:S(2)}) collective-permute-start(bf16[64,128,128]{2,1,0:T(8,128)(2,1)S(1)} %all-to-all-done.6.half), channel_id=1, source_target_pairs={{0,1},{1,0},{2,3},{3,2},{4,5},{5,4},{6,7},{7,6},{8,9},{9,8},{10,11... | collective-permute-start | bytes 6291464 | tf_op jit(solution)/shard_map/ppermute | solution.py:639
Sparse Core Ops, SparseCore 0:
  177.6 86.5 reduce-scatter.1

commit v7 on v5

--- a/solution.py
+++ b/solution.py
@@ -322,7 +322,7 @@
 
     def block(q, carry):
         for ref, parity in ((keep, mine), (send, 1 - mine)):
-            at = pl.ds(pl.multiple_of((2 * q + parity) * rows, rows), rows)
+            at = pl.ds(pl.multiple_of(((q % 4 * 2 + parity) * 16 + q // 4) * rows, rows), rows)
             ref[q] = tree_sum([a[at, :] for a in accs]).astype(bf16)
         return carry
 
@@ -334,16 +334,8 @@
     for k in range(1, parts.shape[0]):
         total = total + parts[k].astype(f32)
     total = total.astype(bf16)
-    for k in range(parts.shape[0]):
+    for k in range(out.shape[0]):
         out[k] = total
-
-
-def place_kernel(other, core, half, *refs):
-    out, sem = refs[-2:]
-    at = core[0] if other == 0 else 1 - core[0]
-    copy = pltpu.make_async_copy(half, out.at[:, at], sem)
-    copy.start()
-    copy.wait()
 
 
 def owner_kernel(peers, stride, cap, asked, first, last, out, rows, *accs):
@@ -572,8 +564,6 @@
     dense = dense.reshape(devices, rows_pad, 2 * rank)
     near = [list(range(d, d + 8)) for d in range(0, devices, 8)]
     dense = lax.psum_scatter(dense, "dev", axis_index_groups=near, tiled=True)
-    dense = axis_sum(dense.reshape(4, 4, rows_pad, 2 * rank), 8).astype(bf16)
-    dense = axis_sum(dense, 32)
     keep_f, send_f = local_call(
         functools.partial(freq_grad_kernel, features),
         [((devices // 2, per_freq, emb), bf16)] * 2,
@@ -610,7 +600,7 @@
     parts, grad_inf = lax.optimization_barrier((parts, grad_inf))
     (spread,) = local_call(
         spread_kernel,
-        [(parts.shape, bf16)],
+        [((devices // 8, per_freq, emb), bf16)],
         [VMEM],
         [],
         "spread",
@@ -618,37 +608,18 @@
         0,
         4 * MIB,
     )(parts)
-    half = lax.all_to_all(
-        spread, "dev", split_axis=0, concat_axis=0, axis_index_groups=same_core, tiled=True
-    )
-    half, dense = lax.optimization_barrier((half, dense))
-    rest = lax.ppermute(half, "dev", other_core)
-    full = (devices // 2, 2, per_freq, emb)
-    (placed,) = local_call(
-        functools.partial(place_kernel, 0),
-        [(full, bf16)],
-        [SMEM, HBM],
-        [pltpu.SemaphoreType.DMA],
-        "place_own",
-        62,
-        0,
-        4 * MIB,
-        [HBM],
-    )(core, half)
-    (placed,) = local_call(
-        functools.partial(place_kernel, 1),
-        [(full, bf16)],
-        [SMEM, HBM, HBM],
-        [pltpu.SemaphoreType.DMA],
-        "place_other",
-        62,
-        0,
-        4 * MIB,
-        [HBM],
-        {2: 0},
-    )(core, rest, placed)
-    grad_freq = placed.reshape(freq_rows, emb)
-
+    sixteen = lax.all_to_all(
+        spread,
+        "dev",
+        split_axis=0,
+        concat_axis=0,
+        axis_index_groups=[list(range(k, devices, 8)) for k in range(8)],
+        tiled=True,
+    ).reshape(freq_rows // 8, emb)
+    sixteen, dense = lax.optimization_barrier((sixteen, dense))
+    grad_freq = lax.all_gather(sixteen, "dev", axis_index_groups=near, tiled=True)
+    dense = axis_sum(dense.reshape(4, 4, rows_pad, 2 * rank), 8).astype(bf16)
+    dense = axis_sum(dense, 32)
     grad_u = dense[:per, :rank]
     grad_v = dense[:per, rank:].T
     grad_b = dense[per, :per]

time: 461 us -> 325 us (0.70)
  Pallas kernels: 292 us -> 162 us
  waiting for transfers between devices: 50.5 us -> 35.3 us
  blocking collectives: 0 us -> 14.9 us
  starting transfers between devices: 81.4 us -> 71.8 us
    pallas_call x3 -> x1, Pallas kernels: 133 us -> 2.7 us  [on_device(): local_call(spread_kernel, [((devices // 8, per_freq, emb), bf16)], [VMEM]...]
    ppermute x6, waiting for transfers between devices: 35.5 us -> 12.6 us  [axis_sum(): total = total + lax.ppermute(block, 'dev', to).astype(f32)]
    all_to_all x0 -> x1, blocking collectives: none -> 14.9 us  [on_device(): lax.all_to_all(spread, 'dev', split_axis=0, concat_axis=0, axis_index_gro...]
    all_to_all x1 -> x0, starting transfers between devices: 8.02 us -> none  [on_device(): lax.all_to_all(spread, 'dev', split_axis=0, concat_axis=0, axis_index_gro...]
    all_gather x0 -> x1, waiting for transfers between devices: none -> 7.7 us  [on_device(): lax.all_gather(sixteen, 'dev', axis_index_groups=near, tiled=True)]
  transfers between devices with their start and end apart: 16 -> 15, of which waited for: 9 -> 10; matrix products, arithmetic and copies ran while one was open for 3% -> 4% of each run, Pallas kernels for 44% -> 43%
where the time goes in v7:
time: 325 us; the launch traced here: 320 us
  Pallas kernels  162 us (50%)
  starting transfers between devices  71.8 us (22%)
  waiting for transfers between devices  35.3 us (11%)
  between operations  15.5 us (5%)
  blocking collectives  14.9 us (5%)
  local copies, waits for them, and re-layouts  12 us (4%)
  other arithmetic  8.43 us (3%)
    pallas_call x3, Pallas kernels, on_device(): local_call(functools.partial(micro_kernel, devices, cap, features, m, m *...  53.7 us
    all_to_all x4, starting transfers between devices, exchange(): lax.all_to_all(rows.reshape(devices, count, emb), 'dev', split_axis=0, co...  40.1 us
    pallas_call x3, Pallas kernels, freq_rows_of(): local_call(functools.partial(freq_kernel, features, samples, first_micro)...  32.5 us
    pallas_call x1, Pallas kernels, on_device(): local_call(functools.partial(freq_grad_kernel, features), [((devices // 2...  28.1 us
    pallas_call x2, Pallas kernels, lookup(): local_call(functools.partial(lookup_kernel, devices, stride, start, count...  17.5 us
    pallas_call x1, Pallas kernels, on_device(): local_call(functools.partial(owner_kernel, devices, stride, cap), [((owne...  17 us
    all_to_all x1, blocking collectives, on_device(): lax.all_to_all(spread, 'dev', split_axis=0, concat_axis=0, axis_index_gro...  14.9 us
    ppermute x6, waiting for transfers between devices, axis_sum(): total = total + lax.ppermute(block, 'dev', to).astype(f32)  12.6 us
  transfers between devices with their start and end apart: 15, of which 10 were waited for; matrix products, arithmetic and copies ran while one was open for 4% of the time, Pallas kernels for 43%

profile of v7, /device:TPU:1, one launch (start us, length us, event | category | flops | bytes accessed | tf_op | source)
XLA Modules:
  0.0 319.8 jit_solution(5638373881068171684)
XLA Ops:
  7.2 0.8 bitcast_select_fusion
  8.0 0.7 copy.44
  8.7 11.5 %all-to-all-start = ((s32[128,1,128]{2,1,0:T(1,128)}), s32[128,1,128]{2,1,0:T(1,128)S(1)}, u32[]{:S(2)}, u32[]{:S(2)}) async-start(s32[128,1,128]{2,1,0:T(1,128)} %copy.44), calls=%async_computation | async-start | bytes 131072 | tf_op jit(solution)/shard_map/all_to_all | solution.py:410
  20.3 1.6 reshape.102.ids
  21.8 10.8 %freq_rows0.1.freq_part_hbm = f32[3328,128]{1,0:T(8,128)} custom-call(s32[19968]{0:T(1024)} %reshape.102.ids, bf16[16384,128]{1,0:T(8,128)(2,1)} %table_ref.9), custom_call_target="tpu_custom_call" | custom-call | bytes 27262976 | tf_op jit(solution)/shard_map/freq_rows0/pallas_call | solution.py:413
  32.6 0.6 broadcast_minimum_fusion.asked
  33.3 7.0 %lookup0.1 = bf16[4096,128]{1,0:T(8,128)(2,1)} custom-call(s32[16384]{0:T(1024)} %broadcast_minimum_fusion.asked, bf16[4096,128]{1,0:T(8,128)(2,1)} %table_ref.7), custom_call_target="tpu_custom_call" | custom-call | bytes 20971520 | tf_op jit(solution)/shard_map/lookup0/pallas_call | solution.py:449
  40.3 9.8 %all-to-all-start.1 = ((bf16[128,32,128]{2,1,0:T(8,128)(2,1)}), bf16[128,32,128]{2,1,0:T(8,128)(2,1)S(1)}, u32[]{:S(2)}, u32[]{:S(2)}) async-start(bf16[128,32,128]{2,1,0:T(8,128)(2,1)} %bitcast.119), calls=%async_computation.1 | async-start | bytes 2097152 | tf_op jit(solution)/shard_map/all_to_all | solution.py:442
  50.1 0.6 reshape.110.bias
  50.7 0.6 reshape.125.weight
  51.3 0.6 convert_element_type.48.labels
  51.9 0.7 fusion.7
  52.6 10.5 %lookup32.1 = bf16[8192,128]{1,0:T(8,128)(2,1)} custom-call(s32[16384]{0:T(1024)} %broadcast_minimum_fusion.asked, bf16[4096,128]{1,0:T(8,128)(2,1)} %table_ref.7), custom_call_target="tpu_custom_call" | custom-call | bytes 41943040 | tf_op jit(solution)/shard_map/lookup32/pallas_call | solution.py:449
  63.1 10.8 %freq_rows1.1.freq_part_hbm = f32[3328,128]{1,0:T(8,128)} custom-call(s32[19968]{0:T(1024)} %reshape.102.ids, bf16[16384,128]{1,0:T(8,128)(2,1)} %table_ref.9), custom_call_target="tpu_custom_call" | custom-call | bytes 27262976 | tf_op jit(solution)/shard_map/freq_rows1/pallas_call | solution.py:413
  74.0 1.0 copy-done.1
  74.9 10.6 %all-to-all-start.2 = ((bf16[128,64,128]{2,1,0:T(8,128)(2,1)}), bf16[128,64,128]{2,1,0:T(8,128)(2,1)}, u32[]{:S(2)}, u32[]{:S(2)}) async-start(bf16[128,64,128]{2,1,0:T(8,128)(2,1)} %bitcast.118), calls=%async_computation.2 | async-start | bytes 4194304 | tf_op jit(solution)/shard_map/all_to_all | solution.py:442
  86.2 10.8 %freq_rows2.1.freq_part_hbm = f32[3328,128]{1,0:T(8,128)} custom-call(s32[19968]{0:T(1024)} %reshape.102.ids, bf16[16384,128]{1,0:T(8,128)(2,1)} %table_ref.9), custom_call_target="tpu_custom_call" | custom-call | bytes 27262976 | tf_op jit(solution)/shard_map/freq_rows2/pallas_call | solution.py:413
  97.0 17.9 %micro0.1 = (bf16[128,64,128]{2,1,0:T(8,128)(2,1)}, f32[3328,128]{1,0:T(8,128)}, bf16[128,3456]{1,0:T(8,128)(2,1)}, bf16[128,512]{1,0:T(8,128)(2,1)}, bf16[128,5...) custom-call(s32[12288]{0:T(1024)} %bitcast.123, f32[1]{0:T(128)} %bitcast.114.out_b, ...), custom_call_target="tpu_custom_call" | custom-call | flops 1358954496 | bytes 62914560 | tf_op jit(solution)/shard_map/micro0/pallas_call | solution.py:479
  115.5 17.9 %micro1.1 = (bf16[128,64,128]{2,1,0:T(8,128)(2,1)}, f32[3328,128]{1,0:T(8,128)}, bf16[128,3456]{1,0:T(8,128)(2,1)}, bf16[128,512]{1,0:T(8,128)(2,1)}, bf16[128,5...) custom-call(s32[12288]{0:T(1024)} %bitcast.124, ...), custom_call_target="tpu_custom_call", output_to_operand_aliasing={{0}: (10, {})} | custom-call | flops 1358954496 | bytes 62914560 | tf_op jit(solution)/shard_map/micro1/pallas_call | solution.py:479
  133.4 9.7 %all-to-all-start.3 = ((bf16[128,64,128]{2,1,0:T(8,128)(2,1)}), bf16[128,64,128]{2,1,0:T(8,128)(2,1)}, u32[]{:S(2)}, u32[]{:S(2)}) async-start(bf16[128,64,128]{2,1,0:T(8,128)(2,1)} %get-tuple-element.99), calls=%async_computation.3 | async-start | bytes 4194304 | tf_op jit(solution)/shard_map/all_to_all | solution.py:442
  143.4 17.8 %micro2.1 = (bf16[128,32,128]{2,1,0:T(8,128)(2,1)}, f32[3328,128]{1,0:T(8,128)}, bf16[128,3456]{1,0:T(8,128)(2,1)}, bf16[128,512]{1,0:T(8,128)(2,1)}, bf16[128,5...) custom-call(s32[12288]{0:T(1024)} %bitcast.125, f32[1]{0:T(128)} %bitcast.116.out_b, ...), custom_call_target="tpu_custom_call" | custom-call | flops 1358954496 | bytes 62914560 | tf_op jit(solution)/shard_map/micro2/pallas_call | solution.py:479
  161.3 0.8 add_add_fusion
  162.4 1.1 pad.9.columns
  163.4 10.4 %dense_grads.1 = bf16[8,16,32,1024]{3,2,1,0:T(8,128)(2,1)} custom-call(f32[128,16,128]{2,1,0:T(8,128)} %pad.9.columns, bf16[128,3456]{1,0:T(8,128)(2,1)} %get-tuple-element.86.x0, bf16[128,3456]{1,0:T(8,128)(2,1)} %get-tuple-element.87.x1, bf16[128,3456]{1,0:T(8,128)(2,1)} %get-tuple-element.88.x2, bf16[128,3456]{1,0:T(8,128)(2,1)} %get-tuple-element.89.g0, ...), custom_call_target="tpu_custom_call" | custom-call | flops 2717908992 | bytes 41943040 | tf_op jit(solution)/shard_map/dense_grads/pallas_call | solution.py:542
  173.9 10.1 %all-to-all-start.4 = ((bf16[128,32,128]{2,1,0:T(8,128)(2,1)}), bf16[128,32,128]{2,1,0:T(8,128)(2,1)S(1)}, u32[]{:S(2)}, u32[]{:S(2)}) async-start(bf16[128,32,128]{2,1,0:T(8,128)(2,1)} %get-tuple-element.107), calls=%async_computation.4 | async-start | bytes 2097152 | tf_op jit(solution)/shard_map/all_to_all | solution.py:442
  184.0 28.1 %freq_grads.1 = (bf16[64,128,128]{2,1,0:T(8,128)(2,1)}, bf16[64,128,128]{2,1,0:T(8,128)(2,1)}) custom-call(s32[1]{0:T(128)} %bitcast.core, s32[19968]{0:T(1024)} %reshape.102.ids, f32[3328,128]{1,0:T(8,128)} %get-tuple-element.102.d0, f32[3328,128]{1,0:T(8,128)} %get-tuple-element.103.d1, f32[3328,128]{1,0:T(8,128)} %get-tuple-element.104.d2), custom_call_target="tpu_custom_call" | custom-call | bytes 125829120 | tf_op jit(solution)/shard_map/freq_grads/pallas_call | solution.py:567
  212.1 1.0 collective-permute-start
  213.2 4.0 %collective-permute-done = bf16[64,128,128]{2,1,0:T(8,128)(2,1)S(1)} collective-permute-done((bf16[64,128,128]{2,1,0:T(8,128)(2,1)}, bf16[64,128,128]{2,1,0:T(8,128)(2,1)S(1)}, u32[]{:S(2)}, u32[]{:S(2)}) %collective-permute-start) | collective-permute-done | bytes 2097184 | tf_op jit(solution)/shard_map/ppermute | solution.py:580
  217.2 3.8 %add_convert_fusion = bf16[64,128,128]{2,1,0:T(8,128)(2,1)} fusion(bf16[64,128,128]{2,1,0:T(8,128)(2,1)S(1)} %collective-permute-done, bf16[64,128,128]{2,1,0:T(8,128)(2,1)} %get-tuple-element.105), kind=kLoop, calls=%fused_computation | loop fusion | flops 4194304 | bytes 6291456 | tf_op jit(solution)/shard_map/convert_element_type | solution.py:581
  221.0 10.6 %all-to-all-start.5 = ((bf16[64,128,128]{2,1,0:T(8,128)(2,1)}), bf16[64,128,128]{2,1,0:T(8,128)(2,1)}, u32[]{:S(2)}, u32[]{:S(2)}) async-start(bf16[64,128,128]{2,1,0:T(8,128)(2,1)} %add_convert_fusion), calls=%async_computation.5 | async-start | bytes 4194304 | tf_op jit(solution)/shard_map/all_to_all | solution.py:582
  231.6 17.0 %owner_grads.1 = bf16[4096,128]{1,0:T(8,128)(2,1)} custom-call(s32[16384]{0:T(1024)} %bitcast.127, bf16[128,64,128]{2,1,0:T(8,128)(2,1)} %bitcast.29.first, bf16[128,32,128]{2,1,0:T(8,128)(2,1)} %copy-done), custom_call_target="tpu_custom_call" | custom-call | bytes 62914560 | tf_op jit(solution)/shard_map/owner_grads/pallas_call | solution.py:585
  248.7 10.4 %all-to-all-done.5.parts = bf16[64,128,128]{2,1,0:T(8,128)(2,1)} async-done(((bf16[64,128,128]{2,1,0:T(8,128)(2,1)}), bf16[64,128,128]{2,1,0:T(8,128)(2,1)}, u32[]{:S(2)}, u32[]{:S(2)}) %all-to-all-start.5) | async-done | bytes 2097184 | tf_op jit(solution)/shard_map/all_to_all | solution.py:582
  259.1 2.7 spread.1
  261.8 14.9 %all_to_all.39 = bf16[16,128,128]{2,1,0:T(8,128)(2,1)} all-to-all(bf16[16,128,128]{2,1,0:T(8,128)(2,1)} %spread.1), channel_id=1, replica_groups={{0,8,16,24,32,40,48,56,64,72,80,88,96,104,112,120},{1,9,17,25,33,41,49,..., dimensions={0} | all-to-all | bytes 1048576 | tf_op jit(solution)/shard_map/all_to_all | solution.py:611
  276.7 1.2 dynamic-slice_bitcast_fusion.2
  278.3 2.5 collective-permute-start.2
  280.7 1.1 collective-permute-start.3
  281.9 2.6 collective-permute-done.1
  284.4 6.1 %collective-permute-done.2 = bf16[4,32,1024]{2,1,0:T(8,128)(2,1)S(1)} collective-permute-done((bf16[4,32,1024]{2,1,0:T(8,128)(2,1)S(1)}, bf16[4,32,1024]{2,1,0:T(8,128)(2,1)S(1)}, u32[]{:S(2)}, u32[]{:S(2)}) %collective-permute-start.2) | collective-permute-done | bytes 262176 | tf_op jit(solution)/shard_map/ppermute | solution.py:438
  290.9 1.1 fusion.2
  292.1 1.4 collective-permute-start.4
  293.5 2.9 collective-permute-start.5
  296.4 0.9 collective-permute-done.4
  297.2 1.5 collective-permute-done.5
  298.8 1.1 collective-permute-done.6
  300.4 0.7 slice_bitcast_fusion
  301.1 7.7 %all-gather.2.cloned.1.call-done = bf16[16384,128]{1,0:T(8,128)(2,1)} async-done(((bf16[2048,128]{1,0:T(8,128)(2,1)}), bf16[16384,128]{1,0:T(8,128)(2,1)}) %all-gather.2.cloned.1.call-update) | async-done | bytes 4194320 | tf_op jit(solution)/shard_map/all_gather | solution.py:620
  308.8 3.7 %copy.56 = bf16[16384,128]{1,0:T(8,128)(2,1)} copy(bf16[16384,128]{1,0:T(8,128)(2,1)} %all-gather.2.cloned.1.call-done) | data formatting | bytes 8388608
  (38 shorter events, 2.6 us)
Async XLA Ops:
  8.7 23.9 %all-to-all-start = ((s32[128,1,128]{2,1,0:T(1,128)}), s32[128,1,128]{2,1,0:T(1,128)S(1)}, u32[]{:S(2)}, u32[]{:S(2)}) async-start(s32[128,1,128]{2,1,0:T(1,128)} %copy.44), calls=%async_computation | async-start | bytes 131072 | tf_op jit(solution)/shard_map/all_to_all | solution.py:410
  32.6 7.7 %copy-start.2 = (s32[128,1,128]{2,1,0:T(1,128)}, s32[128,1,128]{2,1,0:T(1,128)S(1)}, u32[]{:S(2)}) copy-start(s32[128,1,128]{2,1,0:T(1,128)S(1)} %all-to-all-done) | copy-start | bytes 196612
  33.3 16.8 %copy-start.7 = (f32[3456]{0:T(1024)S(1)}, f32[3456]{0:T(1024)}, u32[]{:S(2)}) copy-start(f32[3456]{0:T(1024)} %param.21) | copy-start | bytes 41476
  33.3 17.4 %copy-start.8 = (bf16[3456]{0:T(1024)(128)(2,1)S(1)}, bf16[3456]{0:T(1024)(128)(2,1)}, u32[]{:S(2)}) copy-start(bf16[3456]{0:T(1024)(128)(2,1)} %param.22) | copy-start | bytes 20740
  33.3 18.0 %copy-start.9 = (s32[3,128]{1,0:T(4,128)S(1)}, s32[3,128]{1,0:T(4,128)}, u32[]{:S(2)}) copy-start(s32[3,128]{1,0:T(4,128)} %param.13) | copy-start | bytes 4612
  33.3 18.6 %copy-start.3 = (s32[3,1,128,32]{2,3,1,0:T(8,128)S(1)}, s32[3,1,128,32]{2,3,1,0:T(8,128)}, u32[]{:S(2)}) copy-start(s32[3,1,128,32]{2,3,1,0:T(8,128)} %param.16) | copy-start | bytes 147460
  33.3 18.6 %copy-start.4 = (s32[3,1,128,32]{2,3,1,0:T(8,128)S(1)}, s32[3,1,128,32]{2,3,1,0:T(8,128)}, u32[]{:S(2)}) copy-start(s32[3,1,128,32]{2,3,1,0:T(8,128)} %param.15) | copy-start | bytes 147460
  40.3 33.7 %all-to-all-start.1 = ((bf16[128,32,128]{2,1,0:T(8,128)(2,1)}), bf16[128,32,128]{2,1,0:T(8,128)(2,1)S(1)}, u32[]{:S(2)}, u32[]{:S(2)}) async-start(bf16[128,32,128]{2,1,0:T(8,128)(2,1)} %bitcast.119), calls=%async_computation.1 | async-start | bytes 2097152 | tf_op jit(solution)/shard_map/all_to_all | solution.py:442
  74.0 1.0 copy-start.1
  74.9 40.6 %all-to-all-start.2 = ((bf16[128,64,128]{2,1,0:T(8,128)(2,1)}), bf16[128,64,128]{2,1,0:T(8,128)(2,1)}, u32[]{:S(2)}, u32[]{:S(2)}) async-start(bf16[128,64,128]{2,1,0:T(8,128)(2,1)} %bitcast.118), calls=%async_computation.2 | async-start | bytes 4194304 | tf_op jit(solution)/shard_map/all_to_all | solution.py:442
  133.4 40.4 %all-to-all-start.3 = ((bf16[128,64,128]{2,1,0:T(8,128)(2,1)}), bf16[128,64,128]{2,1,0:T(8,128)(2,1)}, u32[]{:S(2)}, u32[]{:S(2)}) async-start(bf16[128,64,128]{2,1,0:T(8,128)(2,1)} %get-tuple-element.99), calls=%async_computation.3 | async-start | bytes 4194304 | tf_op jit(solution)/shard_map/all_to_all | solution.py:442
  143.1 133.5 %reduce-scatter.2.cloned.1.call-start = ((), (), s32[]{:S(2)}) async-start(), calls=%async_computation.8 | async-start | bytes 9437184 | tf_op jit(solution)/shard_map/reduce_scatter | solution.py:566
  143.4 17.9 %copy-start.5 = (f32[2,3456]{1,0:T(2,128)S(1)}, f32[2,3456]{1,0:T(2,128)}, u32[]{:S(2)}) copy-start(f32[2,3456]{1,0:T(2,128)} %get-tuple-element.77) | copy-start | bytes 82948
  143.4 17.9 %copy-start.6 = (f32[2,3456]{1,0:T(2,128)S(1)}, f32[2,3456]{1,0:T(2,128)}, u32[]{:S(2)}) copy-start(f32[2,3456]{1,0:T(2,128)} %get-tuple-element.82) | copy-start | bytes 82948
  173.9 38.3 %all-to-all-start.4 = ((bf16[128,32,128]{2,1,0:T(8,128)(2,1)}), bf16[128,32,128]{2,1,0:T(8,128)(2,1)S(1)}, u32[]{:S(2)}, u32[]{:S(2)}) async-start(bf16[128,32,128]{2,1,0:T(8,128)(2,1)} %get-tuple-element.107), calls=%async_computation.4 | async-start | bytes 2097152 | tf_op jit(solution)/shard_map/all_to_all | solution.py:442
  212.1 8.8 %copy-start = (bf16[128,32,128]{2,1,0:T(8,128)(2,1)}, bf16[128,32,128]{2,1,0:T(8,128)(2,1)S(1)}, u32[]{:S(2)}) copy-start(bf16[128,32,128]{2,1,0:T(8,128)(2,1)S(1)} %all-to-all-done.4) | copy-start | bytes 3145732
  212.1 5.0 %collective-permute-start = (bf16[64,128,128]{2,1,0:T(8,128)(2,1)}, bf16[64,128,128]{2,1,0:T(8,128)(2,1)S(1)}, u32[]{:S(2)}, u32[]{:S(2)}) collective-permute-start(bf16[64,128,128]{2,1,0:T(8,128)(2,1)} %get-tuple-element.108), channel_id=1, source_target_pairs={{0,1},{1,0},{2,3},{3,2},{4,5},{5,4},{6,7},{7,6},{8,9},{9,8},{10,11... | collective-permute-start | bytes 6291464 | tf_op jit(solution)/shard_map/ppermute | solution.py:580
  221.0 38.1 %all-to-all-start.5 = ((bf16[64,128,128]{2,1,0:T(8,128)(2,1)}), bf16[64,128,128]{2,1,0:T(8,128)(2,1)}, u32[]{:S(2)}, u32[]{:S(2)}) async-start(bf16[64,128,128]{2,1,0:T(8,128)(2,1)} %add_convert_fusion), calls=%async_computation.5 | async-start | bytes 4194304 | tf_op jit(solution)/shard_map/all_to_all | solution.py:582
  231.6 77.2 %all-gather.2.cloned.1.call-start = ((), (), s32[]{:S(2)}) async-start(), calls=%async_computation.9 | async-start | bytes 4718592 | tf_op jit(solution)/shard_map/all_gather | solution.py:620
  277.9 6.5 %collective-permute-start.1 = (bf16[4,32,1024]{2,1,0:T(8,128)(2,1)S(1)}, bf16[4,32,1024]{2,1,0:T(8,128)(2,1)S(1)}, u32[]{:S(2)}, u32[]{:S(2)}) collective-permute-start(bf16[4,32,1024]{2,1,0:T(8,128)(2,1)S(1)} %get-tuple-element.116), channel_id=1, source_target_pairs={{0,8},{1,9},{2,10},{3,11},{4,12},{5,13},{6,14},{7,15},{8,16},{9,17... | collective-permute-start | bytes 786440 | tf_op jit(solution)/shard_map/ppermute | solution.py:438
  278.3 12.2 %collective-permute-start.2 = (bf16[4,32,1024]{2,1,0:T(8,128)(2,1)S(1)}, bf16[4,32,1024]{2,1,0:T(8,128)(2,1)S(1)}, u32[]{:S(2)}, u32[]{:S(2)}) collective-permute-start(bf16[4,32,1024]{2,1,0:T(8,128)(2,1)S(1)} %get-tuple-element.118), channel_id=1, source_target_pairs={{0,16},{1,17},{2,18},{3,19},{4,20},{5,21},{6,22},{7,23},{8,24},{9,... | collective-permute-start | bytes 786440 | tf_op jit(solution)/shard_map/ppermute | solution.py:438
  280.7 10.2 %collective-permute-start.3 = (bf16[4,32,1024]{2,1,0:T(8,128)(2,1)S(1)}, bf16[4,32,1024]{2,1,0:T(8,128)(2,1)S(1)}, u32[]{:S(2)}, u32[]{:S(2)}) collective-permute-start(bf16[4,32,1024]{2,1,0:T(8,128)(2,1)S(1)} %get-tuple-element.117), channel_id=1, source_target_pairs={{0,24},{1,25},{2,26},{3,27},{4,28},{5,29},{6,30},{7,31},{8,0},{9,1... | collective-permute-start | bytes 786440 | tf_op jit(solution)/shard_map/ppermute | solution.py:438
  292.1 5.1 %collective-permute-start.4 = (bf16[32,1024]{1,0:T(8,128)(2,1)S(1)}, bf16[32,1024]{1,0:T(8,128)(2,1)S(1)}, u32[]{:S(2)}, u32[]{:S(2)}) collective-permute-start(bf16[32,1024]{1,0:T(8,128)(2,1)S(1)} %get-tuple-element.119), channel_id=1, source_target_pairs={{0,32},{1,33},{2,34},{3,35},{4,36},{5,37},{6,38},{7,39},{8,40},{9,... | collective-permute-start | bytes 196616 | tf_op jit(solution)/shard_map/ppermute | solution.py:438
  293.5 5.3 %collective-permute-start.5 = (bf16[32,1024]{1,0:T(8,128)(2,1)S(1)}, bf16[32,1024]{1,0:T(8,128)(2,1)S(1)}, u32[]{:S(2)}, u32[]{:S(2)}) collective-permute-start(bf16[32,1024]{1,0:T(8,128)(2,1)S(1)} %get-tuple-element.121), channel_id=1, source_target_pairs={{0,64},{1,65},{2,66},{3,67},{4,68},{5,69},{6,70},{7,71},{8,72},{9,... | collective-permute-start | bytes 196616 | tf_op jit(solution)/shard_map/ppermute | solution.py:438
  296.4 3.5 %collective-permute-start.6 = (bf16[32,1024]{1,0:T(8,128)(2,1)S(1)}, bf16[32,1024]{1,0:T(8,128)(2,1)S(1)}, u32[]{:S(2)}, u32[]{:S(2)}) collective-permute-start(bf16[32,1024]{1,0:T(8,128)(2,1)S(1)} %get-tuple-element.120), channel_id=1, source_target_pairs={{0,96},{1,97},{2,98},{3,99},{4,100},{5,101},{6,102},{7,103},{8,104... | collective-permute-start | bytes 196616 | tf_op jit(solution)/shard_map/ppermute | solution.py:438
Sparse Core Ops, SparseCore 0:
  174.0 84.8 reduce-scatter.1
  276.8 31.9 all-gather.1

commit v8 on v7

--- a/solution.py
+++ b/solution.py
@@ -338,13 +338,13 @@
         out[k] = total
 
 
-def owner_kernel(peers, stride, cap, asked, first, last, out, rows, *accs):
+def owner_kernel(peers, stride, cap, asked, arrived, out, rows, *accs):
     ways = len(accs)
     for a in accs:
         a[...] = jnp.zeros_like(a)
     emb = out.shape[1]
     for m in range(3):
-        part = last[...] if m == 2 else first[:, m * cap : (m + 1) * cap, :]
+        part = arrived[:, m * cap : (m + 1) * cap, :]
         rows[...] = part.astype(f32).reshape(peers * cap, emb)
 
         def peer(d, carry):
@@ -485,11 +485,11 @@
                 m,
                 m * n_req,
                 max(m - 1, 0) * cap,
-                cap if m == 1 else 0,
+                m * cap,
                 loss_mult,
             ),
             [
-                ((devices, cap if m == 2 else 2 * cap, emb), bf16),
+                ((devices, micro * cap, emb), bf16),
                 ((n_slots, emb), f32),
                 ((samples, width), bf16),
                 ((samples, rank), bf16),
@@ -497,7 +497,7 @@
                 ((samples, width), bf16),
                 ((2, width), f32),
             ],
-            [SMEM, SMEM, HBM, HBM, VMEM, VMEM, HBM, HBM, VMEM, VMEM] + ([HBM] if m == 1 else []),
+            [SMEM, SMEM, HBM, HBM, VMEM, VMEM, HBM, HBM, VMEM, VMEM] + ([HBM] if m else []),
             [pltpu.VMEM((n_req, emb), f32)]
             + [pltpu.VMEM((n_slots + 8, emb), f32)] * 8
             + [pltpu.VMEM((samples, width), f32)]
@@ -511,7 +511,7 @@
             6 * samples * width * rank,
             60 * MIB,
             [HBM] * 6 + [VMEM],
-            {10: 0} if m == 1 else {},
+            {10: 0} if m else {},
         )(
             place,
             bias_b,
@@ -523,14 +523,12 @@
             cross_v,
             bias,
             weight,
-            *([outs[0][0]] if m == 1 else []),
+            *([outs[m - 1][0]] if m else []),
         )
         outs.append(list(out))
         if m == 1:
             place, outs[1][6] = lax.optimization_barrier((place, outs[1][6]))
-    arrived_first = exchange(outs[1][0], 2 * cap)
-    outs[2][0], arrived_first = lax.optimization_barrier((outs[2][0], arrived_first))
-    arrived_last = exchange(outs[2][0], cap)
+    arrived = exchange(outs[2][0], micro * cap)
     d_pooled = [o[1] for o in outs]
     grad_bw = ((outs[0][6] + outs[1][6]) + outs[2][6]).reshape(2, devices, per)
     columns = jnp.pad(
@@ -560,7 +558,7 @@
         *[o[3] for o in outs],
         *[o[4] for o in outs],
     )
-    core, dense, arrived_first = lax.optimization_barrier((core, dense, arrived_first))
+    core, dense = lax.optimization_barrier((core, dense))
     dense = dense.reshape(devices, rows_pad, 2 * rank)
     near = [list(range(d, d + 8)) for d in range(0, devices, 8)]
     dense = lax.psum_scatter(dense, "dev", axis_index_groups=near, tiled=True)
@@ -576,16 +574,16 @@
         0,
         120 * MIB,
     )(core, ids, *d_pooled)
-    send_f, arrived_last = lax.optimization_barrier((send_f, arrived_last))
     got = lax.ppermute(send_f, "dev", other_core)
     both = (keep_f.astype(f32) + got.astype(f32)).astype(bf16)
+    both, arrived = lax.optimization_barrier((both, arrived))
     parts = lax.all_to_all(
         both, "dev", split_axis=0, concat_axis=0, axis_index_groups=same_core, tiled=True
     )
     (grad_inf,) = local_call(
         functools.partial(owner_kernel, devices, stride, cap),
         [((owned, emb), bf16)],
-        [SMEM, VMEM, VMEM],
+        [SMEM, VMEM],
         [pltpu.VMEM((n_req, emb), f32)] + [pltpu.VMEM((owned + 8, emb), f32)] * 8,
         "owner_grads",
         62,
@@ -593,8 +591,7 @@
         60 * MIB,
     )(
         asked,
-        arrived_first.reshape(devices, 2 * cap, emb),
-        arrived_last.reshape(devices, cap, emb),
+        arrived.reshape(devices, micro * cap, emb),
     )
 
     parts, grad_inf = lax.optimization_barrier((parts, grad_inf))

time: 325 us -> 325 us (level)
  starting transfers between devices: 71.8 us -> 58.7 us
  waiting for transfers between devices: 35.3 us -> 47.8 us
    all_to_all x4 -> x3, starting transfers between devices: 40.1 us -> 30 us  [exchange(): lax.all_to_all(rows.reshape(devices, count, emb), 'dev', split_axis=0, co...]
    reduce_scatter x1, waiting for transfers between devices: 0.01 us -> 7.11 us  [on_device(): dense = lax.psum_scatter(dense, 'dev', axis_index_groups=near, tiled=True)]
    all_to_all x4 -> x3, waiting for transfers between devices: 0.58 us -> 5.19 us  [exchange(): lax.all_to_all(rows.reshape(devices, count, emb), 'dev', split_axis=0, co...]
    all_to_all x1, starting transfers between devices: 10.6 us -> 6.76 us  [on_device(): lax.all_to_all(both, 'dev', split_axis=0, concat_axis=0, axis_index_group...]
  transfers between devices with their start and end apart: 15 -> 14, of which waited for: 10 -> 11; matrix products, arithmetic and copies ran while one was open for 4% -> 4% of each run, Pallas kernels for 43% -> 34%
where the time goes in v8:
time: 325 us; the launch traced here: 319 us
  Pallas kernels  162 us (50%)
  starting transfers between devices  58.7 us (18%)
  waiting for transfers between devices  47.8 us (15%)
  between operations  15.4 us (5%)
  blocking collectives  14.6 us (4%)
  local copies, waits for them, and re-layouts  12 us (4%)
  other arithmetic  8.44 us (3%)
    pallas_call x3, Pallas kernels, on_device(): local_call(functools.partial(micro_kernel, devices, cap, features, m, m *...  53.9 us
    pallas_call x3, Pallas kernels, freq_rows_of(): local_call(functools.partial(freq_kernel, features, samples, first_micro)...  32.8 us
    all_to_all x3, starting transfers between devices, exchange(): lax.all_to_all(rows.reshape(devices, count, emb), 'dev', split_axis=0, co...  30 us
    pallas_call x1, Pallas kernels, on_device(): local_call(functools.partial(freq_grad_kernel, features), [((devices // 2...  28 us
    pallas_call x2, Pallas kernels, lookup(): local_call(functools.partial(lookup_kernel, devices, stride, start, count...  17.5 us
    pallas_call x1, Pallas kernels, on_device(): local_call(functools.partial(owner_kernel, devices, stride, cap), [((owne...  17.1 us
    all_to_all x1, blocking collectives, on_device(): lax.all_to_all(spread, 'dev', split_axis=0, concat_axis=0, axis_index_gro...  14.6 us
    ppermute x6, waiting for transfers between devices, axis_sum(): total = total + lax.ppermute(block, 'dev', to).astype(f32)  14.4 us
  transfers between devices with their start and end apart: 14, of which 11 were waited for; matrix products, arithmetic and copies ran while one was open for 4% of the time, Pallas kernels for 34%

profile of v8, /device:TPU:1, one launch (start us, length us, event | category | flops | bytes accessed | tf_op | source)
XLA Modules:
  0.0 319.3 jit_solution(4107106189729372942)
XLA Ops:
  7.2 0.8 bitcast_select_fusion
  8.0 0.7 copy.45
  8.7 11.5 %all-to-all-start = ((s32[128,1,128]{2,1,0:T(1,128)}), s32[128,1,128]{2,1,0:T(1,128)S(1)}, u32[]{:S(2)}, u32[]{:S(2)}) async-start(s32[128,1,128]{2,1,0:T(1,128)} %copy.45), calls=%async_computation | async-start | bytes 131072 | tf_op jit(solution)/shard_map/all_to_all | solution.py:410
  20.3 1.6 reshape.96.ids
  21.8 10.9 %freq_rows0.1.freq_part_hbm = f32[3328,128]{1,0:T(8,128)} custom-call(s32[19968]{0:T(1024)} %reshape.96.ids, bf16[16384,128]{1,0:T(8,128)(2,1)} %table_ref.9), custom_call_target="tpu_custom_call" | custom-call | bytes 27262976 | tf_op jit(solution)/shard_map/freq_rows0/pallas_call | solution.py:413
  32.8 0.6 broadcast_minimum_fusion.asked
  33.4 7.0 %lookup0.1 = bf16[4096,128]{1,0:T(8,128)(2,1)} custom-call(s32[16384]{0:T(1024)} %broadcast_minimum_fusion.asked, bf16[4096,128]{1,0:T(8,128)(2,1)} %table_ref.7), custom_call_target="tpu_custom_call" | custom-call | bytes 20971520 | tf_op jit(solution)/shard_map/lookup0/pallas_call | solution.py:449
  40.4 9.8 %all-to-all-start.1 = ((bf16[128,32,128]{2,1,0:T(8,128)(2,1)}), bf16[128,32,128]{2,1,0:T(8,128)(2,1)S(1)}, u32[]{:S(2)}, u32[]{:S(2)}) async-start(bf16[128,32,128]{2,1,0:T(8,128)(2,1)} %bitcast.117), calls=%async_computation.1 | async-start | bytes 2097152 | tf_op jit(solution)/shard_map/all_to_all | solution.py:442
  50.2 0.6 reshape.104.bias
  50.8 0.6 reshape.117.weight
  52.0 0.7 fusion.7
  52.7 10.6 %lookup32.1 = bf16[8192,128]{1,0:T(8,128)(2,1)} custom-call(s32[16384]{0:T(1024)} %broadcast_minimum_fusion.asked, bf16[4096,128]{1,0:T(8,128)(2,1)} %table_ref.7), custom_call_target="tpu_custom_call" | custom-call | bytes 41943040 | tf_op jit(solution)/shard_map/lookup32/pallas_call | solution.py:449
  63.3 10.8 %freq_rows1.1.freq_part_hbm = f32[3328,128]{1,0:T(8,128)} custom-call(s32[19968]{0:T(1024)} %reshape.96.ids, bf16[16384,128]{1,0:T(8,128)(2,1)} %table_ref.9), custom_call_target="tpu_custom_call" | custom-call | bytes 27262976 | tf_op jit(solution)/shard_map/freq_rows1/pallas_call | solution.py:413
  74.1 1.0 copy-done
  75.1 10.2 %all-to-all-start.2 = ((bf16[128,64,128]{2,1,0:T(8,128)(2,1)}), bf16[128,64,128]{2,1,0:T(8,128)(2,1)}, u32[]{:S(2)}, u32[]{:S(2)}) async-start(bf16[128,64,128]{2,1,0:T(8,128)(2,1)} %bitcast.116), calls=%async_computation.2 | async-start | bytes 4194304 | tf_op jit(solution)/shard_map/all_to_all | solution.py:442
  86.0 11.0 %freq_rows2.1.freq_part_hbm = f32[3328,128]{1,0:T(8,128)} custom-call(s32[19968]{0:T(1024)} %reshape.96.ids, bf16[16384,128]{1,0:T(8,128)(2,1)} %table_ref.9), custom_call_target="tpu_custom_call" | custom-call | bytes 27262976 | tf_op jit(solution)/shard_map/freq_rows2/pallas_call | solution.py:413
  97.0 17.8 %micro0.1 = (bf16[128,96,128]{2,1,0:T(8,128)(2,1)}, f32[3328,128]{1,0:T(8,128)}, bf16[128,3456]{1,0:T(8,128)(2,1)}, bf16[128,512]{1,0:T(8,128)(2,1)}, bf16[128,5...) custom-call(s32[12288]{0:T(1024)} %bitcast.121, f32[1]{0:T(128)} %bitcast.112.out_b, ...), custom_call_target="tpu_custom_call" | custom-call | flops 1358954496 | bytes 62914560 | tf_op jit(solution)/shard_map/micro0/pallas_call | solution.py:479
  115.4 17.9 %micro1.1 = (bf16[128,96,128]{2,1,0:T(8,128)(2,1)}, f32[3328,128]{1,0:T(8,128)}, bf16[128,3456]{1,0:T(8,128)(2,1)}, bf16[128,512]{1,0:T(8,128)(2,1)}, bf16[128,5...) custom-call(s32[12288]{0:T(1024)} %bitcast.122, ...), custom_call_target="tpu_custom_call", output_to_operand_aliasing={{0}: (10, {})} | custom-call | flops 1358954496 | bytes 62914560 | tf_op jit(solution)/shard_map/micro1/pallas_call | solution.py:479
  133.4 18.1 %micro2.1 = (bf16[128,96,128]{2,1,0:T(8,128)(2,1)}, f32[3328,128]{1,0:T(8,128)}, bf16[128,3456]{1,0:T(8,128)(2,1)}, bf16[128,512]{1,0:T(8,128)(2,1)}, bf16[128,5...) custom-call(s32[12288]{0:T(1024)} %bitcast.123, ...), custom_call_target="tpu_custom_call", output_to_operand_aliasing={{0}: (10, {})} | custom-call | flops 1358954496 | bytes 62914560 | tf_op jit(solution)/shard_map/micro2/pallas_call | solution.py:479
  151.5 0.8 add_add_fusion
  152.6 1.1 pad.9.columns
  153.7 10.3 %dense_grads.1 = bf16[8,16,32,1024]{3,2,1,0:T(8,128)(2,1)} custom-call(f32[128,16,128]{2,1,0:T(8,128)} %pad.9.columns, bf16[128,3456]{1,0:T(8,128)(2,1)} %get-tuple-element.84.x0, bf16[128,3456]{1,0:T(8,128)(2,1)} %get-tuple-element.85.x1, bf16[128,3456]{1,0:T(8,128)(2,1)} %get-tuple-element.86.x2, bf16[128,3456]{1,0:T(8,128)(2,1)} %get-tuple-element.87.g0, ...), custom_call_target="tpu_custom_call" | custom-call | flops 2717908992 | bytes 41943040 | tf_op jit(solution)/shard_map/dense_grads/pallas_call | solution.py:540
  164.1 10.0 %all-to-all-start.3 = ((bf16[128,96,128]{2,1,0:T(8,128)(2,1)}), bf16[128,96,128]{2,1,0:T(8,128)(2,1)}, u32[]{:S(2)}, u32[]{:S(2)}) async-start(bf16[128,96,128]{2,1,0:T(8,128)(2,1)} %get-tuple-element.102), calls=%async_computation.3 | async-start | bytes 6291456 | tf_op jit(solution)/shard_map/all_to_all | solution.py:442
  174.1 28.0 %freq_grads.1 = (bf16[64,128,128]{2,1,0:T(8,128)(2,1)}, bf16[64,128,128]{2,1,0:T(8,128)(2,1)}) custom-call(s32[1]{0:T(128)} %bitcast.core, s32[19968]{0:T(1024)} %reshape.96.ids, f32[3328,128]{1,0:T(8,128)} %get-tuple-element.97.d0, f32[3328,128]{1,0:T(8,128)} %get-tuple-element.98.d1, f32[3328,128]{1,0:T(8,128)} %get-tuple-element.99.d2), custom_call_target="tpu_custom_call" | custom-call | bytes 125829120 | tf_op jit(solution)/shard_map/freq_grads/pallas_call | solution.py:565
  202.1 1.0 collective-permute-start
  203.2 4.0 %collective-permute-done = bf16[64,128,128]{2,1,0:T(8,128)(2,1)S(1)} collective-permute-done((bf16[64,128,128]{2,1,0:T(8,128)(2,1)}, bf16[64,128,128]{2,1,0:T(8,128)(2,1)S(1)}, u32[]{:S(2)}, u32[]{:S(2)}) %collective-permute-start) | collective-permute-done | bytes 2097184 | tf_op jit(solution)/shard_map/ppermute | solution.py:577
  207.2 3.7 %add_convert_fusion = bf16[64,128,128]{2,1,0:T(8,128)(2,1)} fusion(bf16[64,128,128]{2,1,0:T(8,128)(2,1)S(1)} %collective-permute-done, bf16[64,128,128]{2,1,0:T(8,128)(2,1)} %get-tuple-element.100), kind=kLoop, calls=%fused_computation | loop fusion | flops 4194304 | bytes 6291456 | tf_op jit(solution)/shard_map/convert_element_type | solution.py:578
  210.9 4.6 %all-to-all-done.3 = bf16[128,96,128]{2,1,0:T(8,128)(2,1)} async-done(((bf16[128,96,128]{2,1,0:T(8,128)(2,1)}), bf16[128,96,128]{2,1,0:T(8,128)(2,1)}, u32[]{:S(2)}, u32[]{:S(2)}) %all-to-all-start.3) | async-done | bytes 3145760 | tf_op jit(solution)/shard_map/all_to_all | solution.py:442
  215.5 6.8 %all-to-all-start.4 = ((bf16[64,128,128]{2,1,0:T(8,128)(2,1)}), bf16[64,128,128]{2,1,0:T(8,128)(2,1)}, u32[]{:S(2)}, u32[]{:S(2)}) async-start(bf16[64,128,128]{2,1,0:T(8,128)(2,1)} %add_convert_fusion), calls=%async_computation.4 | async-start | bytes 4194304 | tf_op jit(solution)/shard_map/all_to_all | solution.py:580
  222.3 17.1 %owner_grads.1 = bf16[4096,128]{1,0:T(8,128)(2,1)} custom-call(s32[16384]{0:T(1024)} %bitcast.125, bf16[128,96,128]{2,1,0:T(8,128)(2,1)} %bitcast.28.arrived), custom_call_target="tpu_custom_call" | custom-call | bytes 62914560 | tf_op jit(solution)/shard_map/owner_grads/pallas_call | solution.py:583
  239.4 10.3 %all-to-all-done.4.parts = bf16[64,128,128]{2,1,0:T(8,128)(2,1)} async-done(((bf16[64,128,128]{2,1,0:T(8,128)(2,1)}), bf16[64,128,128]{2,1,0:T(8,128)(2,1)}, u32[]{:S(2)}, u32[]{:S(2)}) %all-to-all-start.4) | async-done | bytes 2097184 | tf_op jit(solution)/shard_map/all_to_all | solution.py:580
  249.8 2.7 spread.1
  252.5 14.6 %all_to_all.34 = bf16[16,128,128]{2,1,0:T(8,128)(2,1)} all-to-all(bf16[16,128,128]{2,1,0:T(8,128)(2,1)} %spread.1), channel_id=1, replica_groups={{0,8,16,24,32,40,48,56,64,72,80,88,96,104,112,120},{1,9,17,25,33,41,49,..., dimensions={0} | all-to-all | bytes 1048576 | tf_op jit(solution)/shard_map/all_to_all | solution.py:608
  267.1 7.1 %reduce-scatter.2.cloned.1.call-done = bf16[16,32,1024]{2,1,0:T(8,128)(2,1)} async-done(((bf16[128,32,1024]{2,1,0:T(8,128)(2,1)}), bf16[16,32,1024]{2,1,0:T(8,128)(2,1)}) %reduce-scatter.2.cloned.1.call-update) | async-done | bytes 1048592 | tf_op jit(solution)/shard_map/reduce_scatter | solution.py:564
  274.3 1.2 dynamic-slice_bitcast_fusion.2
  275.5 0.7 collective-permute-start.1
  276.2 3.9 %collective-permute-start.2 = (bf16[4,32,1024]{2,1,0:T(8,128)(2,1)S(1)}, bf16[4,32,1024]{2,1,0:T(8,128)(2,1)S(1)}, u32[]{:S(2)}, u32[]{:S(2)}) collective-permute-start(bf16[4,32,1024]{2,1,0:T(8,128)(2,1)S(1)} %get-tuple-element.112), channel_id=1, source_target_pairs={{0,16},{1,17},{2,18},{3,19},{4,20},{5,21},{6,22},{7,23},{8,24},{9,... | collective-permute-start | bytes 786440 | tf_op jit(solution)/shard_map/ppermute | solution.py:438
  280.1 5.5 %collective-permute-done.1 = bf16[4,32,1024]{2,1,0:T(8,128)(2,1)S(1)} collective-permute-done((bf16[4,32,1024]{2,1,0:T(8,128)(2,1)S(1)}, bf16[4,32,1024]{2,1,0:T(8,128)(2,1)S(1)}, u32[]{:S(2)}, u32[]{:S(2)}) %collective-permute-start.1) | collective-permute-done | bytes 262176 | tf_op jit(solution)/shard_map/ppermute | solution.py:438
  285.6 6.9 %collective-permute-done.2 = bf16[4,32,1024]{2,1,0:T(8,128)(2,1)S(1)} collective-permute-done((bf16[4,32,1024]{2,1,0:T(8,128)(2,1)S(1)}, bf16[4,32,1024]{2,1,0:T(8,128)(2,1)S(1)}, u32[]{:S(2)}, u32[]{:S(2)}) %collective-permute-start.2) | collective-permute-done | bytes 262176 | tf_op jit(solution)/shard_map/ppermute | solution.py:438
  292.5 1.1 fusion.2
  293.7 0.7 collective-permute-start.4
  294.4 2.0 collective-permute-start.5
  296.4 2.0 collective-permute-start.6
  298.5 1.1 collective-permute-done.5
  299.5 0.8 collective-permute-done.6
  300.9 0.7 slice_bitcast_fusion
  301.5 6.7 %all-gather.2.cloned.1.call-done = bf16[16384,128]{1,0:T(8,128)(2,1)} async-done(((bf16[2048,128]{1,0:T(8,128)(2,1)}), bf16[16384,128]{1,0:T(8,128)(2,1)}) %all-gather.2.cloned.1.call-update) | async-done | bytes 4194320 | tf_op jit(solution)/shard_map/all_gather | solution.py:617
  308.3 3.7 %copy.58 = bf16[16384,128]{1,0:T(8,128)(2,1)} copy(bf16[16384,128]{1,0:T(8,128)(2,1)} %all-gather.2.cloned.1.call-done) | data formatting | bytes 8388608
  (34 shorter events, 2.3 us)
Async XLA Ops:
  8.7 24.0 %all-to-all-start = ((s32[128,1,128]{2,1,0:T(1,128)}), s32[128,1,128]{2,1,0:T(1,128)S(1)}, u32[]{:S(2)}, u32[]{:S(2)}) async-start(s32[128,1,128]{2,1,0:T(1,128)} %copy.45), calls=%async_computation | async-start | bytes 131072 | tf_op jit(solution)/shard_map/all_to_all | solution.py:410
  32.8 7.7 %copy-start.1 = (s32[128,1,128]{2,1,0:T(1,128)}, s32[128,1,128]{2,1,0:T(1,128)S(1)}, u32[]{:S(2)}) copy-start(s32[128,1,128]{2,1,0:T(1,128)S(1)} %all-to-all-done) | copy-start | bytes 196612
  33.4 16.8 %copy-start.6 = (f32[3456]{0:T(1024)S(1)}, f32[3456]{0:T(1024)}, u32[]{:S(2)}) copy-start(f32[3456]{0:T(1024)} %param.21) | copy-start | bytes 41476
  33.4 17.4 %copy-start.7 = (bf16[3456]{0:T(1024)(128)(2,1)S(1)}, bf16[3456]{0:T(1024)(128)(2,1)}, u32[]{:S(2)}) copy-start(bf16[3456]{0:T(1024)(128)(2,1)} %param.22) | copy-start | bytes 20740
  33.4 18.0 %copy-start.8 = (s32[3,128]{1,0:T(4,128)S(1)}, s32[3,128]{1,0:T(4,128)}, u32[]{:S(2)}) copy-start(s32[3,128]{1,0:T(4,128)} %param.13) | copy-start | bytes 4612
  33.4 18.6 %copy-start.2 = (s32[3,1,128,32]{2,3,1,0:T(8,128)S(1)}, s32[3,1,128,32]{2,3,1,0:T(8,128)}, u32[]{:S(2)}) copy-start(s32[3,1,128,32]{2,3,1,0:T(8,128)} %param.16) | copy-start | bytes 147460
  33.4 18.6 %copy-start.3 = (s32[3,1,128,32]{2,3,1,0:T(8,128)S(1)}, s32[3,1,128,32]{2,3,1,0:T(8,128)}, u32[]{:S(2)}) copy-start(s32[3,1,128,32]{2,3,1,0:T(8,128)} %param.15) | copy-start | bytes 147460
  40.4 33.7 %all-to-all-start.1 = ((bf16[128,32,128]{2,1,0:T(8,128)(2,1)}), bf16[128,32,128]{2,1,0:T(8,128)(2,1)S(1)}, u32[]{:S(2)}, u32[]{:S(2)}) async-start(bf16[128,32,128]{2,1,0:T(8,128)(2,1)} %bitcast.117), calls=%async_computation.1 | async-start | bytes 2097152 | tf_op jit(solution)/shard_map/all_to_all | solution.py:442
  74.1 1.0 copy-start
  75.1 40.4 %all-to-all-start.2 = ((bf16[128,64,128]{2,1,0:T(8,128)(2,1)}), bf16[128,64,128]{2,1,0:T(8,128)(2,1)}, u32[]{:S(2)}, u32[]{:S(2)}) async-start(bf16[128,64,128]{2,1,0:T(8,128)(2,1)} %bitcast.116), calls=%async_computation.2 | async-start | bytes 4194304 | tf_op jit(solution)/shard_map/all_to_all | solution.py:442
  85.3 188.9 %reduce-scatter.2.cloned.1.call-start = ((), (), s32[]{:S(2)}) async-start(), calls=%async_computation.7 | async-start | bytes 9437184 | tf_op jit(solution)/shard_map/reduce_scatter | solution.py:564
  133.4 18.2 %copy-start.4 = (f32[2,3456]{1,0:T(2,128)S(1)}, f32[2,3456]{1,0:T(2,128)}, u32[]{:S(2)}) copy-start(f32[2,3456]{1,0:T(2,128)} %get-tuple-element.74) | copy-start | bytes 82948
  133.4 18.1 %copy-start.5 = (f32[2,3456]{1,0:T(2,128)S(1)}, f32[2,3456]{1,0:T(2,128)}, u32[]{:S(2)}) copy-start(f32[2,3456]{1,0:T(2,128)} %get-tuple-element.79) | copy-start | bytes 82948
  164.1 51.5 %all-to-all-start.3 = ((bf16[128,96,128]{2,1,0:T(8,128)(2,1)}), bf16[128,96,128]{2,1,0:T(8,128)(2,1)}, u32[]{:S(2)}, u32[]{:S(2)}) async-start(bf16[128,96,128]{2,1,0:T(8,128)(2,1)} %get-tuple-element.102), calls=%async_computation.3 | async-start | bytes 6291456 | tf_op jit(solution)/shard_map/all_to_all | solution.py:442
  202.1 5.0 %collective-permute-start = (bf16[64,128,128]{2,1,0:T(8,128)(2,1)}, bf16[64,128,128]{2,1,0:T(8,128)(2,1)S(1)}, u32[]{:S(2)}, u32[]{:S(2)}) collective-permute-start(bf16[64,128,128]{2,1,0:T(8,128)(2,1)} %get-tuple-element.101), channel_id=1, source_target_pairs={{0,1},{1,0},{2,3},{3,2},{4,5},{5,4},{6,7},{7,6},{8,9},{9,8},{10,11... | collective-permute-start | bytes 6291464 | tf_op jit(solution)/shard_map/ppermute | solution.py:577
  215.5 34.3 %all-to-all-start.4 = ((bf16[64,128,128]{2,1,0:T(8,128)(2,1)}), bf16[64,128,128]{2,1,0:T(8,128)(2,1)}, u32[]{:S(2)}, u32[]{:S(2)}) async-start(bf16[64,128,128]{2,1,0:T(8,128)(2,1)} %add_convert_fusion), calls=%async_computation.4 | async-start | bytes 4194304 | tf_op jit(solution)/shard_map/all_to_all | solution.py:580
  222.3 86.0 %all-gather.2.cloned.1.call-start = ((), (), s32[]{:S(2)}) async-start(), calls=%async_computation.8 | async-start | bytes 4718592 | tf_op jit(solution)/shard_map/all_gather | solution.py:617
  275.5 10.0 %collective-permute-start.1 = (bf16[4,32,1024]{2,1,0:T(8,128)(2,1)S(1)}, bf16[4,32,1024]{2,1,0:T(8,128)(2,1)S(1)}, u32[]{:S(2)}, u32[]{:S(2)}) collective-permute-start(bf16[4,32,1024]{2,1,0:T(8,128)(2,1)S(1)} %get-tuple-element.110), channel_id=1, source_target_pairs={{0,8},{1,9},{2,10},{3,11},{4,12},{5,13},{6,14},{7,15},{8,16},{9,17... | collective-permute-start | bytes 786440 | tf_op jit(solution)/shard_map/ppermute | solution.py:438
  276.2 16.3 %collective-permute-start.2 = (bf16[4,32,1024]{2,1,0:T(8,128)(2,1)S(1)}, bf16[4,32,1024]{2,1,0:T(8,128)(2,1)S(1)}, u32[]{:S(2)}, u32[]{:S(2)}) collective-permute-start(bf16[4,32,1024]{2,1,0:T(8,128)(2,1)S(1)} %get-tuple-element.112), channel_id=1, source_target_pairs={{0,16},{1,17},{2,18},{3,19},{4,20},{5,21},{6,22},{7,23},{8,24},{9,... | collective-permute-start | bytes 786440 | tf_op jit(solution)/shard_map/ppermute | solution.py:438
  280.1 12.4 %collective-permute-start.3 = (bf16[4,32,1024]{2,1,0:T(8,128)(2,1)S(1)}, bf16[4,32,1024]{2,1,0:T(8,128)(2,1)S(1)}, u32[]{:S(2)}, u32[]{:S(2)}) collective-permute-start(bf16[4,32,1024]{2,1,0:T(8,128)(2,1)S(1)} %get-tuple-element.111), channel_id=1, source_target_pairs={{0,24},{1,25},{2,26},{3,27},{4,28},{5,29},{6,30},{7,31},{8,0},{9,1... | collective-permute-start | bytes 786440 | tf_op jit(solution)/shard_map/ppermute | solution.py:438
  293.7 4.8 %collective-permute-start.4 = (bf16[32,1024]{1,0:T(8,128)(2,1)S(1)}, bf16[32,1024]{1,0:T(8,128)(2,1)S(1)}, u32[]{:S(2)}, u32[]{:S(2)}) collective-permute-start(bf16[32,1024]{1,0:T(8,128)(2,1)S(1)} %get-tuple-element.113), channel_id=1, source_target_pairs={{0,32},{1,33},{2,34},{3,35},{4,36},{5,37},{6,38},{7,39},{8,40},{9,... | collective-permute-start | bytes 196616 | tf_op jit(solution)/shard_map/ppermute | solution.py:438
  294.4 5.2 %collective-permute-start.5 = (bf16[32,1024]{1,0:T(8,128)(2,1)S(1)}, bf16[32,1024]{1,0:T(8,128)(2,1)S(1)}, u32[]{:S(2)}, u32[]{:S(2)}) collective-permute-start(bf16[32,1024]{1,0:T(8,128)(2,1)S(1)} %get-tuple-element.115), channel_id=1, source_target_pairs={{0,64},{1,65},{2,66},{3,67},{4,68},{5,69},{6,70},{7,71},{8,72},{9,... | collective-permute-start | bytes 196616 | tf_op jit(solution)/shard_map/ppermute | solution.py:438
  296.4 3.9 %collective-permute-start.6 = (bf16[32,1024]{1,0:T(8,128)(2,1)S(1)}, bf16[32,1024]{1,0:T(8,128)(2,1)S(1)}, u32[]{:S(2)}, u32[]{:S(2)}) collective-permute-start(bf16[32,1024]{1,0:T(8,128)(2,1)S(1)} %get-tuple-element.114), channel_id=1, source_target_pairs={{0,96},{1,97},{2,98},{3,99},{4,100},{5,101},{6,102},{7,103},{8,104... | collective-permute-start | bytes 196616 | tf_op jit(solution)/shard_map/ppermute | solution.py:438
Sparse Core Ops, SparseCore 0:
  164.2 110.0 reduce-scatter.1
  275.9 32.2 all-gather.1

commit v9 on v7

--- a/solution.py
+++ b/solution.py
@@ -338,13 +338,13 @@
         out[k] = total
 
 
-def owner_kernel(peers, stride, cap, asked, first, last, out, rows, *accs):
+def owner_kernel(peers, stride, cap, micros, asked, arrived, before, out, rows, *accs):
     ways = len(accs)
     for a in accs:
         a[...] = jnp.zeros_like(a)
-    emb = out.shape[1]
-    for m in range(3):
-        part = last[...] if m == 2 else first[:, m * cap : (m + 1) * cap, :]
+    owned, emb = out.shape
+    for k, m in enumerate(micros):
+        part = arrived[:, k * cap : (k + 1) * cap, :]
         rows[...] = part.astype(f32).reshape(peers * cap, emb)
 
         def peer(d, carry):
@@ -359,8 +359,14 @@
             return carry
 
         lax.fori_loop(0, peers, peer, 0)
-    at = slice(0, out.shape[0])
-    out[...] = tree_sum([a[at, :] for a in accs]).astype(bf16)
+    total = tree_sum([a[0:owned, :] for a in accs])
+    if before is not None:
+        total = total + before[...]
+    out[...] = total.astype(out.dtype)
+
+
+def first_owner_kernel(peers, stride, cap, micros, asked, arrived, out, rows, *accs):
+    owner_kernel(peers, stride, cap, micros, asked, arrived, None, out, rows, *accs)
 
 
 def on_device(
@@ -529,8 +535,6 @@
         if m == 1:
             place, outs[1][6] = lax.optimization_barrier((place, outs[1][6]))
     arrived_first = exchange(outs[1][0], 2 * cap)
-    outs[2][0], arrived_first = lax.optimization_barrier((outs[2][0], arrived_first))
-    arrived_last = exchange(outs[2][0], cap)
     d_pooled = [o[1] for o in outs]
     grad_bw = ((outs[0][6] + outs[1][6]) + outs[2][6]).reshape(2, devices, per)
     columns = jnp.pad(
@@ -576,28 +580,23 @@
         0,
         120 * MIB,
     )(core, ids, *d_pooled)
-    send_f, arrived_last = lax.optimization_barrier((send_f, arrived_last))
     got = lax.ppermute(send_f, "dev", other_core)
     both = (keep_f.astype(f32) + got.astype(f32)).astype(bf16)
     parts = lax.all_to_all(
         both, "dev", split_axis=0, concat_axis=0, axis_index_groups=same_core, tiled=True
     )
-    (grad_inf,) = local_call(
-        functools.partial(owner_kernel, devices, stride, cap),
-        [((owned, emb), bf16)],
-        [SMEM, VMEM, VMEM],
-        [pltpu.VMEM((n_req, emb), f32)] + [pltpu.VMEM((owned + 8, emb), f32)] * 8,
-        "owner_grads",
+    owner_scratch = [pltpu.VMEM((n_req, emb), f32)] + [pltpu.VMEM((owned + 8, emb), f32)] * 8
+    (partial_inf,) = local_call(
+        functools.partial(first_owner_kernel, devices, stride, cap, (0, 1)),
+        [((owned, emb), f32)],
+        [SMEM, VMEM],
+        owner_scratch,
+        "owner_first",
         62,
         0,
-        60 * MIB,
-    )(
-        asked,
-        arrived_first.reshape(devices, 2 * cap, emb),
-        arrived_last.reshape(devices, cap, emb),
-    )
-
-    parts, grad_inf = lax.optimization_barrier((parts, grad_inf))
+        40 * MIB,
+    )(asked, arrived_first.reshape(devices, 2 * cap, emb))
+    parts, partial_inf, dense = lax.optimization_barrier((parts, partial_inf, dense))
     (spread,) = local_call(
         spread_kernel,
         [((devices // 8, per_freq, emb), bf16)],
@@ -616,10 +615,21 @@
         axis_index_groups=[list(range(k, devices, 8)) for k in range(8)],
         tiled=True,
     ).reshape(freq_rows // 8, emb)
-    sixteen, dense = lax.optimization_barrier((sixteen, dense))
+    sixteen, last = lax.optimization_barrier((sixteen, outs[2][0]))
+    arrived_last = exchange(last, cap)
     grad_freq = lax.all_gather(sixteen, "dev", axis_index_groups=near, tiled=True)
     dense = axis_sum(dense.reshape(4, 4, rows_pad, 2 * rank), 8).astype(bf16)
     dense = axis_sum(dense, 32)
+    (grad_inf,) = local_call(
+        functools.partial(owner_kernel, devices, stride, cap, (2,)),
+        [((owned, emb), bf16)],
+        [SMEM, VMEM, VMEM],
+        owner_scratch,
+        "owner_last",
+        62,
+        0,
+        25 * MIB,
+    )(asked, arrived_last.reshape(devices, cap, emb), partial_inf)
     grad_u = dense[:per, :rank]
     grad_v = dense[:per, rank:].T
     grad_b = dense[per, :per]

time: 325 us -> 329 us (1.012)
  Pallas kernels: 162 us -> 168 us
  starting transfers between devices: 71.8 us -> 68.4 us
  blocking collectives: 14.9 us -> 18.2 us
    all_gather x1, waiting for transfers between devices: 7.7 us -> 1.6 us  [on_device(): lax.all_gather(sixteen, 'dev', axis_index_groups=near, tiled=True)]
    pallas_call x1 -> x2, Pallas kernels: 17 us -> 22.2 us  [the longest x1 13.2 us: on_device(): local_call(functools.partial(first_owner_kernel, devices, stride, cap, (0...]
    all_to_all x1, waiting for transfers between devices: 10.4 us -> 14.2 us  [on_device(): lax.all_to_all(both, 'dev', split_axis=0, concat_axis=0, axis_index_group...]
    all_to_all x1, blocking collectives: 14.9 us -> 18.2 us  [on_device(): lax.all_to_all(spread, 'dev', split_axis=0, concat_axis=0, axis_index_gro...]
  transfers between devices with their start and end apart: 15 -> 15, of which waited for: 10 -> 8; matrix products, arithmetic and copies ran while one was open for 4% -> 4% of each run, Pallas kernels for 43% -> 43%
where the time goes in v9:
time: 329 us; the launch traced here: 324 us
  Pallas kernels  168 us (51%)
  starting transfers between devices  68.4 us (21%)
  waiting for transfers between devices  33.7 us (10%)
  blocking collectives  18.2 us (6%)
  between operations  15.5 us (5%)
  local copies, waits for them, and re-layouts  11.9 us (4%)
  other arithmetic  8.47 us (3%)
    pallas_call x3, Pallas kernels, on_device(): local_call(functools.partial(micro_kernel, devices, cap, features, m, m *...  53.9 us
    all_to_all x4, starting transfers between devices, exchange(): lax.all_to_all(rows.reshape(devices, count, emb), 'dev', split_axis=0, co...  38.8 us
    pallas_call x3, Pallas kernels, freq_rows_of(): local_call(functools.partial(freq_kernel, features, samples, first_micro)...  32.5 us
    pallas_call x1, Pallas kernels, on_device(): local_call(functools.partial(freq_grad_kernel, features), [((devices // 2...  28.4 us
    all_to_all x1, blocking collectives, on_device(): lax.all_to_all(spread, 'dev', split_axis=0, concat_axis=0, axis_index_gro...  18.2 us
    pallas_call x2, Pallas kernels, lookup(): local_call(functools.partial(lookup_kernel, devices, stride, start, count...  17.5 us
    all_to_all x1, waiting for transfers between devices, on_device(): lax.all_to_all(both, 'dev', split_axis=0, concat_axis=0, axis_index_group...  14.2 us
    pallas_call x1, Pallas kernels, on_device(): local_call(functools.partial(first_owner_kernel, devices, stride, cap, (0...  13.2 us
  transfers between devices with their start and end apart: 15, of which 8 were waited for; matrix products, arithmetic and copies ran while one was open for 4% of the time, Pallas kernels for 43%

profile of v9, /device:TPU:1, one launch (start us, length us, event | category | flops | bytes accessed | tf_op | source)
XLA Modules:
  0.0 323.7 jit_solution(1465337673489466307)
XLA Ops:
  7.2 0.8 bitcast_select_fusion
  8.0 0.7 copy.44
  8.7 11.5 %all-to-all-start = ((s32[128,1,128]{2,1,0:T(1,128)}), s32[128,1,128]{2,1,0:T(1,128)S(1)}, u32[]{:S(2)}, u32[]{:S(2)}) async-start(s32[128,1,128]{2,1,0:T(1,128)} %copy.44), calls=%async_computation | async-start | bytes 131072 | tf_op jit(solution)/shard_map/all_to_all | solution.py:416
  20.3 1.6 reshape.96.ids
  21.8 10.8 %freq_rows0.1.freq_part_hbm = f32[3328,128]{1,0:T(8,128)} custom-call(s32[19968]{0:T(1024)} %reshape.96.ids, bf16[16384,128]{1,0:T(8,128)(2,1)} %table_ref.9), custom_call_target="tpu_custom_call" | custom-call | bytes 27262976 | tf_op jit(solution)/shard_map/freq_rows0/pallas_call | solution.py:419
  32.6 0.6 broadcast_minimum_fusion.asked
  33.3 7.0 %lookup0.1 = bf16[4096,128]{1,0:T(8,128)(2,1)} custom-call(s32[16384]{0:T(1024)} %broadcast_minimum_fusion.asked, bf16[4096,128]{1,0:T(8,128)(2,1)} %table_ref.7), custom_call_target="tpu_custom_call" | custom-call | bytes 20971520 | tf_op jit(solution)/shard_map/lookup0/pallas_call | solution.py:455
  40.3 9.8 %all-to-all-start.1 = ((bf16[128,32,128]{2,1,0:T(8,128)(2,1)}), bf16[128,32,128]{2,1,0:T(8,128)(2,1)S(1)}, u32[]{:S(2)}, u32[]{:S(2)}) async-start(bf16[128,32,128]{2,1,0:T(8,128)(2,1)} %bitcast.117), calls=%async_computation.1 | async-start | bytes 2097152 | tf_op jit(solution)/shard_map/all_to_all | solution.py:448
  50.1 0.6 reshape.104.bias
  50.7 0.6 reshape.117.weight
  51.3 0.6 convert_element_type.48.labels
  51.9 0.7 fusion.7
  52.6 10.5 %lookup32.1 = bf16[8192,128]{1,0:T(8,128)(2,1)} custom-call(s32[16384]{0:T(1024)} %broadcast_minimum_fusion.asked, bf16[4096,128]{1,0:T(8,128)(2,1)} %table_ref.7), custom_call_target="tpu_custom_call" | custom-call | bytes 41943040 | tf_op jit(solution)/shard_map/lookup32/pallas_call | solution.py:455
  63.1 10.8 %freq_rows1.1.freq_part_hbm = f32[3328,128]{1,0:T(8,128)} custom-call(s32[19968]{0:T(1024)} %reshape.96.ids, bf16[16384,128]{1,0:T(8,128)(2,1)} %table_ref.9), custom_call_target="tpu_custom_call" | custom-call | bytes 27262976 | tf_op jit(solution)/shard_map/freq_rows1/pallas_call | solution.py:419
  74.0 1.0 copy-done.1
  74.9 10.6 %all-to-all-start.2 = ((bf16[128,64,128]{2,1,0:T(8,128)(2,1)}), bf16[128,64,128]{2,1,0:T(8,128)(2,1)}, u32[]{:S(2)}, u32[]{:S(2)}) async-start(bf16[128,64,128]{2,1,0:T(8,128)(2,1)} %bitcast.116), calls=%async_computation.2 | async-start | bytes 4194304 | tf_op jit(solution)/shard_map/all_to_all | solution.py:448
  86.2 10.8 %freq_rows2.1.freq_part_hbm = f32[3328,128]{1,0:T(8,128)} custom-call(s32[19968]{0:T(1024)} %reshape.96.ids, bf16[16384,128]{1,0:T(8,128)(2,1)} %table_ref.9), custom_call_target="tpu_custom_call" | custom-call | bytes 27262976 | tf_op jit(solution)/shard_map/freq_rows2/pallas_call | solution.py:419
  97.0 17.9 %micro0.1 = (bf16[128,64,128]{2,1,0:T(8,128)(2,1)}, f32[3328,128]{1,0:T(8,128)}, bf16[128,3456]{1,0:T(8,128)(2,1)}, bf16[128,512]{1,0:T(8,128)(2,1)}, bf16[128,5...) custom-call(s32[12288]{0:T(1024)} %bitcast.124, f32[1]{0:T(128)} %bitcast.112.out_b, ...), custom_call_target="tpu_custom_call" | custom-call | flops 1358954496 | bytes 62914560 | tf_op jit(solution)/shard_map/micro0/pallas_call | solution.py:485
  114.9 0.6 all-to-all-done.2
  115.5 17.9 %micro1.1 = (bf16[128,64,128]{2,1,0:T(8,128)(2,1)}, f32[3328,128]{1,0:T(8,128)}, bf16[128,3456]{1,0:T(8,128)(2,1)}, bf16[128,512]{1,0:T(8,128)(2,1)}, bf16[128,5...) custom-call(s32[12288]{0:T(1024)} %bitcast.125, ...), custom_call_target="tpu_custom_call", output_to_operand_aliasing={{0}: (10, {})} | custom-call | flops 1358954496 | bytes 62914560 | tf_op jit(solution)/shard_map/micro1/pallas_call | solution.py:485
  133.4 9.7 %all-to-all-start.3 = ((bf16[128,64,128]{2,1,0:T(8,128)(2,1)}), bf16[128,64,128]{2,1,0:T(8,128)(2,1)}, u32[]{:S(2)}, u32[]{:S(2)}) async-start(bf16[128,64,128]{2,1,0:T(8,128)(2,1)} %get-tuple-element.95), calls=%async_computation.3 | async-start | bytes 4194304 | tf_op jit(solution)/shard_map/all_to_all | solution.py:448
  143.2 18.0 %micro2.1 = (bf16[128,32,128]{2,1,0:T(8,128)(2,1)}, f32[3328,128]{1,0:T(8,128)}, bf16[128,3456]{1,0:T(8,128)(2,1)}, bf16[128,512]{1,0:T(8,128)(2,1)}, bf16[128,5...) custom-call(s32[12288]{0:T(1024)} %bitcast.126, f32[1]{0:T(128)} %bitcast.114.out_b, ...), custom_call_target="tpu_custom_call" | custom-call | flops 1358954496 | bytes 62914560 | tf_op jit(solution)/shard_map/micro2/pallas_call | solution.py:485
  161.2 0.8 add_add_fusion
  162.3 1.1 pad.9.columns
  163.4 10.4 %dense_grads.1 = bf16[8,16,32,1024]{3,2,1,0:T(8,128)(2,1)} custom-call(f32[128,16,128]{2,1,0:T(8,128)} %pad.9.columns, bf16[128,3456]{1,0:T(8,128)(2,1)} %get-tuple-element.83.x0, bf16[128,3456]{1,0:T(8,128)(2,1)} %get-tuple-element.84.x1, bf16[128,3456]{1,0:T(8,128)(2,1)} %get-tuple-element.85.x2, bf16[128,3456]{1,0:T(8,128)(2,1)} %get-tuple-element.86.g0, ...), custom_call_target="tpu_custom_call" | custom-call | flops 2717908992 | bytes 41943040 | tf_op jit(solution)/shard_map/dense_grads/pallas_call | solution.py:546
  173.8 28.4 %freq_grads.1 = (bf16[64,128,128]{2,1,0:T(8,128)(2,1)}, bf16[64,128,128]{2,1,0:T(8,128)(2,1)}) custom-call(s32[1]{0:T(128)} %bitcast.core, s32[19968]{0:T(1024)} %reshape.96.ids, f32[3328,128]{1,0:T(8,128)} %get-tuple-element.97.d0, f32[3328,128]{1,0:T(8,128)} %get-tuple-element.98.d1, f32[3328,128]{1,0:T(8,128)} %get-tuple-element.99.d2), custom_call_target="tpu_custom_call" | custom-call | bytes 125829120 | tf_op jit(solution)/shard_map/freq_grads/pallas_call | solution.py:571
  202.2 1.2 collective-permute-start
  203.4 4.0 %collective-permute-done = bf16[64,128,128]{2,1,0:T(8,128)(2,1)S(1)} collective-permute-done((bf16[64,128,128]{2,1,0:T(8,128)(2,1)}, bf16[64,128,128]{2,1,0:T(8,128)(2,1)S(1)}, u32[]{:S(2)}, u32[]{:S(2)}) %collective-permute-start) | collective-permute-done | bytes 2097184 | tf_op jit(solution)/shard_map/ppermute | solution.py:583
  207.4 3.8 %add_convert_fusion = bf16[64,128,128]{2,1,0:T(8,128)(2,1)} fusion(bf16[64,128,128]{2,1,0:T(8,128)(2,1)S(1)} %collective-permute-done, bf16[64,128,128]{2,1,0:T(8,128)(2,1)} %get-tuple-element.100), kind=kLoop, calls=%fused_computation | loop fusion | flops 4194304 | bytes 6291456 | tf_op jit(solution)/shard_map/convert_element_type | solution.py:584
  211.2 10.1 %all-to-all-start.4 = ((bf16[64,128,128]{2,1,0:T(8,128)(2,1)}), bf16[64,128,128]{2,1,0:T(8,128)(2,1)}, u32[]{:S(2)}, u32[]{:S(2)}) async-start(bf16[64,128,128]{2,1,0:T(8,128)(2,1)} %add_convert_fusion), calls=%async_computation.4 | async-start | bytes 4194304 | tf_op jit(solution)/shard_map/all_to_all | solution.py:585
  221.4 13.2 %owner_first.1.before = f32[4096,128]{1,0:T(8,128)} custom-call(s32[16384]{0:T(1024)} %bitcast.120, bf16[128,64,128]{2,1,0:T(8,128)(2,1)} %bitcast.28.arrived), custom_call_target="tpu_custom_call" | custom-call | bytes 41943040 | tf_op jit(solution)/shard_map/owner_first/pallas_call | solution.py:589
  234.6 14.2 %all-to-all-done.4.parts = bf16[64,128,128]{2,1,0:T(8,128)(2,1)} async-done(((bf16[64,128,128]{2,1,0:T(8,128)(2,1)}), bf16[64,128,128]{2,1,0:T(8,128)(2,1)}, u32[]{:S(2)}, u32[]{:S(2)}) %all-to-all-start.4) | async-done | bytes 2097184 | tf_op jit(solution)/shard_map/all_to_all | solution.py:585
  248.8 2.8 spread.1
  251.6 18.2 %all_to_all.39 = bf16[16,128,128]{2,1,0:T(8,128)(2,1)} all-to-all(bf16[16,128,128]{2,1,0:T(8,128)(2,1)} %spread.1), channel_id=1, replica_groups={{0,8,16,24,32,40,48,56,64,72,80,88,96,104,112,120},{1,9,17,25,33,41,49,..., dimensions={0} | all-to-all | bytes 1048576 | tf_op jit(solution)/shard_map/all_to_all | solution.py:610
  270.5 1.4 collective-permute-start.2
  271.9 1.1 collective-permute-start.3
  273.0 8.8 %all-to-all-start.6 = ((bf16[128,32,128]{2,1,0:T(8,128)(2,1)}), bf16[128,32,128]{2,1,0:T(8,128)(2,1)S(1)}, u32[]{:S(2)}, u32[]{:S(2)}) async-start(bf16[128,32,128]{2,1,0:T(8,128)(2,1)} %get-tuple-element.108), calls=%async_computation.7 | async-start | bytes 2097152 | tf_op jit(solution)/shard_map/all_to_all | solution.py:448
  281.8 3.7 %collective-permute-done.3 = bf16[4,32,1024]{2,1,0:T(8,128)(2,1)S(1)} collective-permute-done((bf16[4,32,1024]{2,1,0:T(8,128)(2,1)S(1)}, bf16[4,32,1024]{2,1,0:T(8,128)(2,1)S(1)}, u32[]{:S(2)}, u32[]{:S(2)}) %collective-permute-start.3) | collective-permute-done | bytes 262176 | tf_op jit(solution)/shard_map/ppermute | solution.py:444
  285.5 1.1 fusion.2
  286.7 3.6 %collective-permute-start.5 = (bf16[32,1024]{1,0:T(8,128)(2,1)S(1)}, bf16[32,1024]{1,0:T(8,128)(2,1)S(1)}, u32[]{:S(2)}, u32[]{:S(2)}) collective-permute-start(bf16[32,1024]{1,0:T(8,128)(2,1)S(1)} %get-tuple-element.115), channel_id=1, source_target_pairs={{0,64},{1,65},{2,66},{3,67},{4,68},{5,69},{6,70},{7,71},{8,72},{9,... | collective-permute-start | bytes 196616 | tf_op jit(solution)/shard_map/ppermute | solution.py:444
  290.3 6.7 %collective-permute-done.4 = bf16[32,1024]{1,0:T(8,128)(2,1)S(1)} collective-permute-done((bf16[32,1024]{1,0:T(8,128)(2,1)S(1)}, bf16[32,1024]{1,0:T(8,128)(2,1)S(1)}, u32[]{:S(2)}, u32[]{:S(2)}) %collective-permute-start.4) | collective-permute-done | bytes 65568 | tf_op jit(solution)/shard_map/ppermute | solution.py:444
  297.0 1.3 collective-permute-done.5
  298.9 0.7 slice_bitcast_fusion
  299.5 1.6 all-to-all-done.6.arrived
  301.1 1.0 copy-done
  302.1 9.0 %owner_last.1 = bf16[4096,128]{1,0:T(8,128)(2,1)} custom-call(s32[16384]{0:T(1024)} %bitcast.121, bf16[128,32,128]{2,1,0:T(8,128)(2,1)} %copy-done, f32[4096,128]{1,0:T(8,128)} %owner_first.1.before), custom_call_target="tpu_custom_call" | custom-call | bytes 26214400 | tf_op jit(solution)/shard_map/owner_last/pallas_call | solution.py:623
  311.1 1.6 all-gather.2.cloned.1.call-done
  312.7 3.7 %copy.56 = bf16[16384,128]{1,0:T(8,128)(2,1)} copy(bf16[16384,128]{1,0:T(8,128)(2,1)} %all-gather.2.cloned.1.call-done) | data formatting | bytes 8388608
  (41 shorter events, 1.7 us)
Async XLA Ops:
  8.7 23.9 %all-to-all-start = ((s32[128,1,128]{2,1,0:T(1,128)}), s32[128,1,128]{2,1,0:T(1,128)S(1)}, u32[]{:S(2)}, u32[]{:S(2)}) async-start(s32[128,1,128]{2,1,0:T(1,128)} %copy.44), calls=%async_computation | async-start | bytes 131072 | tf_op jit(solution)/shard_map/all_to_all | solution.py:416
  32.6 7.7 %copy-start.2 = (s32[128,1,128]{2,1,0:T(1,128)}, s32[128,1,128]{2,1,0:T(1,128)S(1)}, u32[]{:S(2)}) copy-start(s32[128,1,128]{2,1,0:T(1,128)S(1)} %all-to-all-done) | copy-start | bytes 196612
  33.3 16.8 %copy-start.8 = (f32[3456]{0:T(1024)S(1)}, f32[3456]{0:T(1024)}, u32[]{:S(2)}) copy-start(f32[3456]{0:T(1024)} %param.21) | copy-start | bytes 41476
  33.3 17.4 %copy-start.9 = (bf16[3456]{0:T(1024)(128)(2,1)S(1)}, bf16[3456]{0:T(1024)(128)(2,1)}, u32[]{:S(2)}) copy-start(bf16[3456]{0:T(1024)(128)(2,1)} %param.22) | copy-start | bytes 20740
  33.3 18.0 %copy-start.10 = (s32[3,128]{1,0:T(4,128)S(1)}, s32[3,128]{1,0:T(4,128)}, u32[]{:S(2)}) copy-start(s32[3,128]{1,0:T(4,128)} %param.13) | copy-start | bytes 4612
  33.3 18.6 %copy-start.4 = (s32[3,1,128,32]{2,3,1,0:T(8,128)S(1)}, s32[3,1,128,32]{2,3,1,0:T(8,128)}, u32[]{:S(2)}) copy-start(s32[3,1,128,32]{2,3,1,0:T(8,128)} %param.16) | copy-start | bytes 147460
  33.3 18.6 %copy-start.5 = (s32[3,1,128,32]{2,3,1,0:T(8,128)S(1)}, s32[3,1,128,32]{2,3,1,0:T(8,128)}, u32[]{:S(2)}) copy-start(s32[3,1,128,32]{2,3,1,0:T(8,128)} %param.15) | copy-start | bytes 147460
  40.3 33.7 %all-to-all-start.1 = ((bf16[128,32,128]{2,1,0:T(8,128)(2,1)}), bf16[128,32,128]{2,1,0:T(8,128)(2,1)S(1)}, u32[]{:S(2)}, u32[]{:S(2)}) async-start(bf16[128,32,128]{2,1,0:T(8,128)(2,1)} %bitcast.117), calls=%async_computation.1 | async-start | bytes 2097152 | tf_op jit(solution)/shard_map/all_to_all | solution.py:448
  74.0 1.0 copy-start.1
  74.9 40.6 %all-to-all-start.2 = ((bf16[128,64,128]{2,1,0:T(8,128)(2,1)}), bf16[128,64,128]{2,1,0:T(8,128)(2,1)}, u32[]{:S(2)}, u32[]{:S(2)}) async-start(bf16[128,64,128]{2,1,0:T(8,128)(2,1)} %bitcast.116), calls=%async_computation.2 | async-start | bytes 4194304 | tf_op jit(solution)/shard_map/all_to_all | solution.py:448
  133.4 40.4 %all-to-all-start.3 = ((bf16[128,64,128]{2,1,0:T(8,128)(2,1)}), bf16[128,64,128]{2,1,0:T(8,128)(2,1)}, u32[]{:S(2)}, u32[]{:S(2)}) async-start(bf16[128,64,128]{2,1,0:T(8,128)(2,1)} %get-tuple-element.95), calls=%async_computation.3 | async-start | bytes 4194304 | tf_op jit(solution)/shard_map/all_to_all | solution.py:448
  143.1 105.7 %reduce-scatter.2.cloned.1.call-start = ((), (), s32[]{:S(2)}) async-start(), calls=%async_computation.8 | async-start | bytes 9437184 | tf_op jit(solution)/shard_map/reduce_scatter | solution.py:570
  143.2 18.1 %copy-start.6 = (f32[2,3456]{1,0:T(2,128)S(1)}, f32[2,3456]{1,0:T(2,128)}, u32[]{:S(2)}) copy-start(f32[2,3456]{1,0:T(2,128)} %get-tuple-element.74) | copy-start | bytes 82948
  143.2 18.1 %copy-start.7 = (f32[2,3456]{1,0:T(2,128)S(1)}, f32[2,3456]{1,0:T(2,128)}, u32[]{:S(2)}) copy-start(f32[2,3456]{1,0:T(2,128)} %get-tuple-element.79) | copy-start | bytes 82948
  202.2 5.2 %collective-permute-start = (bf16[64,128,128]{2,1,0:T(8,128)(2,1)}, bf16[64,128,128]{2,1,0:T(8,128)(2,1)S(1)}, u32[]{:S(2)}, u32[]{:S(2)}) collective-permute-start(bf16[64,128,128]{2,1,0:T(8,128)(2,1)} %get-tuple-element.101), channel_id=1, source_target_pairs={{0,1},{1,0},{2,3},{3,2},{4,5},{5,4},{6,7},{7,6},{8,9},{9,8},{10,11... | collective-permute-start | bytes 6291464 | tf_op jit(solution)/shard_map/ppermute | solution.py:583
  211.2 37.6 %all-to-all-start.4 = ((bf16[64,128,128]{2,1,0:T(8,128)(2,1)}), bf16[64,128,128]{2,1,0:T(8,128)(2,1)}, u32[]{:S(2)}, u32[]{:S(2)}) async-start(bf16[64,128,128]{2,1,0:T(8,128)(2,1)} %add_convert_fusion), calls=%async_computation.4 | async-start | bytes 4194304 | tf_op jit(solution)/shard_map/all_to_all | solution.py:585
  221.3 91.4 %all-gather.2.cloned.1.call-start = ((), (), s32[]{:S(2)}) async-start(), calls=%async_computation.9 | async-start | bytes 4718592 | tf_op jit(solution)/shard_map/all_gather | solution.py:620
  248.8 21.1 %copy-start.3 = (bf16[16,32,1024]{2,1,0:T(8,128)(2,1)S(1)}, bf16[16,32,1024]{2,1,0:T(8,128)(2,1)}, u32[]{:S(2)}) copy-start(bf16[16,32,1024]{2,1,0:T(8,128)(2,1)} %reduce-scatter.2.cloned.1.call-done) | copy-start | bytes 3145732
  270.0 11.8 %collective-permute-start.1 = (bf16[4,32,1024]{2,1,0:T(8,128)(2,1)S(1)}, bf16[4,32,1024]{2,1,0:T(8,128)(2,1)S(1)}, u32[]{:S(2)}, u32[]{:S(2)}) collective-permute-start(bf16[4,32,1024]{2,1,0:T(8,128)(2,1)S(1)} %get-tuple-element.110), channel_id=1, source_target_pairs={{0,8},{1,9},{2,10},{3,11},{4,12},{5,13},{6,14},{7,15},{8,16},{9,17... | collective-permute-start | bytes 786440 | tf_op jit(solution)/shard_map/ppermute | solution.py:444
  270.5 11.3 %collective-permute-start.2 = (bf16[4,32,1024]{2,1,0:T(8,128)(2,1)S(1)}, bf16[4,32,1024]{2,1,0:T(8,128)(2,1)S(1)}, u32[]{:S(2)}, u32[]{:S(2)}) collective-permute-start(bf16[4,32,1024]{2,1,0:T(8,128)(2,1)S(1)} %get-tuple-element.112), channel_id=1, source_target_pairs={{0,16},{1,17},{2,18},{3,19},{4,20},{5,21},{6,22},{7,23},{8,24},{9,... | collective-permute-start | bytes 786440 | tf_op jit(solution)/shard_map/ppermute | solution.py:444
  271.9 13.6 %collective-permute-start.3 = (bf16[4,32,1024]{2,1,0:T(8,128)(2,1)S(1)}, bf16[4,32,1024]{2,1,0:T(8,128)(2,1)S(1)}, u32[]{:S(2)}, u32[]{:S(2)}) collective-permute-start(bf16[4,32,1024]{2,1,0:T(8,128)(2,1)S(1)} %get-tuple-element.111), channel_id=1, source_target_pairs={{0,24},{1,25},{2,26},{3,27},{4,28},{5,29},{6,30},{7,31},{8,0},{9,1... | collective-permute-start | bytes 786440 | tf_op jit(solution)/shard_map/ppermute | solution.py:444
  273.0 28.1 %all-to-all-start.6 = ((bf16[128,32,128]{2,1,0:T(8,128)(2,1)}), bf16[128,32,128]{2,1,0:T(8,128)(2,1)S(1)}, u32[]{:S(2)}, u32[]{:S(2)}) async-start(bf16[128,32,128]{2,1,0:T(8,128)(2,1)} %get-tuple-element.108), calls=%async_computation.7 | async-start | bytes 2097152 | tf_op jit(solution)/shard_map/all_to_all | solution.py:448
  286.7 10.4 %collective-permute-start.4 = (bf16[32,1024]{1,0:T(8,128)(2,1)S(1)}, bf16[32,1024]{1,0:T(8,128)(2,1)S(1)}, u32[]{:S(2)}, u32[]{:S(2)}) collective-permute-start(bf16[32,1024]{1,0:T(8,128)(2,1)S(1)} %get-tuple-element.113), channel_id=1, source_target_pairs={{0,32},{1,33},{2,34},{3,35},{4,36},{5,37},{6,38},{7,39},{8,40},{9,... | collective-permute-start | bytes 196616 | tf_op jit(solution)/shard_map/ppermute | solution.py:444
  286.7 11.6 %collective-permute-start.5 = (bf16[32,1024]{1,0:T(8,128)(2,1)S(1)}, bf16[32,1024]{1,0:T(8,128)(2,1)S(1)}, u32[]{:S(2)}, u32[]{:S(2)}) collective-permute-start(bf16[32,1024]{1,0:T(8,128)(2,1)S(1)} %get-tuple-element.115), channel_id=1, source_target_pairs={{0,64},{1,65},{2,66},{3,67},{4,68},{5,69},{6,70},{7,71},{8,72},{9,... | collective-permute-start | bytes 196616 | tf_op jit(solution)/shard_map/ppermute | solution.py:444
  290.3 8.0 %collective-permute-start.6 = (bf16[32,1024]{1,0:T(8,128)(2,1)S(1)}, bf16[32,1024]{1,0:T(8,128)(2,1)S(1)}, u32[]{:S(2)}, u32[]{:S(2)}) collective-permute-start(bf16[32,1024]{1,0:T(8,128)(2,1)S(1)} %get-tuple-element.114), channel_id=1, source_target_pairs={{0,96},{1,97},{2,98},{3,99},{4,100},{5,101},{6,102},{7,103},{8,104... | collective-permute-start | bytes 196616 | tf_op jit(solution)/shard_map/ppermute | solution.py:444
  301.1 1.0 copy-start
Sparse Core Ops, SparseCore 0:
  173.9 71.2 reduce-scatter.1
  269.9 42.7 all-gather.1

commit v10 on v8

--- a/solution.py
+++ b/solution.py
@@ -46,7 +46,7 @@
 def freq_kernel(blocks, samples, first_micro, ids, table_ref, *refs):
     *outs, table = refs
     table[...] = table_ref[...].astype(f32)
-    unroll = 32
+    unroll = 128
     for m, out in enumerate(outs):
         start = (first_micro + m) * blocks * 2 * samples
 
@@ -90,7 +90,7 @@
     loss_mult,
     slots,
     out_b,
-    fetched_hbm,
+    fetched_ref,
     freq_part_hbm,
     bottom,
     labels,
@@ -120,27 +120,32 @@
         cross_v,
         sems,
     ) = refs[-25:]
+    before = refs[0]
     acc0 = accs[0]
     samples, width = x_zero.shape
     emb = bottom.shape[2]
     n_slots = features * samples
     ways = len(accs)
     loads = [
-        pltpu.make_async_copy(
-            fetched_hbm.at[:, pl.ds(fetch_start, cap), :], returned, sems.at[6]
-        ),
         pltpu.make_async_copy(freq_part_hbm, acc0.at[pl.ds(0, n_slots), :], sems.at[7]),
         pltpu.make_async_copy(cross_u_hbm, cross_u, sems.at[8]),
         pltpu.make_async_copy(cross_v_hbm, cross_v, sems.at[9]),
     ]
+    if m > 0:
+        fetch = pltpu.make_async_copy(
+            fetched_ref.at[:, pl.ds(fetch_start, cap), :], returned, sems.at[6]
+        )
+        fetch.start()
     for load in loads:
         load.start()
     for a in accs[1:]:
         a[...] = jnp.zeros_like(a)
     acc0[n_slots:, :] = jnp.zeros((acc0.shape[0] - n_slots, emb), f32)
+    if m > 0:
+        fetch.wait()
+    source = returned if m > 0 else fetched_ref
+    arrived[...] = source[...].astype(f32).reshape(peers * cap, emb)
     loads[0].wait()
-    arrived[...] = returned[...].astype(f32).reshape(peers * cap, emb)
-    loads[1].wait()
 
     def add_peer(o, carry):
         for c in range(0, cap, ways):
@@ -161,8 +166,8 @@
         total = tree_sum([a[rows, :] for a in accs])
         x_zero[:, (f + 1) * emb : (f + 2) * emb] = total.astype(bf16)
 
+    loads[1].wait()
     loads[2].wait()
-    loads[3].wait()
     hidden = jnp.dot(x_zero[...], cross_u[...], preferred_element_type=f32).astype(bf16)
     hidden_out[...] = hidden
     copies = [
@@ -195,8 +200,14 @@
         d_gate = (d_logit * weight[:, cols]) * x_float
         gate_low[:, cols] = d_gate.astype(bf16)
         crossed = x_float * gate[:, cols] + x_float
-        grad_bw[0:1, cols] = jnp.sum(d_gate, axis=0, keepdims=True)
-        grad_bw[1:2, cols] = jnp.sum(d_logit * crossed, axis=0, keepdims=True)
+        sums = [
+            jnp.sum(d_gate, axis=0, keepdims=True),
+            jnp.sum(d_logit * crossed, axis=0, keepdims=True),
+        ]
+        for k_row in range(2):
+            if m > 0:
+                sums[k_row] = sums[k_row] + before[k_row : k_row + 1, cols]
+            grad_bw[k_row : k_row + 1, cols] = sums[k_row]
     d_hidden = lax.dot_general(
         gate_low[...], cross_v[...], NT, preferred_element_type=f32
     ).astype(bf16)
@@ -497,7 +508,7 @@
                 ((samples, width), bf16),
                 ((2, width), f32),
             ],
-            [SMEM, SMEM, HBM, HBM, VMEM, VMEM, HBM, HBM, VMEM, VMEM] + ([HBM] if m else []),
+            [SMEM, SMEM, HBM if m else VMEM, HBM, VMEM, VMEM, HBM, HBM, VMEM, VMEM] + ([VMEM, HBM] if m else []),
             [pltpu.VMEM((n_req, emb), f32)]
             + [pltpu.VMEM((n_slots + 8, emb), f32)] * 8
             + [pltpu.VMEM((samples, width), f32)]
@@ -511,7 +522,7 @@
             6 * samples * width * rank,
             60 * MIB,
             [HBM] * 6 + [VMEM],
-            {10: 0} if m else {},
+            {11: 0} if m else {},
         )(
             place,
             bias_b,
@@ -523,14 +534,14 @@
             cross_v,
             bias,
             weight,
-            *([outs[m - 1][0]] if m else []),
+            *([outs[m - 1][6], outs[m - 1][0]] if m else []),
         )
         outs.append(list(out))
         if m == 1:
             place, outs[1][6] = lax.optimization_barrier((place, outs[1][6]))
     arrived = exchange(outs[2][0], micro * cap)
     d_pooled = [o[1] for o in outs]
-    grad_bw = ((outs[0][6] + outs[1][6]) + outs[2][6]).reshape(2, devices, per)
+    grad_bw = outs[2][6].reshape(2, devices, per)
     columns = jnp.pad(
         jnp.transpose(grad_bw, (1, 0, 2)), ((0, 0), (per - 16, 30 - per), (0, 128 - per))
     )

time: 325 us -> 320 us (0.985)
  Pallas kernels: 162 us -> 158 us
    pallas_call x3, Pallas kernels: 32.8 us -> 28.3 us  [freq_rows_of(): local_call(functools.partial(freq_kernel, features, samples, first_micro)...]
  transfers between devices with their start and end apart: 14 -> 14, of which waited for: 11 -> 11; matrix products, arithmetic and copies ran while one was open for 4% -> 4% of each run, Pallas kernels for 34% -> 33%
where the time goes in v10:
time: 320 us; the launch traced here: 314 us
  Pallas kernels  158 us (49%)
  starting transfers between devices  56.9 us (18%)
  waiting for transfers between devices  49.6 us (16%)
  between operations  15.4 us (5%)
  blocking collectives  14.6 us (5%)
  local copies, waits for them, and re-layouts  12.8 us (4%)
  other arithmetic  7.63 us (2%)
    pallas_call x3, Pallas kernels, on_device(): local_call(functools.partial(micro_kernel, devices, cap, features, m, m *...  53.6 us
    pallas_call x3, Pallas kernels, freq_rows_of(): local_call(functools.partial(freq_kernel, features, samples, first_micro)...  28.3 us
    all_to_all x3, starting transfers between devices, exchange(): lax.all_to_all(rows.reshape(devices, count, emb), 'dev', split_axis=0, co...  28.2 us
    pallas_call x1, Pallas kernels, on_device(): local_call(functools.partial(freq_grad_kernel, features), [((devices // 2...  28 us
    pallas_call x2, Pallas kernels, lookup(): local_call(functools.partial(lookup_kernel, devices, stride, start, count...  17.5 us
    pallas_call x1, Pallas kernels, on_device(): local_call(functools.partial(owner_kernel, devices, stride, cap), [((owne...  17.1 us
    all_to_all x1, blocking collectives, on_device(): lax.all_to_all(spread, 'dev', split_axis=0, concat_axis=0, axis_index_gro...  14.6 us
    ppermute x6, waiting for transfers between devices, axis_sum(): total = total + lax.ppermute(block, 'dev', to).astype(f32)  14.4 us
  transfers between devices with their start and end apart: 14, of which 11 were waited for; matrix products, arithmetic and copies ran while one was open for 4% of the time, Pallas kernels for 33%

profile of v10, /device:TPU:1, one launch (start us, length us, event | category | flops | bytes accessed | tf_op | source)
XLA Modules:
  0.0 314.4 jit_solution(17695759331438018905)
XLA Ops:
  7.2 0.8 bitcast_select_fusion
  8.0 0.7 copy.45
  8.7 11.5 %all-to-all-start = ((s32[128,1,128]{2,1,0:T(1,128)}), s32[128,1,128]{2,1,0:T(1,128)S(1)}, u32[]{:S(2)}, u32[]{:S(2)}) async-start(s32[128,1,128]{2,1,0:T(1,128)} %copy.45), calls=%async_computation | async-start | bytes 131072 | tf_op jit(solution)/shard_map/all_to_all | solution.py:421
  20.3 1.6 reshape.96.ids
  21.8 9.4 %freq_rows0.1.freq_part_hbm = f32[3328,128]{1,0:T(8,128)} custom-call(s32[19968]{0:T(1024)} %reshape.96.ids, bf16[16384,128]{1,0:T(8,128)(2,1)} %table_ref.9), custom_call_target="tpu_custom_call" | custom-call | bytes 27262976 | tf_op jit(solution)/shard_map/freq_rows0/pallas_call | solution.py:424
  31.2 0.6 broadcast_minimum_fusion.asked
  31.9 7.0 %lookup0.1 = bf16[4096,128]{1,0:T(8,128)(2,1)} custom-call(s32[16384]{0:T(1024)} %broadcast_minimum_fusion.asked, bf16[4096,128]{1,0:T(8,128)(2,1)} %table_ref.7), custom_call_target="tpu_custom_call" | custom-call | bytes 20971520 | tf_op jit(solution)/shard_map/lookup0/pallas_call | solution.py:460
  38.9 9.8 %all-to-all-start.1 = ((bf16[128,32,128]{2,1,0:T(8,128)(2,1)}), bf16[128,32,128]{2,1,0:T(8,128)(2,1)S(1)}, u32[]{:S(2)}, u32[]{:S(2)}) async-start(bf16[128,32,128]{2,1,0:T(8,128)(2,1)} %bitcast.117), calls=%async_computation.1 | async-start | bytes 2097152 | tf_op jit(solution)/shard_map/all_to_all | solution.py:453
  49.3 0.6 reshape.117.weight
  50.5 0.7 fusion.7
  51.1 10.5 %lookup32.1 = bf16[8192,128]{1,0:T(8,128)(2,1)} custom-call(s32[16384]{0:T(1024)} %broadcast_minimum_fusion.asked, bf16[4096,128]{1,0:T(8,128)(2,1)} %table_ref.7), custom_call_target="tpu_custom_call" | custom-call | bytes 41943040 | tf_op jit(solution)/shard_map/lookup32/pallas_call | solution.py:460
  61.7 9.3 %freq_rows1.1.freq_part_hbm = f32[3328,128]{1,0:T(8,128)} custom-call(s32[19968]{0:T(1024)} %reshape.96.ids, bf16[16384,128]{1,0:T(8,128)(2,1)} %table_ref.9), custom_call_target="tpu_custom_call" | custom-call | bytes 27262976 | tf_op jit(solution)/shard_map/freq_rows1/pallas_call | solution.py:424
  71.0 1.0 copy-done
  72.0 10.2 %all-to-all-start.2 = ((bf16[128,64,128]{2,1,0:T(8,128)(2,1)}), bf16[128,64,128]{2,1,0:T(8,128)(2,1)}, u32[]{:S(2)}, u32[]{:S(2)}) async-start(bf16[128,64,128]{2,1,0:T(8,128)(2,1)} %bitcast.116), calls=%async_computation.2 | async-start | bytes 4194304 | tf_op jit(solution)/shard_map/all_to_all | solution.py:453
  82.9 9.5 %freq_rows2.1.freq_part_hbm = f32[3328,128]{1,0:T(8,128)} custom-call(s32[19968]{0:T(1024)} %reshape.96.ids, bf16[16384,128]{1,0:T(8,128)(2,1)} %table_ref.9), custom_call_target="tpu_custom_call" | custom-call | bytes 27262976 | tf_op jit(solution)/shard_map/freq_rows2/pallas_call | solution.py:424
  92.5 17.5 %micro0.1 = (bf16[128,96,128]{2,1,0:T(8,128)(2,1)}, f32[3328,128]{1,0:T(8,128)}, bf16[128,3456]{1,0:T(8,128)(2,1)}, bf16[128,512]{1,0:T(8,128)(2,1)}, bf16[128,5...) custom-call(s32[12288]{0:T(1024)} %bitcast.121, f32[1]{0:T(128)} %bitcast.112.out_b, ...), custom_call_target="tpu_custom_call" | custom-call | flops 1358954496 | bytes 62914560 | tf_op jit(solution)/shard_map/micro0/pallas_call | solution.py:490
  110.0 2.4 all-to-all-done.2
  112.4 17.9 %micro1.1 = (bf16[128,96,128]{2,1,0:T(8,128)(2,1)}, f32[3328,128]{1,0:T(8,128)}, bf16[128,3456]{1,0:T(8,128)(2,1)}, bf16[128,512]{1,0:T(8,128)(2,1)}, bf16[128,5...) custom-call(s32[12288]{0:T(1024)} %bitcast.122, ...), custom_call_target="tpu_custom_call", output_to_operand_aliasing={{0}: (11, {})} | custom-call | flops 1358954496 | bytes 62914560 | tf_op jit(solution)/shard_map/micro1/pallas_call | solution.py:490
  130.3 18.2 %micro2.1 = (bf16[128,96,128]{2,1,0:T(8,128)(2,1)}, f32[3328,128]{1,0:T(8,128)}, bf16[128,3456]{1,0:T(8,128)(2,1)}, bf16[128,512]{1,0:T(8,128)(2,1)}, bf16[128,5...) custom-call(s32[12288]{0:T(1024)} %bitcast.123, ...), custom_call_target="tpu_custom_call", output_to_operand_aliasing={{0}: (11, {})} | custom-call | flops 1358954496 | bytes 62914560 | tf_op jit(solution)/shard_map/micro2/pallas_call | solution.py:490
  148.5 1.0 reshape.110
  149.6 1.1 pad.9.columns
  150.6 10.3 %dense_grads.1 = bf16[8,16,32,1024]{3,2,1,0:T(8,128)(2,1)} custom-call(f32[128,16,128]{2,1,0:T(8,128)} %pad.9.columns, bf16[128,3456]{1,0:T(8,128)(2,1)} %get-tuple-element.84.x0, bf16[128,3456]{1,0:T(8,128)(2,1)} %get-tuple-element.85.x1, bf16[128,3456]{1,0:T(8,128)(2,1)} %get-tuple-element.86.x2, bf16[128,3456]{1,0:T(8,128)(2,1)} %get-tuple-element.87.g0, ...), custom_call_target="tpu_custom_call" | custom-call | flops 2717908992 | bytes 41943040 | tf_op jit(solution)/shard_map/dense_grads/pallas_call | solution.py:551
  161.0 8.2 %all-to-all-start.3 = ((bf16[128,96,128]{2,1,0:T(8,128)(2,1)}), bf16[128,96,128]{2,1,0:T(8,128)(2,1)}, u32[]{:S(2)}, u32[]{:S(2)}) async-start(bf16[128,96,128]{2,1,0:T(8,128)(2,1)} %get-tuple-element.102), calls=%async_computation.3 | async-start | bytes 6291456 | tf_op jit(solution)/shard_map/all_to_all | solution.py:453
  169.2 28.0 %freq_grads.1 = (bf16[64,128,128]{2,1,0:T(8,128)(2,1)}, bf16[64,128,128]{2,1,0:T(8,128)(2,1)}) custom-call(s32[1]{0:T(128)} %bitcast.core, s32[19968]{0:T(1024)} %reshape.96.ids, f32[3328,128]{1,0:T(8,128)} %get-tuple-element.97.d0, f32[3328,128]{1,0:T(8,128)} %get-tuple-element.98.d1, f32[3328,128]{1,0:T(8,128)} %get-tuple-element.99.d2), custom_call_target="tpu_custom_call" | custom-call | bytes 125829120 | tf_op jit(solution)/shard_map/freq_grads/pallas_call | solution.py:576
  197.2 1.0 collective-permute-start
  198.3 4.0 %collective-permute-done = bf16[64,128,128]{2,1,0:T(8,128)(2,1)S(1)} collective-permute-done((bf16[64,128,128]{2,1,0:T(8,128)(2,1)}, bf16[64,128,128]{2,1,0:T(8,128)(2,1)S(1)}, u32[]{:S(2)}, u32[]{:S(2)}) %collective-permute-start) | collective-permute-done | bytes 2097184 | tf_op jit(solution)/shard_map/ppermute | solution.py:588
  202.3 3.7 %add_convert_fusion = bf16[64,128,128]{2,1,0:T(8,128)(2,1)} fusion(bf16[64,128,128]{2,1,0:T(8,128)(2,1)S(1)} %collective-permute-done, bf16[64,128,128]{2,1,0:T(8,128)(2,1)} %get-tuple-element.100), kind=kLoop, calls=%fused_computation | loop fusion | flops 4194304 | bytes 6291456 | tf_op jit(solution)/shard_map/convert_element_type | solution.py:589
  206.0 4.6 %all-to-all-done.3 = bf16[128,96,128]{2,1,0:T(8,128)(2,1)} async-done(((bf16[128,96,128]{2,1,0:T(8,128)(2,1)}), bf16[128,96,128]{2,1,0:T(8,128)(2,1)}, u32[]{:S(2)}, u32[]{:S(2)}) %all-to-all-start.3) | async-done | bytes 3145760 | tf_op jit(solution)/shard_map/all_to_all | solution.py:453
  210.6 6.8 %all-to-all-start.4 = ((bf16[64,128,128]{2,1,0:T(8,128)(2,1)}), bf16[64,128,128]{2,1,0:T(8,128)(2,1)}, u32[]{:S(2)}, u32[]{:S(2)}) async-start(bf16[64,128,128]{2,1,0:T(8,128)(2,1)} %add_convert_fusion), calls=%async_computation.4 | async-start | bytes 4194304 | tf_op jit(solution)/shard_map/all_to_all | solution.py:591
  217.5 17.1 %owner_grads.1 = bf16[4096,128]{1,0:T(8,128)(2,1)} custom-call(s32[16384]{0:T(1024)} %bitcast.125, bf16[128,96,128]{2,1,0:T(8,128)(2,1)} %bitcast.28.arrived), custom_call_target="tpu_custom_call" | custom-call | bytes 62914560 | tf_op jit(solution)/shard_map/owner_grads/pallas_call | solution.py:594
  234.6 10.3 %all-to-all-done.4.parts = bf16[64,128,128]{2,1,0:T(8,128)(2,1)} async-done(((bf16[64,128,128]{2,1,0:T(8,128)(2,1)}), bf16[64,128,128]{2,1,0:T(8,128)(2,1)}, u32[]{:S(2)}, u32[]{:S(2)}) %all-to-all-start.4) | async-done | bytes 2097184 | tf_op jit(solution)/shard_map/all_to_all | solution.py:591
  244.9 2.7 spread.1
  247.6 14.6 %all_to_all.34 = bf16[16,128,128]{2,1,0:T(8,128)(2,1)} all-to-all(bf16[16,128,128]{2,1,0:T(8,128)(2,1)} %spread.1), channel_id=1, replica_groups={{0,8,16,24,32,40,48,56,64,72,80,88,96,104,112,120},{1,9,17,25,33,41,49,..., dimensions={0} | all-to-all | bytes 1048576 | tf_op jit(solution)/shard_map/all_to_all | solution.py:619
  262.3 7.1 %reduce-scatter.2.cloned.1.call-done = bf16[16,32,1024]{2,1,0:T(8,128)(2,1)} async-done(((bf16[128,32,1024]{2,1,0:T(8,128)(2,1)}), bf16[16,32,1024]{2,1,0:T(8,128)(2,1)}) %reduce-scatter.2.cloned.1.call-update) | async-done | bytes 1048592 | tf_op jit(solution)/shard_map/reduce_scatter | solution.py:575
  269.5 1.2 dynamic-slice_bitcast_fusion.2
  270.7 0.7 collective-permute-start.1
  271.3 3.9 %collective-permute-start.2 = (bf16[4,32,1024]{2,1,0:T(8,128)(2,1)S(1)}, bf16[4,32,1024]{2,1,0:T(8,128)(2,1)S(1)}, u32[]{:S(2)}, u32[]{:S(2)}) collective-permute-start(bf16[4,32,1024]{2,1,0:T(8,128)(2,1)S(1)} %get-tuple-element.112), channel_id=1, source_target_pairs={{0,16},{1,17},{2,18},{3,19},{4,20},{5,21},{6,22},{7,23},{8,24},{9,... | collective-permute-start | bytes 786440 | tf_op jit(solution)/shard_map/ppermute | solution.py:449
  275.2 5.4 %collective-permute-done.1 = bf16[4,32,1024]{2,1,0:T(8,128)(2,1)S(1)} collective-permute-done((bf16[4,32,1024]{2,1,0:T(8,128)(2,1)S(1)}, bf16[4,32,1024]{2,1,0:T(8,128)(2,1)S(1)}, u32[]{:S(2)}, u32[]{:S(2)}) %collective-permute-start.1) | collective-permute-done | bytes 262176 | tf_op jit(solution)/shard_map/ppermute | solution.py:449
  280.7 6.9 %collective-permute-done.2 = bf16[4,32,1024]{2,1,0:T(8,128)(2,1)S(1)} collective-permute-done((bf16[4,32,1024]{2,1,0:T(8,128)(2,1)S(1)}, bf16[4,32,1024]{2,1,0:T(8,128)(2,1)S(1)}, u32[]{:S(2)}, u32[]{:S(2)}) %collective-permute-start.2) | collective-permute-done | bytes 262176 | tf_op jit(solution)/shard_map/ppermute | solution.py:449
  287.6 1.1 fusion.2
  288.8 0.7 collective-permute-start.4
  289.5 2.0 collective-permute-start.5
  291.5 2.0 collective-permute-start.6
  293.6 1.1 collective-permute-done.5
  294.7 0.8 collective-permute-done.6
  296.1 0.7 slice_bitcast_fusion
  296.7 6.7 %all-gather.2.cloned.1.call-done = bf16[16384,128]{1,0:T(8,128)(2,1)} async-done(((bf16[2048,128]{1,0:T(8,128)(2,1)}), bf16[16384,128]{1,0:T(8,128)(2,1)}) %all-gather.2.cloned.1.call-update) | async-done | bytes 4194320 | tf_op jit(solution)/shard_map/all_gather | solution.py:628
  303.4 3.7 %copy.58 = bf16[16384,128]{1,0:T(8,128)(2,1)} copy(bf16[16384,128]{1,0:T(8,128)(2,1)} %all-gather.2.cloned.1.call-done) | data formatting | bytes 8388608
  (29 shorter events, 2.1 us)
Async XLA Ops:
  8.7 22.5 %all-to-all-start = ((s32[128,1,128]{2,1,0:T(1,128)}), s32[128,1,128]{2,1,0:T(1,128)S(1)}, u32[]{:S(2)}, u32[]{:S(2)}) async-start(s32[128,1,128]{2,1,0:T(1,128)} %copy.45), calls=%async_computation | async-start | bytes 131072 | tf_op jit(solution)/shard_map/all_to_all | solution.py:421
  31.2 7.7 %copy-start.1 = (s32[128,1,128]{2,1,0:T(1,128)}, s32[128,1,128]{2,1,0:T(1,128)S(1)}, u32[]{:S(2)}) copy-start(s32[128,1,128]{2,1,0:T(1,128)S(1)} %all-to-all-done) | copy-start | bytes 196612
  31.9 16.8 %copy-start.4 = (f32[3456]{0:T(1024)S(1)}, f32[3456]{0:T(1024)}, u32[]{:S(2)}) copy-start(f32[3456]{0:T(1024)} %param.21) | copy-start | bytes 41476
  31.9 17.4 %copy-start.5 = (bf16[3456]{0:T(1024)(128)(2,1)S(1)}, bf16[3456]{0:T(1024)(128)(2,1)}, u32[]{:S(2)}) copy-start(bf16[3456]{0:T(1024)(128)(2,1)} %param.22) | copy-start | bytes 20740
  31.9 18.0 %copy-start.6 = (s32[3,128]{1,0:T(4,128)S(1)}, s32[3,128]{1,0:T(4,128)}, u32[]{:S(2)}) copy-start(s32[3,128]{1,0:T(4,128)} %param.13) | copy-start | bytes 4612
  31.9 18.6 %copy-start.2 = (s32[3,1,128,32]{2,3,1,0:T(8,128)S(1)}, s32[3,1,128,32]{2,3,1,0:T(8,128)}, u32[]{:S(2)}) copy-start(s32[3,1,128,32]{2,3,1,0:T(8,128)} %param.16) | copy-start | bytes 147460
  31.9 18.6 %copy-start.3 = (s32[3,1,128,32]{2,3,1,0:T(8,128)S(1)}, s32[3,1,128,32]{2,3,1,0:T(8,128)}, u32[]{:S(2)}) copy-start(s32[3,1,128,32]{2,3,1,0:T(8,128)} %param.15) | copy-start | bytes 147460
  38.9 32.1 %all-to-all-start.1 = ((bf16[128,32,128]{2,1,0:T(8,128)(2,1)}), bf16[128,32,128]{2,1,0:T(8,128)(2,1)S(1)}, u32[]{:S(2)}, u32[]{:S(2)}) async-start(bf16[128,32,128]{2,1,0:T(8,128)(2,1)} %bitcast.117), calls=%async_computation.1 | async-start | bytes 2097152 | tf_op jit(solution)/shard_map/all_to_all | solution.py:453
  71.0 1.0 copy-start
  72.0 40.4 %all-to-all-start.2 = ((bf16[128,64,128]{2,1,0:T(8,128)(2,1)}), bf16[128,64,128]{2,1,0:T(8,128)(2,1)}, u32[]{:S(2)}, u32[]{:S(2)}) async-start(bf16[128,64,128]{2,1,0:T(8,128)(2,1)} %bitcast.116), calls=%async_computation.2 | async-start | bytes 4194304 | tf_op jit(solution)/shard_map/all_to_all | solution.py:453
  82.2 187.1 %reduce-scatter.2.cloned.1.call-start = ((), (), s32[]{:S(2)}) async-start(), calls=%async_computation.7 | async-start | bytes 9437184 | tf_op jit(solution)/shard_map/reduce_scatter | solution.py:575
  161.0 49.6 %all-to-all-start.3 = ((bf16[128,96,128]{2,1,0:T(8,128)(2,1)}), bf16[128,96,128]{2,1,0:T(8,128)(2,1)}, u32[]{:S(2)}, u32[]{:S(2)}) async-start(bf16[128,96,128]{2,1,0:T(8,128)(2,1)} %get-tuple-element.102), calls=%async_computation.3 | async-start | bytes 6291456 | tf_op jit(solution)/shard_map/all_to_all | solution.py:453
  197.2 5.0 %collective-permute-start = (bf16[64,128,128]{2,1,0:T(8,128)(2,1)}, bf16[64,128,128]{2,1,0:T(8,128)(2,1)S(1)}, u32[]{:S(2)}, u32[]{:S(2)}) collective-permute-start(bf16[64,128,128]{2,1,0:T(8,128)(2,1)} %get-tuple-element.101), channel_id=1, source_target_pairs={{0,1},{1,0},{2,3},{3,2},{4,5},{5,4},{6,7},{7,6},{8,9},{9,8},{10,11... | collective-permute-start | bytes 6291464 | tf_op jit(solution)/shard_map/ppermute | solution.py:588
  210.6 34.3 %all-to-all-start.4 = ((bf16[64,128,128]{2,1,0:T(8,128)(2,1)}), bf16[64,128,128]{2,1,0:T(8,128)(2,1)}, u32[]{:S(2)}, u32[]{:S(2)}) async-start(bf16[64,128,128]{2,1,0:T(8,128)(2,1)} %add_convert_fusion), calls=%async_computation.4 | async-start | bytes 4194304 | tf_op jit(solution)/shard_map/all_to_all | solution.py:591
  217.4 86.0 %all-gather.2.cloned.1.call-start = ((), (), s32[]{:S(2)}) async-start(), calls=%async_computation.8 | async-start | bytes 4718592 | tf_op jit(solution)/shard_map/all_gather | solution.py:628
  270.7 10.0 %collective-permute-start.1 = (bf16[4,32,1024]{2,1,0:T(8,128)(2,1)S(1)}, bf16[4,32,1024]{2,1,0:T(8,128)(2,1)S(1)}, u32[]{:S(2)}, u32[]{:S(2)}) collective-permute-start(bf16[4,32,1024]{2,1,0:T(8,128)(2,1)S(1)} %get-tuple-element.110), channel_id=1, source_target_pairs={{0,8},{1,9},{2,10},{3,11},{4,12},{5,13},{6,14},{7,15},{8,16},{9,17... | collective-permute-start | bytes 786440 | tf_op jit(solution)/shard_map/ppermute | solution.py:449
  271.3 16.2 %collective-permute-start.2 = (bf16[4,32,1024]{2,1,0:T(8,128)(2,1)S(1)}, bf16[4,32,1024]{2,1,0:T(8,128)(2,1)S(1)}, u32[]{:S(2)}, u32[]{:S(2)}) collective-permute-start(bf16[4,32,1024]{2,1,0:T(8,128)(2,1)S(1)} %get-tuple-element.112), channel_id=1, source_target_pairs={{0,16},{1,17},{2,18},{3,19},{4,20},{5,21},{6,22},{7,23},{8,24},{9,... | collective-permute-start | bytes 786440 | tf_op jit(solution)/shard_map/ppermute | solution.py:449
  275.2 12.4 %collective-permute-start.3 = (bf16[4,32,1024]{2,1,0:T(8,128)(2,1)S(1)}, bf16[4,32,1024]{2,1,0:T(8,128)(2,1)S(1)}, u32[]{:S(2)}, u32[]{:S(2)}) collective-permute-start(bf16[4,32,1024]{2,1,0:T(8,128)(2,1)S(1)} %get-tuple-element.111), channel_id=1, source_target_pairs={{0,24},{1,25},{2,26},{3,27},{4,28},{5,29},{6,30},{7,31},{8,0},{9,1... | collective-permute-start | bytes 786440 | tf_op jit(solution)/shard_map/ppermute | solution.py:449
  288.8 4.8 %collective-permute-start.4 = (bf16[32,1024]{1,0:T(8,128)(2,1)S(1)}, bf16[32,1024]{1,0:T(8,128)(2,1)S(1)}, u32[]{:S(2)}, u32[]{:S(2)}) collective-permute-start(bf16[32,1024]{1,0:T(8,128)(2,1)S(1)} %get-tuple-element.113), channel_id=1, source_target_pairs={{0,32},{1,33},{2,34},{3,35},{4,36},{5,37},{6,38},{7,39},{8,40},{9,... | collective-permute-start | bytes 196616 | tf_op jit(solution)/shard_map/ppermute | solution.py:449
  289.5 5.2 %collective-permute-start.5 = (bf16[32,1024]{1,0:T(8,128)(2,1)S(1)}, bf16[32,1024]{1,0:T(8,128)(2,1)S(1)}, u32[]{:S(2)}, u32[]{:S(2)}) collective-permute-start(bf16[32,1024]{1,0:T(8,128)(2,1)S(1)} %get-tuple-element.115), channel_id=1, source_target_pairs={{0,64},{1,65},{2,66},{3,67},{4,68},{5,69},{6,70},{7,71},{8,72},{9,... | collective-permute-start | bytes 196616 | tf_op jit(solution)/shard_map/ppermute | solution.py:449
  291.5 4.0 %collective-permute-start.6 = (bf16[32,1024]{1,0:T(8,128)(2,1)S(1)}, bf16[32,1024]{1,0:T(8,128)(2,1)S(1)}, u32[]{:S(2)}, u32[]{:S(2)}) collective-permute-start(bf16[32,1024]{1,0:T(8,128)(2,1)S(1)} %get-tuple-element.114), channel_id=1, source_target_pairs={{0,96},{1,97},{2,98},{3,99},{4,100},{5,101},{6,102},{7,103},{8,104... | collective-permute-start | bytes 196616 | tf_op jit(solution)/shard_map/ppermute | solution.py:449
Sparse Core Ops, SparseCore 0:
  161.1 108.1 reduce-scatter.1
  271.1 32.3 all-gather.1
